TPU v7x, 32 devices: a whole 2x2x4 slice. The times are simulated.
32 devices in a mesh: dp: 8 (over z, y), blk: 4 (over x, core).
Axes of the slice: x: 2, y: 2, z: 4, core: 2. Of those that a mesh axis runs over, the one named last changes fastest.
Arguments:
- inputs: bfloat16 [4096, 512], P('dp'), may hold values from -6 to 6
- out_grads: bfloat16 [4096, 512], P('dp'), may hold values from -6 to 6
- pre_act: bfloat16 [4096, 36864], P('dp', 'blk'), may hold values from -6 to 6
- w_in: bfloat16 [36864, 512], P('blk'), may hold values from -0.03125 to 0.03125
- w_out: bfloat16 [36864, 512], P('blk'), may hold values from -0.25 to 0.25
Outputs:
- grad_inputs: bfloat16 [4096, 512], P(('dp', 'blk'))
- grad_w_in: float32 [36864, 512], P(('blk', 'dp'))
- grad_w_out: float32 [36864, 512], P(('blk', 'dp'))
All inputs are finite; a program needn't handle non-finite values.
Results may differ from a plain program's by a relative error of at most 0.0049.
Values sent between devices are 32-bit elements; how exact they have to be, the bound alone decides.
No kernel may reach another device: no remote copies, remote signals or barrier semaphores. Data moves between devices by JAX's collectives and lax.ppermute only.
A program may use at most 128 MiB of HBM per device.

v0:
```python
import jax
import jax.numpy as jnp
from jax import lax
from jax.sharding import PartitionSpec as P


def contract_rows(left, right):
    return lax.dot_general(
        left, right, (((0,), (0,)), ((), ())), preferred_element_type=jnp.float32
    )


def hidden_grads(out_grads, pre_act, w_out):
    back = lax.dot_general(
        out_grads, w_out, (((1,), (1,)), ((), ())), preferred_element_type=jnp.float32
    )
    return jnp.where(pre_act > 0, back, jnp.zeros_like(back)).astype(jnp.bfloat16)


def body(inputs, out_grads, pre_act, w_in, w_out):
    group_rows = inputs.shape[0]
    token_total = group_rows * lax.axis_size("dp")
    factor = lax.rsqrt(jnp.asarray(token_total, jnp.float32))
    act = jnp.maximum(pre_act, jnp.zeros_like(pre_act))
    grad_hidden = hidden_grads(out_grads, pre_act, w_out)
    grad_out = contract_rows(act, out_grads) * factor
    grad_in = contract_rows(grad_hidden, inputs) * factor
    grad_w_in, grad_w_out = (
        lax.psum_scatter(grad_in, "dp", scatter_dimension=0, tiled=True),
        lax.psum_scatter(grad_out, "dp", scatter_dimension=0, tiled=True),
    )
    grad_inputs = lax.psum_scatter(
        jnp.dot(grad_hidden, w_in, preferred_element_type=jnp.float32),
        "blk",
        scatter_dimension=0,
        tiled=True,
    ).astype(jnp.bfloat16)
    return (grad_inputs, grad_w_in, grad_w_out)


def solution(mesh):
    return jax.shard_map(
        body,
        mesh=mesh,
        in_specs=(P("dp", None), P("dp", None), P("dp", "blk"), P("blk", None), P("blk", None)),
        out_specs=(P(("dp", "blk"), None), P(("blk", "dp"), None), P(("blk", "dp"), None)),
        check_vma=False,
    )
```

profile of v0, /device:TPU:16, one launch (start us, length us, event | category | flops | bytes accessed | tf_op | source)
XLA Modules:
  0.0 699.8 jit_solution(1279868817003604070)
XLA Ops:
  7.2 0.0 copy-start
  7.2 0.0 reduce-scatter.4.cloned.1.call-start
  7.2 1.0 copy-done
  8.2 12.7 %select_convert_fusion = bf16[512,9216]{1,0:T(8,128)(2,1)} fusion(bf16[512,9216]{1,0:T(8,128)(2,1)} %param.7, bf16[512,512]{1,0:T(8,128)(2,1)S(1)} %copy-done, bf16[9216,512]{1,0:T(8,128)(2,1)} %param.9), kind=kOutput, calls=%fused_computation | convolution fusion | flops 4845993984 | bytes 28835840 | tf_op jit(solution)/shard_map/dot_general | solution.py:14
  20.9 0.0 copy-start.1
  20.9 11.2 %fusion.3 = f32[512,512]{1,0:T(8,128)} fusion(bf16[512,9216]{1,0:T(8,128)(2,1)} %select_convert_fusion, bf16[9216,512]{1,0:T(8,128)(2,1)} %param.8), kind=kOutput, calls=%fused_computation.6 | convolution fusion | flops 4831838208 | bytes 19922944 | tf_op jit(solution)/shard_map/dot_general | solution.py:33
  32.1 0.0 reduce-scatter.4.cloned.1.call-update
  32.2 0.0 reduce-scatter.6.cloned.1.call-start
  32.2 0.0 copy-done.1
  32.2 13.0 %convolution_multiply_fusion.1 = f32[9216,512]{1,0:T(8,128)} fusion(bf16[512,9216]{1,0:T(8,128)(2,1)} %select_convert_fusion, bf16[512,512]{1,0:T(8,128)(2,1)S(1)} %copy-done.1), kind=kOutput, calls=%fused_computation.2 | convolution fusion | flops 4836556800 | bytes 28835840 | tf_op jit(solution)/shard_map/dot_general | solution.py:8
  45.2 0.0 reduce-scatter.6.cloned.1.call-update
  45.2 0.0 reduce-scatter.8.cloned.1.call-start
  45.3 13.2 %convolution_multiply_fusion = f32[9216,512]{1,0:T(8,128)} fusion(bf16[512,512]{1,0:T(8,128)(2,1)S(1)} %copy-done, bf16[512,9216]{1,0:T(8,128)(2,1)} %param.7), kind=kOutput, calls=%fused_computation.1 | convolution fusion | flops 4841275392 | bytes 28835840 | tf_op jit(solution)/shard_map/dot_general | solution.py:8
  58.4 0.0 reduce-scatter.8.cloned.1.call-update
  58.5 0.0 reduce-scatter.4.cloned.1.call-done
  58.5 1.6 convert_element_type.7
  60.1 315.7 %reduce-scatter.6.cloned.1.call-done = f32[1152,512]{1,0:T(8,128)} async-done(((f32[9216,512]{1,0:T(8,128)}), f32[1152,512]{1,0:T(8,128)}) %reduce-scatter.6.cloned.1.call-update) | async-done | bytes 2359312 | tf_op jit(solution)/shard_map/reduce_scatter | solution.py:29
  375.8 317.4 %reduce-scatter.8.cloned.1.call-done = f32[1152,512]{1,0:T(8,128)} async-done(((f32[9216,512]{1,0:T(8,128)}), f32[1152,512]{1,0:T(8,128)}) %reduce-scatter.8.cloned.1.call-update) | async-done | bytes 2359312 | tf_op jit(solution)/shard_map/reduce_scatter | solution.py:30
Async XLA Ops:
  7.2 1.0 copy-start
  7.2 51.3 %reduce-scatter.4.cloned.1.call-start = ((), (), s32[]{:S(2)}) async-start(), calls=%async_computation.3 | async-start | bytes 1310720 | tf_op jit(solution)/shard_map/reduce_scatter | solution.py:32
  20.9 11.3 %copy-start.1 = (bf16[512,512]{1,0:T(8,128)(2,1)S(1)}, bf16[512,512]{1,0:T(8,128)(2,1)}, u32[]{:S(2)}) copy-start(bf16[512,512]{1,0:T(8,128)(2,1)} %param.5) | copy-start | bytes 1572868
  32.2 343.6 %reduce-scatter.6.cloned.1.call-start = ((), (), s32[]{:S(2)}) async-start(), calls=%async_computation.4 | async-start | bytes 21233664 | tf_op jit(solution)/shard_map/reduce_scatter | solution.py:29
  45.2 648.0 %reduce-scatter.8.cloned.1.call-start = ((), (), s32[]{:S(2)}) async-start(), calls=%async_computation.5 | async-start | bytes 21233664 | tf_op jit(solution)/shard_map/reduce_scatter | solution.py:30
Sparse Core Ops, SparseCore 0:
  32.3 25.9 reduce-scatter.3
  63.2 312.5 reduce-scatter.5
  380.8 312.4 reduce-scatter.7
where the time goes:
time: 702 us; the launch traced here: 700 us
  waiting for transfers between devices  633 us (90%)
  matrix products  50.1 us (7%)
  between operations  13.8 us (2%)
    reduce_scatter x1, waiting for transfers between devices, body(): lax.psum_scatter(grad_out, 'dp', scatter_dimension=0, tiled=True)  317 us
    reduce_scatter x1, waiting for transfers between devices, body(): lax.psum_scatter(grad_in, 'dp', scatter_dimension=0, tiled=True)  316 us
    dot_general x2, matrix products, contract_rows(): lax.dot_general(left, right, (((0,), (0,)), ((), ())), preferred_element_...  26.2 us
  transfers between devices with their start and end apart: 3, of which 2 were waited for; matrix products, arithmetic and copies ran while one was open for 4% of the time, Pallas kernels for 0%

commit v1 on v0

v1 whole, which is shorter than its diff:
```python
import functools

import jax
import jax.numpy as jnp
from jax import lax
from jax.experimental import pallas as pl
from jax.experimental.pallas import tpu as pltpu
from jax.sharding import PartitionSpec as P

PIECES = 3
LAG = 2
VMEM_LIMIT = 48 * 1024 * 1024


def contract_rows(left, right):
    return lax.dot_general(
        left, right, (((0,), (0,)), ((), ())), preferred_element_type=jnp.float32
    )


def hidden_grads(out_grads, pre_act, w_out):
    back = lax.dot_general(
        out_grads, w_out, (((1,), (1,)), ((), ())), preferred_element_type=jnp.float32
    )
    return jnp.where(pre_act > 0, back, jnp.zeros_like(back)).astype(jnp.bfloat16)


def input_grads(grad_hidden, w_in):
    return lax.psum_scatter(
        jnp.dot(grad_hidden, w_in, preferred_element_type=jnp.float32),
        "blk",
        scatter_dimension=0,
        tiled=True,
    ).astype(jnp.bfloat16)


def plain_body(inputs, out_grads, pre_act, w_in, w_out):
    token_total = inputs.shape[0] * lax.axis_size("dp")
    factor = lax.rsqrt(jnp.asarray(token_total, jnp.float32))
    act = jnp.maximum(pre_act, jnp.zeros_like(pre_act))
    grad_hidden = hidden_grads(out_grads, pre_act, w_out)
    grad_out = contract_rows(act, out_grads) * factor
    grad_in = contract_rows(grad_hidden, inputs) * factor
    return (
        input_grads(grad_hidden, w_in),
        lax.psum_scatter(grad_in, "dp", scatter_dimension=0, tiled=True),
        lax.psum_scatter(grad_out, "dp", scatter_dimension=0, tiled=True),
    )


def join_kernel(core_ref, grads_ref, inputs_ref, mine_ref, other_ref, g_ref, x_ref):
    rows = grads_ref.shape[0]
    half = rows // 2
    core = core_ref[0]
    g_ref[:rows, :] = grads_ref[...]
    x_ref[:rows, :] = inputs_ref[...]
    mine = pl.ds(pl.multiple_of(rows + core * half, half), half)
    other = pl.ds(pl.multiple_of(rows + (1 - core) * half, half), half)
    g_ref[mine, :] = mine_ref[:half, :].astype(jnp.bfloat16)
    x_ref[mine, :] = mine_ref[half:, :].astype(jnp.bfloat16)
    g_ref[other, :] = other_ref[:half, :].astype(jnp.bfloat16)
    x_ref[other, :] = other_ref[half:, :].astype(jnp.bfloat16)


def join(core, out_grads, inputs, mine, other):
    rows, width = out_grads.shape
    shape = jax.ShapeDtypeStruct((2 * rows, width), jnp.bfloat16)
    vmem = pl.BlockSpec(memory_space=pltpu.VMEM)
    return pl.pallas_call(
        join_kernel,
        out_shape=(shape, shape),
        in_specs=[pl.BlockSpec(memory_space=pltpu.SMEM)] + [vmem] * 4,
        out_specs=(vmem, vmem),
        compiler_params=pltpu.CompilerParams(vmem_limit_bytes=VMEM_LIMIT),
        name="join_tokens",
    )(core.reshape(1), out_grads, inputs, mine, other)


def piece_math(scale, own, partner, g, x, w, sums):
    partner = partner.astype(jnp.bfloat16)
    pre = jnp.concatenate([own, partner], axis=0)
    back = lax.dot_general(g, w, (((1,), (1,)), ((), ())), preferred_element_type=jnp.float32)
    hidden = jnp.where(pre > 0, back, 0.0).astype(jnp.bfloat16)
    act = jnp.maximum(pre, jnp.zeros_like(pre))
    grad_in = contract_rows(hidden, x) * scale
    grad_out = contract_rows(act, g) * scale
    for ref in sums:
        grad_in = grad_in + ref[0]
        grad_out = grad_out + ref[1]
    return grad_in, grad_out


def piece_kernel(scale, n_sums, idx_ref, own_ref, partner_ref, g_ref, x_ref, w_ref, *refs):
    sums, out_ref = refs[:n_sums], refs[n_sums]
    out_ref[0], out_ref[1] = piece_math(
        scale, own_ref[...], partner_ref[...], g_ref[...], x_ref[...], w_ref[...], sums
    )


def final_kernel(scale, n_sums, idx_ref, own_ref, inner_ref, outer_ref, g_ref, x_ref, w_ref, *refs):
    sums, (in_ref, out_ref) = refs[:n_sums], refs[-2:]
    partner = jnp.where(idx_ref[1] > 0, inner_ref[...], outer_ref[...])
    in_ref[...], out_ref[...] = piece_math(
        scale, own_ref[...], partner, g_ref[...], x_ref[...], w_ref[...], sums
    )


def piece_specs(rows, size, width, n_partners, n_sums):
    whole = lambda shape: pl.BlockSpec(shape, lambda i, idx: (0,) * len(shape))
    return (
        [pl.BlockSpec((rows, size), lambda i, idx: (0, idx[0]))]
        + [whole((rows, size))] * n_partners
        + [whole((2 * rows, width))] * 2
        + [pl.BlockSpec((size, width), lambda i, idx: (idx[0], 0))]
        + [whole((2, size, width))] * n_sums
    )


def piece_cost(rows, size, width, n_sums):
    return pl.CostEstimate(
        flops=3 * 2 * 2 * rows * size * width,
        bytes_accessed=rows * size * 6 + rows * width * 8 + size * width * (10 + 8 * n_sums),
        transcendentals=0,
    )


def piece(scale, index, pre_act, partner, g, x, w_out, sums):
    rows, size = partner.shape
    width = g.shape[1]
    return pl.pallas_call(
        functools.partial(piece_kernel, scale, len(sums)),
        grid_spec=pltpu.PrefetchScalarGridSpec(
            num_scalar_prefetch=1,
            grid=(1,),
            in_specs=piece_specs(rows, size, width, 1, len(sums)),
            out_specs=pl.BlockSpec((2, size, width), lambda i, idx: (0, 0, 0)),
        ),
        out_shape=jax.ShapeDtypeStruct((2, size, width), jnp.float32),
        compiler_params=pltpu.CompilerParams(vmem_limit_bytes=VMEM_LIMIT),
        cost_estimate=piece_cost(rows, size, width, len(sums)),
        name="piece",
    )(index.reshape(1), pre_act, partner, g, x, w_out, *sums)


def final(scale, place, count, index, is_inner, pre_act, partners, g, x, w_out, sums, held):
    rows, size = partners[0].shape
    width = g.shape[1]
    shape = jax.ShapeDtypeStruct((count * size, width), jnp.float32)
    first = 6 + 1 + len(sums)
    return pl.pallas_call(
        functools.partial(final_kernel, scale, len(sums)),
        grid_spec=pltpu.PrefetchScalarGridSpec(
            num_scalar_prefetch=1,
            grid=(1,),
            in_specs=piece_specs(rows, size, width, 2, len(sums))
            + [pl.BlockSpec(memory_space=pl.ANY)] * len(held),
            out_specs=[pl.BlockSpec((size, width), lambda i, idx: (place, 0))] * 2,
        ),
        out_shape=(shape, shape),
        input_output_aliases={first + i: i for i in range(len(held))},
        compiler_params=pltpu.CompilerParams(vmem_limit_bytes=VMEM_LIMIT),
        cost_estimate=piece_cost(rows, size, width, len(sums)),
        name="final_piece",
    )(jnp.stack([index, is_inner]), pre_act, *partners, g, x, w_out, *sums, *held)


def line_body(inputs, out_grads, pre_act, w_in, w_out):
    count = PIECES
    rows, hidden = pre_act.shape
    size = hidden // (8 * count)
    scale = 1.0 / (rows * lax.axis_size("dp")) ** 0.5
    me = lax.axis_index("dp")
    plane, half = me // 2, me % 2
    core = lax.axis_index("blk") % 2
    side = plane // 2
    is_inner = jnp.where((plane == 1) | (plane == 2), 1, 0).astype(jnp.int32)

    def links(pairs):
        return [(2 * a + h, 2 * b + h) for a, b in pairs for h in range(2)]

    def swaps(planes):
        return [(2 * a + h, 2 * a + 1 - h) for a in planes for h in range(2)]

    outer_to_inner = links([(0, 1), (3, 2)])
    inner_to_inner = links([(1, 2), (2, 1)])
    inner_to_outer = links([(1, 0), (2, 3)])

    def block(q, which):
        place = q // count
        chunk = jnp.where(side == 0, 3 - place, place)
        return (chunk * 2 + which) * count + q % count

    quarter = rows // 2
    part = jnp.concatenate(
        [
            lax.dynamic_slice_in_dim(out_grads, core * quarter, quarter, 0),
            lax.dynamic_slice_in_dim(inputs, core * quarter, quarter, 0),
        ],
        axis=0,
    ).astype(jnp.float32)
    mine = lax.ppermute(part, "dp", swaps(range(4)))
    blks = lax.axis_size("blk")
    other = lax.ppermute(mine, "blk", [(i, i ^ 1) for i in range(blks)])
    g, x = join(core, out_grads, inputs, mine, other)

    started = []

    def exchange(q, planes):
        if len(started) >= 2:
            q, started[-2][0] = lax.optimization_barrier((q, started[-2][0]))
        start = block(q, 1 - half) * size
        send = lax.dynamic_slice_in_dim(pre_act, start, size, 1).astype(jnp.float32)
        box = [lax.ppermute(send, "dp", swaps(planes))]
        started.append(box)
        return box

    main_steps = 3 * count
    every, outer, inner = (0, 1, 2, 3), (0, 3), (1, 2)
    main_q = [
        jnp.clip(s - LAG * is_inner, 0, (2 * count - 1) * is_inner + (main_steps - 1) * (1 - is_inner))
        for s in range(main_steps)
    ]
    near_outer = [jnp.int32(main_steps + j) for j in range(count)]
    near_inner = [jnp.int32(2 * count + j) for j in range(count)]

    y_main, y_no, y_ni = [], [], []
    for s in range(main_steps):
        relevant = outer if s < LAG or s >= 2 * count + LAG else every
        y_main.append(exchange(main_q[s], relevant))
        j = s - (LAG + 2)
        if 0 <= j < count:
            y_no.append(exchange(near_outer[j], every))
        if s >= main_steps - count:
            y_ni.append(exchange(near_inner[s - (main_steps - count)], inner))

    def run(q, partner, sums):
        return piece(scale, block(q, half), pre_act, partner, g, x, w_out, sums)

    from_outer, from_inner, to_outer = [], [], []
    for s in range(main_steps):
        out = run(main_q[s], y_main[s][0], [from_outer[s - LAG]] if s >= LAG else [])
        from_outer.append(lax.ppermute(out, "dp", outer_to_inner))
        if LAG <= s < 2 * count + LAG:
            from_inner.append(lax.ppermute(out, "dp", inner_to_inner))
        j = s - (LAG + 2)
        if 0 <= j < count:
            out = run(near_outer[j], y_no[j][0], [from_inner[j]])
            to_outer.append(lax.ppermute(out, "dp", inner_to_outer))

    held = ()
    for i in range(count):
        q = jnp.where(is_inner > 0, near_inner[i], near_outer[i])
        held = final(
            scale,
            i,
            count,
            block(q, half),
            is_inner,
            pre_act,
            (y_ni[i][0], y_no[i][0]),
            g,
            x,
            w_out,
            [from_outer[2 * count + i], from_inner[count + i], to_outer[i]],
            held,
        )

    grad_inputs = input_grads(hidden_grads(out_grads, pre_act, w_out), w_in)
    return (grad_inputs, held[0], held[1])


def solution(mesh):
    def body(inputs, out_grads, pre_act, w_in, w_out):
        fits = pre_act.shape[1] % (8 * PIECES * 128) == 0 and inputs.shape[0] % 32 == 0
        paired = mesh.shape["blk"] % 2 == 0
        run = line_body if mesh.shape["dp"] == 8 and paired and fits else plain_body
        return run(inputs, out_grads, pre_act, w_in, w_out)

    return jax.shard_map(
        body,
        mesh=mesh,
        in_specs=(P("dp", None), P("dp", None), P("dp", "blk"), P("blk", None), P("blk", None)),
        out_specs=(P(("dp", "blk"), None), P(("blk", "dp"), None), P(("blk", "dp"), None)),
        check_vma=False,
    )
```

time: 702 us -> 462 us (0.66)
  waiting for transfers between devices: 633 us -> 271 us
  Pallas kernels: 0 us -> 72.1 us
  starting transfers between devices: 0.12 us -> 58.5 us
  matrix products: 50.1 us -> 16.3 us
  other arithmetic: 1.62 us -> 21.1 us
    reduce_scatter x3 -> x1, waiting for transfers between devices: 633 us -> 0.01 us  [input_grads(): lax.psum_scatter(jnp.dot(grad_hidden, w_in, preferred_element_type=jnp.fl...]
    ppermute x0 -> x35, waiting for transfers between devices: none -> 271 us  [the longest x9 171 us: line_body(): from_outer.append(lax.ppermute(out, 'dp', outer_to_inner))]
    pallas_call x0 -> x16, Pallas kernels: none -> 72.1 us  [the longest x12 53.9 us: piece(): pl.pallas_call(functools.partial(piece_kernel, scale, len(sums)), grid_sp...]
    ppermute x0 -> x35, starting transfers between devices: none -> 58.5 us  [the longest x15 21.8 us: exchange(): box = [lax.ppermute(send, 'dp', swaps(planes))]]
    dot_general x4 -> x1, matrix products: 50.1 us -> 16.3 us  [input_grads(): jnp.dot(grad_hidden, w_in, preferred_element_type=jnp.float32)]
    convert_element_type x1 -> x10, other arithmetic: 1.62 us -> 20.8 us  [the longest x8 18.1 us: exchange(): send = lax.dynamic_slice_in_dim(pre_act, start, size, 1).astype(jnp.float32)]
  transfers between devices with their start and end apart: 3 -> 36, of which waited for: 2 -> 16; matrix products, arithmetic and copies ran while one was open for 4% -> 8% of each run, Pallas kernels for 0% -> 14%
where the time goes in v1:
time: 462 us; the launch traced here: 460 us
  waiting for transfers between devices  271 us (59%)
  Pallas kernels  72.1 us (16%)
  starting transfers between devices  58.5 us (13%)
  other arithmetic  21.1 us (5%)
  matrix products  16.3 us (4%)
  between operations  14.7 us (3%)
  local copies, waits for them, and re-layouts  6.51 us (1%)
    ppermute x9, waiting for transfers between devices, line_body(): from_outer.append(lax.ppermute(out, 'dp', outer_to_inner))  171 us
    ppermute x15, waiting for transfers between devices, exchange(): box = [lax.ppermute(send, 'dp', swaps(planes))]  69.4 us
    pallas_call x12, Pallas kernels, piece(): pl.pallas_call(functools.partial(piece_kernel, scale, len(sums)), grid_sp...  53.9 us
    ppermute x15, starting transfers between devices, exchange(): box = [lax.ppermute(send, 'dp', swaps(planes))]  21.8 us
    ppermute x1, waiting for transfers between devices, line_body(): mine = lax.ppermute(part, 'dp', swaps(range(4)))  19.9 us
    convert_element_type x8, other arithmetic, exchange(): send = lax.dynamic_slice_in_dim(pre_act, start, size, 1).astype(jnp.float32)  18.1 us
    pallas_call x3, Pallas kernels, final(): pl.pallas_call(functools.partial(final_kernel, scale, len(sums)), grid_sp...  18 us
    dot_general x1, matrix products, input_grads(): jnp.dot(grad_hidden, w_in, preferred_element_type=jnp.float32)  16.3 us
  transfers between devices with their start and end apart: 36, of which 16 were waited for; matrix products, arithmetic and copies ran while one was open for 8% of the time, Pallas kernels for 14%

profile of v1, /device:TPU:16, one launch (start us, length us, event | category | flops | bytes accessed | tf_op | source)
XLA Modules:
  0.0 460.4 jit_solution(12802639817076580137)
XLA Ops:
  18.5 19.9 %collective-permute-done.13.mine_ref = f32[512,512]{1,0:T(8,128)S(1)} collective-permute-done((f32[512,512]{1,0:T(8,128)}, f32[512,512]{1,0:T(8,128)S(1)}, u32[]{:S(2)}, u32[]{:S(2)}) %collective-permute-start.13) | collective-permute-done | bytes 1048608 | tf_op jit(solution)/shard_map/ppermute | solution.py:201
  38.4 15.8 %collective-permute-done.1.partner_ref = f32[512,384]{1,0:T(8,128)} collective-permute-done((f32[512,384]{1,0:T(8,128)}, f32[512,384]{1,0:T(8,128)}, u32[]{:S(2)}, u32[]{:S(2)}) %collective-permute-start.1) | collective-permute-done | bytes 786464 | tf_op jit(solution)/shard_map/ppermute | solution.py:213
  62.2 15.2 %collective-permute-done.2.partner_ref = f32[512,384]{1,0:T(8,128)} collective-permute-done((f32[512,384]{1,0:T(8,128)}, f32[512,384]{1,0:T(8,128)}, u32[]{:S(2)}, u32[]{:S(2)}) %collective-permute-start.2) | collective-permute-done | bytes 786464 | tf_op jit(solution)/shard_map/ppermute | solution.py:213
  77.4 14.8 %collective-permute-done.9.partner_ref = f32[512,384]{1,0:T(8,128)} collective-permute-done((f32[512,384]{1,0:T(8,128)}, f32[512,384]{1,0:T(8,128)}, u32[]{:S(2)}, u32[]{:S(2)}) %collective-permute-start.9) | collective-permute-done | bytes 786464 | tf_op jit(solution)/shard_map/ppermute | solution.py:213
  108.3 21.0 %collective-permute-done.3.partner_ref = f32[512,384]{1,0:T(8,128)} collective-permute-done((f32[512,384]{1,0:T(8,128)}, f32[512,384]{1,0:T(8,128)}, u32[]{:S(2)}, u32[]{:S(2)}) %collective-permute-start.3) | collective-permute-done | bytes 786464 | tf_op jit(solution)/shard_map/ppermute | solution.py:213
  133.6 38.0 %collective-permute-done.17.refs_0_ = f32[2,384,512]{2,1,0:T(8,128)} collective-permute-done((f32[2,384,512]{2,1,0:T(8,128)}, f32[2,384,512]{2,1,0:T(8,128)}, u32[]{:S(2)}, u32[]{:S(2)}) %collective-permute-start.17) | collective-permute-done | bytes 1572896 | tf_op jit(solution)/shard_map/ppermute | solution.py:242
  184.0 21.3 %collective-permute-done.22.refs_0_ = f32[2,384,512]{2,1,0:T(8,128)} collective-permute-done((f32[2,384,512]{2,1,0:T(8,128)}, f32[2,384,512]{2,1,0:T(8,128)}, u32[]{:S(2)}, u32[]{:S(2)}) %collective-permute-start.22) | collective-permute-done | bytes 1572896 | tf_op jit(solution)/shard_map/ppermute | solution.py:242
  205.4 4.6 %piece.18 = f32[2,384,512]{2,1,0:T(8,128)} custom-call(s32[1]{0:T(128)} %bitcast.10.idx_ref, bf16[512,9216]{1,0:T(8,128)(2,1)} %own_ref.29, f32[512,384]{1,0:T(8,128)} %collective-permute-done.9.partner_ref, bf16[1024,512]{1,0:T(8,128)(2,1)S(1)} %get-tuple-element.49.g_ref, bf16[1024,512]{1,0:T(8,128)(2,1)S(1)} %get-tuple-element.50.x_ref, ...), custom_call_target="tpu_custom_call" | custom-call | flops 1207959552 | bytes 6815744 | tf_op jit(solution)/shard_map/piece/pallas_call | solution.py:130
  222.2 16.8 %collective-permute-done.18.refs_0_ = f32[2,384,512]{2,1,0:T(8,128)} collective-permute-done((f32[2,384,512]{2,1,0:T(8,128)}, f32[2,384,512]{2,1,0:T(8,128)}, u32[]{:S(2)}, u32[]{:S(2)}) %collective-permute-start.18) | collective-permute-done | bytes 1572896 | tf_op jit(solution)/shard_map/ppermute | solution.py:242
  241.0 4.6 %piece.14 = f32[2,384,512]{2,1,0:T(8,128)} custom-call(s32[1]{0:T(128)} %bitcast.5.idx_ref, bf16[512,9216]{1,0:T(8,128)(2,1)} %own_ref.29, f32[512,384]{1,0:T(8,128)} %collective-permute-done.2.partner_ref, bf16[1024,512]{1,0:T(8,128)(2,1)S(1)} %get-tuple-element.49.g_ref, bf16[1024,512]{1,0:T(8,128)(2,1)S(1)} %get-tuple-element.50.x_ref, ...), custom_call_target="tpu_custom_call" | custom-call | flops 1207959552 | bytes 6815744 | tf_op jit(solution)/shard_map/piece/pallas_call | solution.py:130
  245.6 23.9 %collective-permute-done.23.refs_0_ = f32[2,384,512]{2,1,0:T(8,128)} collective-permute-done((f32[2,384,512]{2,1,0:T(8,128)}, f32[2,384,512]{2,1,0:T(8,128)}, u32[]{:S(2)}, u32[]{:S(2)}) %collective-permute-start.23) | collective-permute-done | bytes 1572896 | tf_op jit(solution)/shard_map/ppermute | solution.py:242
  270.8 4.6 %piece.19 = f32[2,384,512]{2,1,0:T(8,128)} custom-call(s32[1]{0:T(128)} %bitcast.9.idx_ref, bf16[512,9216]{1,0:T(8,128)(2,1)} %own_ref.29, f32[512,384]{1,0:T(8,128)} %collective-permute-done.3.partner_ref, bf16[1024,512]{1,0:T(8,128)(2,1)S(1)} %get-tuple-element.49.g_ref, bf16[1024,512]{1,0:T(8,128)(2,1)S(1)} %get-tuple-element.50.x_ref, ...), custom_call_target="tpu_custom_call" | custom-call | flops 1207959552 | bytes 6815744 | tf_op jit(solution)/shard_map/piece/pallas_call | solution.py:130
  291.2 4.6 %piece.22 = f32[2,384,512]{2,1,0:T(8,128)} custom-call(s32[1]{0:T(128)} %bitcast.14.idx_ref, bf16[512,9216]{1,0:T(8,128)(2,1)} %own_ref.29, f32[512,384]{1,0:T(8,128)} %collective-permute-done.11.partner_ref.outer_ref, bf16[1024,512]{1,0:T(8,128)(2,1)S(1)} %get-tuple-element.49.g_ref, bf16[1024,512]{1,0:T(8,128)(2,1)S(1)} %get-tuple-element.50.x_ref, ...), custom_call_target="tpu_custom_call" | custom-call | flops 1207959552 | bytes 6815744 | tf_op jit(solution)/shard_map/piece/pallas_call | solution.py:130
  295.8 13.2 %collective-permute-done.19.refs_0_ = f32[2,384,512]{2,1,0:T(8,128)} collective-permute-done((f32[2,384,512]{2,1,0:T(8,128)}, f32[2,384,512]{2,1,0:T(8,128)}, u32[]{:S(2)}, u32[]{:S(2)}) %collective-permute-start.19) | collective-permute-done | bytes 1572896 | tf_op jit(solution)/shard_map/ppermute | solution.py:242
  311.7 4.6 %piece.15 = f32[2,384,512]{2,1,0:T(8,128)} custom-call(s32[1]{0:T(128)} %bitcast.4.idx_ref, bf16[512,9216]{1,0:T(8,128)(2,1)} %own_ref.29, f32[512,384]{1,0:T(8,128)} %collective-permute-done.4.partner_ref, bf16[1024,512]{1,0:T(8,128)(2,1)S(1)} %get-tuple-element.49.g_ref, bf16[1024,512]{1,0:T(8,128)(2,1)S(1)} %get-tuple-element.50.x_ref, ...), custom_call_target="tpu_custom_call" | custom-call | flops 1207959552 | bytes 6815744 | tf_op jit(solution)/shard_map/piece/pallas_call | solution.py:130
  316.3 22.2 %collective-permute-done.24.refs_0_ = f32[2,384,512]{2,1,0:T(8,128)} collective-permute-done((f32[2,384,512]{2,1,0:T(8,128)}, f32[2,384,512]{2,1,0:T(8,128)}, u32[]{:S(2)}, u32[]{:S(2)}) %collective-permute-start.24) | collective-permute-done | bytes 1572896 | tf_op jit(solution)/shard_map/ppermute | solution.py:242
  348.4 16.3 %fusion = f32[512,512]{1,0:T(8,128)} fusion(bf16[9216,512]{1,0:T(8,128)(2,1)} %param.8, bf16[512,9216]{1,0:T(8,128)(2,1)} %own_ref.29, bf16[512,512]{1,0:T(8,128)(2,1)S(1)} %copy-done.1, bf16[9216,512]{1,0:T(8,128)(2,1)} %w_ref.29), kind=kOutput, calls=%fused_computation.1 | convolution fusion | flops 9677832192 | bytes 29884416 | tf_op jit(solution)/shard_map/dot_general | solution.py:30
  364.8 4.6 %piece.21 = f32[2,384,512]{2,1,0:T(8,128)} custom-call(s32[1]{0:T(128)} %bitcast.12.idx_ref, bf16[512,9216]{1,0:T(8,128)(2,1)} %own_ref.29, f32[512,384]{1,0:T(8,128)} %collective-permute-done.12.partner_ref.outer_ref, bf16[1024,512]{1,0:T(8,128)(2,1)S(1)} %get-tuple-element.49.g_ref, bf16[1024,512]{1,0:T(8,128)(2,1)S(1)} %get-tuple-element.50.x_ref, ...), custom_call_target="tpu_custom_call" | custom-call | flops 1207959552 | bytes 6815744 | tf_op jit(solution)/shard_map/piece/pallas_call | solution.py:130
  369.4 16.0 %collective-permute-done.20.refs_0_ = f32[2,384,512]{2,1,0:T(8,128)} collective-permute-done((f32[2,384,512]{2,1,0:T(8,128)}, f32[2,384,512]{2,1,0:T(8,128)}, u32[]{:S(2)}, u32[]{:S(2)}) %collective-permute-start.20) | collective-permute-done | bytes 1572896 | tf_op jit(solution)/shard_map/ppermute | solution.py:242
  399.8 19.3 %collective-permute-done.28.refs_0_ = f32[2,384,512]{2,1,0:T(8,128)} collective-permute-done((f32[2,384,512]{2,1,0:T(8,128)}, f32[2,384,512]{2,1,0:T(8,128)}, u32[]{:S(2)}, u32[]{:S(2)}) %collective-permute-start.28) | collective-permute-done | bytes 1572896 | tf_op jit(solution)/shard_map/ppermute | solution.py:242
  424.4 5.9 %final_piece.3 = (f32[1152,512]{1,0:T(8,128)}, f32[1152,512]{1,0:T(8,128)}) custom-call(s32[2]{0:T(128)S(1)} %pad_add_fusion.2.idx_ref, bf16[512,9216]{1,0:T(8,128)(2,1)} %own_ref.29, f32[512,384]{1,0:T(8,128)} %collective-permute-done.5.inner_ref, f32[512,384]{1,0:T(8,128)S(1)} %collective-permute-done.10.partner_ref.outer_ref, ...), custom_call_target="tpu_custom_call" | custom-call | flops 1207959552 | bytes 9961472 | tf_op jit(solution)/shard_map/final_piece/pallas_call | solution.py:150
  430.3 6.1 %final_piece.4 = (f32[1152,512]{1,0:T(8,128)}, f32[1152,512]{1,0:T(8,128)}) custom-call(s32[2]{0:T(128)S(1)} %pad_add_fusion.1.idx_ref, bf16[512,9216]{1,0:T(8,128)(2,1)} %own_ref.29, f32[512,384]{1,0:T(8,128)} %collective-permute-done.6.inner_ref, ...), custom_call_target="tpu_custom_call", output_to_operand_aliasing={{0}: (10, {}), {1}: (11, {})} | custom-call | flops 1207959552 | bytes 9961472 | tf_op jit(solution)/shard_map/final_piece/pallas_call | solution.py:150
  436.4 10.8 %collective-permute-done.25.refs_1_ = f32[2,384,512]{2,1,0:T(8,128)} collective-permute-done((f32[2,384,512]{2,1,0:T(8,128)}, f32[2,384,512]{2,1,0:T(8,128)}, u32[]{:S(2)}, u32[]{:S(2)}) %collective-permute-start.25) | collective-permute-done | bytes 1572896 | tf_op jit(solution)/shard_map/ppermute | solution.py:244
  447.5 6.1 %final_piece.5 = (f32[1152,512]{1,0:T(8,128)}, f32[1152,512]{1,0:T(8,128)}) custom-call(s32[2]{0:T(128)S(1)} %pad_add_fusion.idx_ref, bf16[512,9216]{1,0:T(8,128)(2,1)} %own_ref.29, f32[512,384]{1,0:T(8,128)} %collective-permute-done.7.inner_ref, ...), custom_call_target="tpu_custom_call", output_to_operand_aliasing={{0}: (10, {}), {1}: (11, {})} | custom-call | flops 1207959552 | bytes 9961472 | tf_op jit(solution)/shard_map/final_piece/pallas_call | solution.py:150
  (97 shorter events, 115.5 us)
Async XLA Ops:
  7.2 415.6 %reduce-scatter.2.cloned.1.call-start = ((), (), s32[]{:S(2)}) async-start(), calls=%async_computation.1 | async-start | bytes 1310720 | tf_op jit(solution)/shard_map/reduce_scatter | solution.py:29
  101.6 70.1 %collective-permute-start.17 = (f32[2,384,512]{2,1,0:T(8,128)}, f32[2,384,512]{2,1,0:T(8,128)}, u32[]{:S(2)}, u32[]{:S(2)}) collective-permute-start(f32[2,384,512]{2,1,0:T(8,128)} %piece.12), channel_id=1, source_target_pairs={{0,8},{4,12},{24,16},{28,20},{1,9},{5,13},{25,17},{29,21},{2,10},{... | collective-permute-start | bytes 4718600 | tf_op jit(solution)/shard_map/ppermute | solution.py:242
  107.0 98.4 %collective-permute-start.22 = (f32[2,384,512]{2,1,0:T(8,128)}, f32[2,384,512]{2,1,0:T(8,128)}, u32[]{:S(2)}, u32[]{:S(2)}) collective-permute-start(f32[2,384,512]{2,1,0:T(8,128)} %piece.17), channel_id=1, source_target_pairs={{0,8},{4,12},{24,16},{28,20},{1,9},{5,13},{25,17},{29,21},{2,10},{... | collective-permute-start | bytes 4718600 | tf_op jit(solution)/shard_map/ppermute | solution.py:242
  131.6 45.9 %collective-permute-start.4 = (f32[512,384]{1,0:T(8,128)}, f32[512,384]{1,0:T(8,128)}, u32[]{:S(2)}, u32[]{:S(2)}) collective-permute-start(f32[512,384]{1,0:T(8,128)} %get-tuple-element.78), channel_id=1, source_target_pairs={{0,4},{4,0},{8,12},{12,8},{16,20},{20,16},{24,28},{28,24},{1,5},{5... | collective-permute-start | bytes 2359304 | tf_op jit(solution)/shard_map/ppermute | solution.py:213
  133.1 44.4 %collective-permute-start.11 = (f32[512,384]{1,0:T(8,128)}, f32[512,384]{1,0:T(8,128)}, u32[]{:S(2)}, u32[]{:S(2)}) collective-permute-start(f32[512,384]{1,0:T(8,128)} %get-tuple-element.77), channel_id=1, source_target_pairs={{0,4},{4,0},{8,12},{12,8},{16,20},{20,16},{24,28},{28,24},{1,5},{5... | collective-permute-start | bytes 2359304 | tf_op jit(solution)/shard_map/ppermute | solution.py:213
  176.3 62.8 %collective-permute-start.18 = (f32[2,384,512]{2,1,0:T(8,128)}, f32[2,384,512]{2,1,0:T(8,128)}, u32[]{:S(2)}, u32[]{:S(2)}) collective-permute-start(f32[2,384,512]{2,1,0:T(8,128)} %piece.13), channel_id=1, source_target_pairs={{0,8},{4,12},{24,16},{28,20},{1,9},{5,13},{25,17},{29,21},{2,10},{... | collective-permute-start | bytes 4718600 | tf_op jit(solution)/shard_map/ppermute | solution.py:242
  210.0 59.5 %collective-permute-start.23 = (f32[2,384,512]{2,1,0:T(8,128)}, f32[2,384,512]{2,1,0:T(8,128)}, u32[]{:S(2)}, u32[]{:S(2)}) collective-permute-start(f32[2,384,512]{2,1,0:T(8,128)} %piece.18), channel_id=1, source_target_pairs={{0,8},{4,12},{24,16},{28,20},{1,9},{5,13},{25,17},{29,21},{2,10},{... | collective-permute-start | bytes 4718600 | tf_op jit(solution)/shard_map/ppermute | solution.py:242
  216.3 59.1 %collective-permute-start.15 = (f32[512,384]{1,0:T(8,128)}, f32[512,384]{1,0:T(8,128)}, u32[]{:S(2)}, u32[]{:S(2)}) collective-permute-start(f32[512,384]{1,0:T(8,128)} %get-tuple-element.73), channel_id=1, source_target_pairs={{0,4},{4,0},{8,12},{12,8},{16,20},{20,16},{24,28},{28,24},{1,5},{5... | collective-permute-start | bytes 2359304 | tf_op jit(solution)/shard_map/ppermute | solution.py:213
  217.8 63.5 %collective-permute-start.33 = (f32[2,384,512]{2,1,0:T(8,128)}, f32[2,384,512]{2,1,0:T(8,128)}, u32[]{:S(2)}, u32[]{:S(2)}) collective-permute-start(f32[2,384,512]{2,1,0:T(8,128)} %piece.13), channel_id=1, source_target_pairs={{8,16},{12,20},{16,8},{20,12},{9,17},{13,21},{17,9},{21,13},{10,18... | collective-permute-start | bytes 4718600 | tf_op jit(solution)/shard_map/ppermute | solution.py:244
  219.7 57.0 %collective-permute-start.6 = (f32[512,384]{1,0:T(8,128)}, f32[512,384]{1,0:T(8,128)}, u32[]{:S(2)}, u32[]{:S(2)}) collective-permute-start(f32[512,384]{1,0:T(8,128)} %get-tuple-element.74), channel_id=1, source_target_pairs={{8,12},{12,8},{16,20},{20,16},{9,13},{13,9},{17,21},{21,17},{10,14... | collective-permute-start | bytes 2359304 | tf_op jit(solution)/shard_map/ppermute | solution.py:213
  239.1 48.2 %collective-permute-start.30 = (f32[2,384,512]{2,1,0:T(8,128)}, f32[2,384,512]{2,1,0:T(8,128)}, u32[]{:S(2)}, u32[]{:S(2)}) collective-permute-start(f32[2,384,512]{2,1,0:T(8,128)} %piece.18), channel_id=1, source_target_pairs={{8,16},{12,20},{16,8},{20,12},{9,17},{13,21},{17,9},{21,13},{10,18... | collective-permute-start | bytes 4718600 | tf_op jit(solution)/shard_map/ppermute | solution.py:244
  269.5 39.5 %collective-permute-start.19 = (f32[2,384,512]{2,1,0:T(8,128)}, f32[2,384,512]{2,1,0:T(8,128)}, u32[]{:S(2)}, u32[]{:S(2)}) collective-permute-start(f32[2,384,512]{2,1,0:T(8,128)} %piece.14), channel_id=1, source_target_pairs={{0,8},{4,12},{24,16},{28,20},{1,9},{5,13},{25,17},{29,21},{2,10},{... | collective-permute-start | bytes 4718600 | tf_op jit(solution)/shard_map/ppermute | solution.py:242
  275.4 63.1 %collective-permute-start.24 = (f32[2,384,512]{2,1,0:T(8,128)}, f32[2,384,512]{2,1,0:T(8,128)}, u32[]{:S(2)}, u32[]{:S(2)}) collective-permute-start(f32[2,384,512]{2,1,0:T(8,128)} %piece.19), channel_id=1, source_target_pairs={{0,8},{4,12},{24,16},{28,20},{1,9},{5,13},{25,17},{29,21},{2,10},{... | collective-permute-start | bytes 4718600 | tf_op jit(solution)/shard_map/ppermute | solution.py:242
  276.7 70.4 %collective-permute-start.26 = (f32[2,384,512]{2,1,0:T(8,128)}, f32[2,384,512]{2,1,0:T(8,128)}, u32[]{:S(2)}, u32[]{:S(2)}) collective-permute-start(f32[2,384,512]{2,1,0:T(8,128)} %piece.14), channel_id=1, source_target_pairs={{8,16},{12,20},{16,8},{20,12},{9,17},{13,21},{17,9},{21,13},{10,18... | collective-permute-start | bytes 4718600 | tf_op jit(solution)/shard_map/ppermute | solution.py:244
  281.3 64.5 %collective-permute-start.16 = (f32[512,384]{1,0:T(8,128)}, f32[512,384]{1,0:T(8,128)}, u32[]{:S(2)}, u32[]{:S(2)}) collective-permute-start(f32[512,384]{1,0:T(8,128)} %get-tuple-element.71), channel_id=1, source_target_pairs={{0,4},{4,0},{24,28},{28,24},{1,5},{5,1},{25,29},{29,25},{2,6},{6,2... | collective-permute-start | bytes 2359304 | tf_op jit(solution)/shard_map/ppermute | solution.py:213
  287.3 108.8 %collective-permute-start.32 = (f32[2,384,512]{2,1,0:T(8,128)}, f32[2,384,512]{2,1,0:T(8,128)}, u32[]{:S(2)}, u32[]{:S(2)}) collective-permute-start(f32[2,384,512]{2,1,0:T(8,128)} %piece.19), channel_id=1, source_target_pairs={{8,16},{12,20},{16,8},{20,12},{9,17},{13,21},{17,9},{21,13},{10,18... | collective-permute-start | bytes 4718600 | tf_op jit(solution)/shard_map/ppermute | solution.py:244
  309.0 83.1 %collective-permute-start.34 = (f32[2,384,512]{2,1,0:T(8,128)}, f32[2,384,512]{2,1,0:T(8,128)}, u32[]{:S(2)}, u32[]{:S(2)}) collective-permute-start(f32[2,384,512]{2,1,0:T(8,128)} %piece.23), channel_id=1, source_target_pairs={{8,0},{12,4},{16,24},{20,28},{9,1},{13,5},{17,25},{21,29},{10,2},{... | collective-permute-start | bytes 4718600 | tf_op jit(solution)/shard_map/ppermute | solution.py:248
  338.6 59.9 %collective-permute-start.31 = (f32[2,384,512]{2,1,0:T(8,128)}, f32[2,384,512]{2,1,0:T(8,128)}, u32[]{:S(2)}, u32[]{:S(2)}) collective-permute-start(f32[2,384,512]{2,1,0:T(8,128)} %piece.22), channel_id=1, source_target_pairs={{8,0},{12,4},{16,24},{20,28},{9,1},{13,5},{17,25},{21,29},{10,2},{... | collective-permute-start | bytes 4718600 | tf_op jit(solution)/shard_map/ppermute | solution.py:248
  345.8 39.5 %collective-permute-start.20 = (f32[2,384,512]{2,1,0:T(8,128)}, f32[2,384,512]{2,1,0:T(8,128)}, u32[]{:S(2)}, u32[]{:S(2)}) collective-permute-start(f32[2,384,512]{2,1,0:T(8,128)} %piece.15), channel_id=1, source_target_pairs={{0,8},{4,12},{24,16},{28,20},{1,9},{5,13},{25,17},{29,21},{2,10},{... | collective-permute-start | bytes 4718600 | tf_op jit(solution)/shard_map/ppermute | solution.py:242
  347.1 71.9 %collective-permute-start.28 = (f32[2,384,512]{2,1,0:T(8,128)}, f32[2,384,512]{2,1,0:T(8,128)}, u32[]{:S(2)}, u32[]{:S(2)}) collective-permute-start(f32[2,384,512]{2,1,0:T(8,128)} %piece.20), channel_id=1, source_target_pairs={{0,8},{4,12},{24,16},{28,20},{1,9},{5,13},{25,17},{29,21},{2,10},{... | collective-permute-start | bytes 4718600 | tf_op jit(solution)/shard_map/ppermute | solution.py:242
  385.4 44.9 %collective-permute-start.29 = (f32[2,384,512]{2,1,0:T(8,128)}, f32[2,384,512]{2,1,0:T(8,128)}, u32[]{:S(2)}, u32[]{:S(2)}) collective-permute-start(f32[2,384,512]{2,1,0:T(8,128)} %piece.15), channel_id=1, source_target_pairs={{8,16},{12,20},{16,8},{20,12},{9,17},{13,21},{17,9},{21,13},{10,18... | collective-permute-start | bytes 4718600 | tf_op jit(solution)/shard_map/ppermute | solution.py:244
  392.1 55.0 %collective-permute-start.25 = (f32[2,384,512]{2,1,0:T(8,128)}, f32[2,384,512]{2,1,0:T(8,128)}, u32[]{:S(2)}, u32[]{:S(2)}) collective-permute-start(f32[2,384,512]{2,1,0:T(8,128)} %piece.20), channel_id=1, source_target_pairs={{8,16},{12,20},{16,8},{20,12},{9,17},{13,21},{17,9},{21,13},{10,18... | collective-permute-start | bytes 4718600 | tf_op jit(solution)/shard_map/ppermute | solution.py:244
  396.1 40.3 %collective-permute-start.27 = (f32[2,384,512]{2,1,0:T(8,128)}, f32[2,384,512]{2,1,0:T(8,128)}, u32[]{:S(2)}, u32[]{:S(2)}) collective-permute-start(f32[2,384,512]{2,1,0:T(8,128)} %piece.21), channel_id=1, source_target_pairs={{8,0},{12,4},{16,24},{20,28},{9,1},{13,5},{17,25},{21,29},{10,2},{... | collective-permute-start | bytes 4718600 | tf_op jit(solution)/shard_map/ppermute | solution.py:248
  398.5 49.0 %collective-permute-start.21 = (f32[2,384,512]{2,1,0:T(8,128)}, f32[2,384,512]{2,1,0:T(8,128)}, u32[]{:S(2)}, u32[]{:S(2)}) collective-permute-start(f32[2,384,512]{2,1,0:T(8,128)} %piece.16), channel_id=1, source_target_pairs={{0,8},{4,12},{24,16},{28,20},{1,9},{5,13},{25,17},{29,21},{2,10},{... | collective-permute-start | bytes 4718600 | tf_op jit(solution)/shard_map/ppermute | solution.py:242
  (20 other events, 450.2 us)
Sparse Core Ops, SparseCore 0:
  364.8 29.3 reduce-scatter.1

commit v2 on v0

v2 whole, which is shorter than its diff:
```python
import functools

import jax
import jax.numpy as jnp
from jax import lax
from jax.experimental import pallas as pl
from jax.experimental.pallas import tpu as pltpu
from jax.sharding import PartitionSpec as P

PIECES = 3
FLOPS = 100_000_000_000
VMEM_LIMIT = 56 * 1024 * 1024


def contract_rows(left, right):
    return lax.dot_general(
        left, right, (((0,), (0,)), ((), ())), preferred_element_type=jnp.float32
    )


def hidden_grads(out_grads, pre_act, w_out):
    back = lax.dot_general(
        out_grads, w_out, (((1,), (1,)), ((), ())), preferred_element_type=jnp.float32
    )
    return jnp.where(pre_act > 0, back, jnp.zeros_like(back)).astype(jnp.bfloat16)


def input_grads(grad_hidden, w_in):
    return lax.psum_scatter(
        jnp.dot(grad_hidden, w_in, preferred_element_type=jnp.float32),
        "blk",
        scatter_dimension=0,
        tiled=True,
    ).astype(jnp.bfloat16)


def plain_body(inputs, out_grads, pre_act, w_in, w_out):
    token_total = inputs.shape[0] * lax.axis_size("dp")
    factor = lax.rsqrt(jnp.asarray(token_total, jnp.float32))
    act = jnp.maximum(pre_act, jnp.zeros_like(pre_act))
    grad_hidden = hidden_grads(out_grads, pre_act, w_out)
    grad_out = contract_rows(act, out_grads) * factor
    grad_in = contract_rows(grad_hidden, inputs) * factor
    return (
        input_grads(grad_hidden, w_in),
        lax.psum_scatter(grad_in, "dp", scatter_dimension=0, tiled=True),
        lax.psum_scatter(grad_out, "dp", scatter_dimension=0, tiled=True),
    )


def params():
    return pltpu.CompilerParams(vmem_limit_bytes=VMEM_LIMIT)


def anywhere(arrays):
    return [pl.BlockSpec(memory_space=pl.ANY)] * len(arrays)


def start_kernel(idx_ref, grads_ref, inputs_ref, *refs):
    columns, (quarter_ref, *outs) = refs[:4], refs[4:]
    quarter, rows = grads_ref.shape[0], columns[0].shape[0]
    quarter_ref[:quarter, :] = grads_ref[...].astype(jnp.float32)
    quarter_ref[quarter:, :] = inputs_ref[...].astype(jnp.float32)
    for k, ref in enumerate(columns):
        place = k % 2
        outs[k // 2][place * rows : (place + 1) * rows, :] = ref[...].astype(jnp.float32)


def start_sends(blk, out_grads, inputs, columns, pre_act, size):
    rows, width = out_grads.shape
    quarter = rows // 4
    tokens = pl.BlockSpec((quarter, width), lambda i, idx: (idx[0], 0))
    shapes = [(2 * quarter, width), (2 * rows, size), (2 * rows, size)]
    return pl.pallas_call(
        start_kernel,
        grid_spec=pltpu.PrefetchScalarGridSpec(
            num_scalar_prefetch=1,
            grid=(1,),
            in_specs=[tokens, tokens]
            + [pl.BlockSpec((rows, size), lambda i, idx, k=k: (0, idx[k])) for k in (1, 2, 3, 4)],
            out_specs=[pl.BlockSpec(shape, lambda i, idx: (0, 0)) for shape in shapes],
        ),
        out_shape=[jax.ShapeDtypeStruct(shape, jnp.float32) for shape in shapes],
        compiler_params=params(),
        cost_estimate=piece_cost(),
        name="start_sends",
    )(jnp.stack([blk, *columns]), out_grads, inputs, *([pre_act] * 4))


def join_kernel(blk_ref, grads_ref, inputs_ref, *refs):
    quarters, (g_ref, x_ref) = refs[:4], refs[-2:]
    rows = grads_ref.shape[0]
    quarter = rows // 4
    g_ref[:rows, :] = grads_ref[...]
    x_ref[:rows, :] = inputs_ref[...]
    for flip, ref in enumerate(quarters):
        where = jnp.bitwise_xor(blk_ref[0], flip)
        place = pl.ds(pl.multiple_of(rows + where * quarter, quarter), quarter)
        g_ref[place, :] = ref[:quarter, :].astype(jnp.bfloat16)
        x_ref[place, :] = ref[quarter:, :].astype(jnp.bfloat16)


def join(blk, out_grads, inputs, quarters, after):
    rows, width = out_grads.shape
    shape = jax.ShapeDtypeStruct((2 * rows, width), jnp.bfloat16)
    vmem = pl.BlockSpec(memory_space=pltpu.VMEM)
    return pl.pallas_call(
        join_kernel,
        out_shape=(shape, shape),
        in_specs=[pl.BlockSpec(memory_space=pltpu.SMEM)] + [vmem] * 6 + anywhere(after),
        out_specs=(vmem, vmem),
        compiler_params=params(),
        name="join_tokens",
    )(blk.reshape(1), out_grads, inputs, *quarters, *after)


def input_kernel(grads_ref, pre_ref, out_rows_ref, in_rows_ref, *refs):
    total_ref = refs[-1]

    @pl.when(pl.program_id(0) == 0)
    def _():
        total_ref[...] = jnp.zeros_like(total_ref)

    hidden = hidden_grads(grads_ref[...], pre_ref[...], out_rows_ref[...])
    total_ref[...] += jnp.dot(hidden, in_rows_ref[...], preferred_element_type=jnp.float32)


def input_partial(out_grads, pre_act, w_in, w_out, size, after):
    rows, hidden = pre_act.shape
    width = out_grads.shape[1]
    tokens = pl.BlockSpec((rows, width), lambda i: (0, 0))
    weights = pl.BlockSpec((size, width), lambda i: (i, 0))
    return pl.pallas_call(
        input_kernel,
        grid=(hidden // size,),
        in_specs=[tokens, pl.BlockSpec((rows, size), lambda i: (0, i)), weights, weights] + anywhere(after),
        out_specs=tokens,
        out_shape=jax.ShapeDtypeStruct((rows, width), jnp.float32),
        compiler_params=params(),
        cost_estimate=piece_cost(),
        name="input_partial",
    )(out_grads, pre_act, w_out, w_in, *after)


def piece_math(scale, own, partner, g, x, w):
    pre = jnp.concatenate([own, partner.astype(jnp.bfloat16)], axis=0)
    hidden = hidden_grads(g, pre, w)
    act = jnp.maximum(pre, jnp.zeros_like(pre))
    return contract_rows(hidden, x) * scale, contract_rows(act, g) * scale


def piece_kernel(scale, counts, idx_ref, own_ref, g_ref, x_ref, w_ref, *refs):
    groups = []
    for n in counts:
        groups.append(refs[:n])
        refs = refs[n:]
    partners, others, columns, sums, _, (out_ref, *sends) = groups + [refs]
    partner = jnp.concatenate([ref[...] for ref in partners], axis=1)
    for ref in others:
        partner = jnp.where(idx_ref[2] > 0, ref[...], partner)
    grad_in, grad_out = piece_math(scale, own_ref[...], partner, g_ref[...], x_ref[...], w_ref[...])
    for ref in sums:
        grad_in = grad_in + ref[0]
        grad_out = grad_out + ref[1]
    out_ref[0], out_ref[1] = grad_in, grad_out
    rows = own_ref.shape[0]
    for ref in sends:
        n = ref.shape[0] // rows
        for k in range(n):
            ref[k * rows : (k + 1) * rows, :] = columns[k][...].astype(jnp.float32)
        columns = columns[n:]


def piece_specs(rows, size, width):
    tokens = pl.BlockSpec((2 * rows, width), lambda i, idx: (0, 0))
    return [
        pl.BlockSpec((rows, size), lambda i, idx: (0, idx[0])),
        tokens,
        tokens,
        pl.BlockSpec((size, width), lambda i, idx: (idx[0], 0)),
    ]


def partner_spec(rows, size, place):
    return pl.BlockSpec((rows, size), lambda i, idx: (place, 0))


def piece_cost(flops=1):
    return pl.CostEstimate(flops=flops, bytes_accessed=1, transcendentals=0)


def piece(
    scale, index, pre_act, partners, place, g, x, w_out, sums=(), other=None, is_inner=None, sends=(), after=(), flops=1
):
    rows, width = pre_act.shape[0], g.shape[1]
    size = sum(p.shape[1] for p in partners)
    whole = pl.BlockSpec((2, size, width), lambda i, idx: (0, 0, 0))
    others, other_specs = [], []
    if other is not None:
        others = [other[0]]
        other_specs = [partner_spec(rows, size, other[1])]
    columns = [column for send in sends for column in send]
    zero = jnp.int32(0)
    counts = (len(partners), len(others), len(columns), len(sums), len(after))
    out, *blocks = pl.pallas_call(
        functools.partial(piece_kernel, scale, counts),
        grid_spec=pltpu.PrefetchScalarGridSpec(
            num_scalar_prefetch=1,
            grid=(1,),
            in_specs=piece_specs(rows, size, width)
            + [partner_spec(rows, p.shape[1], place) for p in partners]
            + other_specs
            + [pl.BlockSpec((rows, size), lambda i, idx, k=k: (0, idx[3 + k])) for k in range(len(columns))]
            + [whole] * len(sums)
            + anywhere(after),
            out_specs=[whole] + [pl.BlockSpec((len(send) * rows, size), lambda i, idx: (0, 0)) for send in sends],
        ),
        out_shape=[jax.ShapeDtypeStruct((2, size, width), jnp.float32)]
        + [jax.ShapeDtypeStruct((len(send) * rows, size), jnp.float32) for send in sends],
        compiler_params=params(),
        cost_estimate=piece_cost(flops),
        name="piece",
    )(
        jnp.stack([index, zero, zero if is_inner is None else is_inner, *columns]),
        pre_act,
        g,
        x,
        w_out,
        *partners,
        *others,
        *([pre_act] * len(columns)),
        *sums,
        *after,
    )
    return out, *blocks


def final_kernel(scale, idx_ref, own_ref, g_ref, x_ref, w_ref, partner_ref, inner_ref, outer_ref, *refs):
    sum_ref, (in_ref, out_ref) = refs[0], refs[-2:]
    grad_in, grad_out = piece_math(
        scale, own_ref[...], partner_ref[...], g_ref[...], x_ref[...], w_ref[...]
    )
    is_inner = idx_ref[1] > 0
    in_ref[...] = jnp.where(is_inner, inner_ref[0], grad_in + outer_ref[0]) + sum_ref[0]
    out_ref[...] = jnp.where(is_inner, inner_ref[1], grad_out + outer_ref[1]) + sum_ref[1]


def final_first(scale, count, index, is_inner, pre_act, partner, place, g, x, w_out, held, received, added, after):
    rows, size, width = pre_act.shape[0], partner.shape[1], g.shape[1]
    whole = pl.BlockSpec((2, size, width), lambda i, idx: (0, 0, 0))
    shape = jax.ShapeDtypeStruct((count * size, width), jnp.float32)
    return pl.pallas_call(
        functools.partial(final_kernel, scale),
        grid_spec=pltpu.PrefetchScalarGridSpec(
            num_scalar_prefetch=1,
            grid=(1,),
            in_specs=piece_specs(rows, size, width)
            + [partner_spec(rows, size, place)]
            + [whole] * 3
            + anywhere(after),
            out_specs=[pl.BlockSpec((size, width), lambda i, idx: (0, 0))] * 2,
        ),
        out_shape=(shape, shape),
        compiler_params=params(),
        cost_estimate=piece_cost(),
        name="final_first",
    )(jnp.stack([index, is_inner]), pre_act, g, x, w_out, partner, held, received, added, *after)


def add_kernel(a_ref, b_ref, *refs):
    in_ref, out_ref = refs[-2:]
    in_ref[...] = a_ref[0] + b_ref[0]
    out_ref[...] = a_ref[1] + b_ref[1]


def final_add(place, a, b, held, after):
    _, size, width = a.shape
    steps = 3
    block = pl.BlockSpec((2, size // steps, width), lambda i: (0, i, 0))
    return pl.pallas_call(
        add_kernel,
        grid=(steps,),
        in_specs=[block, block] + anywhere(held) + anywhere(after),
        out_specs=[pl.BlockSpec((size // steps, width), lambda i: (place * steps + i, 0))] * 2,
        out_shape=[jax.ShapeDtypeStruct(h.shape, h.dtype) for h in held],
        input_output_aliases={2: 0, 3: 1},
        compiler_params=params(),
        name="final_add",
    )(a, b, *held, *after)


def line_body(inputs, out_grads, pre_act, w_in, w_out):
    count = PIECES
    rows, hidden = pre_act.shape
    size = hidden // (8 * count)
    scale = 1.0 / (rows * lax.axis_size("dp")) ** 0.5
    me, blk = lax.axis_index("dp"), lax.axis_index("blk")
    plane, half = me // 2, me % 2
    side = plane // 2
    inner = jnp.where((plane == 1) | (plane == 2), 1, 0).astype(jnp.int32)

    def by_role(on_inner, on_outer):
        return jnp.where(inner > 0, jnp.int32(on_inner), jnp.int32(on_outer))

    def links(pairs):
        return [(2 * a + h, 2 * b + h) for a, b in pairs for h in range(2)]

    def swap(array, planes):
        return lax.ppermute(array, "dp", [(2 * a + h, 2 * a + 1 - h) for a in planes for h in range(2)])

    def flip(array, bit):
        return lax.ppermute(array, "blk", [(i, i ^ bit) for i in range(4)])

    outer_to_inner = links([(0, 1), (3, 2)])
    inner_to_inner = links([(1, 2), (2, 1)])
    inner_to_outer = links([(1, 0), (2, 3)])
    every, outer_planes, inner_planes = (0, 1, 2, 3), (0, 3), (1, 2)

    def block(q, which):
        place = q // count
        chunk = jnp.where(side == 0, 3 - place, place)
        return (chunk * 2 + which) * count + q % count

    def mine(q):
        return block(q, half)

    def theirs(q):
        return block(q, 1 - half)

    near_inner = [2 * count + j for j in range(count)]
    near_outer = [3 * count + j for j in range(count)]
    steps = 3 * count - 1
    ahead = [s if s < 2 * count else s + 1 for s in range(steps)]
    main = [by_role(min(max(s - 2, 0), 2 * count - 1), ahead[s]) for s in range(steps)]
    own_chunk = [by_role(near_inner[j], near_outer[j]) for j in range(count)]
    double = steps - count
    first = jnp.int32(near_inner[0])

    quarter, send, raw = start_sends(
        blk,
        out_grads,
        inputs,
        [theirs(main[0]), theirs(main[1]), theirs(first), mine(first)],
        pre_act,
        size,
    )
    pair_0 = swap(quarter, every)
    received = swap(send, outer_planes)
    y = {0: (received, 0), 1: (received, 1)}
    quarter_in = lax.ppermute(quarter, "dp", outer_to_inner)
    raw_in = lax.ppermute(raw, "dp", outer_to_inner)
    pair_1, pair_2 = flip(pair_0, 1), flip(pair_0, 2)
    pair_3 = flip(pair_2, 1)
    g, x = join(blk, out_grads, inputs, [pair_0, pair_1, pair_2, pair_3], [])
    last = g

    def run(q, partner, **more):
        return piece(scale, mine(q), pre_act, [partner[0]], partner[1], g, x, w_out, **more)

    no, own = {}, {}
    toward, across = [], {}
    for s in range(steps):
        block_names, sends = [], []
        if s % 2 == 0:
            for store, key, q in (
                (y, s + 2, main[s + 2] if s + 2 < steps else None),
                (y, s + 3, main[s + 3] if s + 3 < steps else None),
                (no, s // 2, jnp.int32(near_outer[s // 2]) if s // 2 < count else None),
            ):
                if q is not None:
                    block_names.append((store, key))
                    sends.append(theirs(q))
            if s + 2 >= steps:
                for i in range(1, count):
                    block_names.append((own, i))
                    sends.append(theirs(own_chunk[i]))
        sums = [toward[s - 2]] if s >= 2 else []
        held_back = ([across[s - 4]] if s >= 4 else []) + ([raw_in, quarter_in] if s == 0 else []) + ([first_in] if s == 3 else [])
        j = s - double
        if j < 0:
            after = [last] + held_back
        else:
            (last,) = run(
                by_role(near_outer[j], ahead[s]),
                y[s],
                sums=[across[j]],
                other=no[j],
                is_inner=inner,
                after=[last] + sums + held_back,
            )
            toward.append(lax.ppermute(last, "dp", outer_to_inner + inner_to_outer))
            after = [last] + ([grad_inputs] if j == 0 else [])
        out, *blocks = run(main[s], y[s], sums=sums, sends=[sends] if sends else [], after=after, flops=FLOPS if s == 3 else 1)
        last = out
        if j < 0:
            toward.append(lax.ppermute(out, "dp", outer_to_inner))
        if blocks:
            received = swap(blocks[0], every)
            for place, (store, key) in enumerate(block_names):
                store[key] = (received, place)
        if s >= 2:
            across[s - 2] = lax.ppermute(out, "dp", inner_to_inner)
        if s == 1:
            in_1, in_2 = flip(quarter_in, 1), flip(quarter_in, 2)
            in_3 = flip(in_2, 1)
            line_g, line_x = join(blk, out_grads, inputs, [quarter_in, in_1, in_2, in_3], [last])
            (last,) = piece(scale, theirs(first), pre_act, [raw_in], 0, line_g, line_x, w_out, after=[last])
            first_in = swap(last, inner_planes)
            last = input_partial(out_grads, pre_act, w_in, w_out, 4 * size, [last])
            grad_inputs = lax.psum_scatter(last, "blk", scatter_dimension=0, tiled=True)
            grad_inputs = grad_inputs.astype(jnp.bfloat16)
        if s == 4:
            (held_in,) = piece(
                scale, mine(first), pre_act, [raw_in], 1, line_g, line_x, w_out, sums=[first_in], after=[last]
            )
            last = held_in

    held = final_first(
        scale,
        count,
        mine(jnp.int32(near_outer[0])),
        inner,
        pre_act,
        no[0][0],
        no[0][1],
        g,
        x,
        w_out,
        held_in,
        toward[double],
        across[count],
        [last],
    )
    for i in range(1, count):
        (out,) = run(own_chunk[i], own[i], sums=[across[count + i]], after=[held[0]])
        held = final_add(i, out, toward[double + i], held, [])
    return (grad_inputs, held[0], held[1])


def solution(mesh):
    def body(inputs, out_grads, pre_act, w_in, w_out):
        fits = pre_act.shape[1] % (8 * PIECES * 128) == 0 and inputs.shape[0] % 64 == 0
        run = line_body if (mesh.shape["dp"], mesh.shape["blk"]) == (8, 4) and fits else plain_body
        return run(inputs, out_grads, pre_act, w_in, w_out)

    return jax.shard_map(
        body,
        mesh=mesh,
        in_specs=(P("dp", None), P("dp", None), P("dp", "blk"), P("blk", None), P("blk", None)),
        out_specs=(P(("dp", "blk"), None), P(("blk", "dp"), None), P(("blk", "dp"), None)),
        check_vma=False,
    )
```

time: 702 us -> 381 us (0.54)
  waiting for transfers between devices: 633 us -> 173 us
  Pallas kernels: 0 us -> 133 us
  matrix products: 50.1 us -> 0 us
  starting transfers between devices: 0.12 us -> 39.2 us
  local copies, waits for them, and re-layouts: 1 us -> 14.5 us
    reduce_scatter x3 -> x1, waiting for transfers between devices: 633 us -> 0.01 us  [line_body(): grad_inputs = lax.psum_scatter(last, 'blk', scatter_dimension=0, tiled=True)]
    ppermute x0 -> x29, waiting for transfers between devices: none -> 173 us  [the longest x7 77.1 us: swap(): lax.ppermute(array, 'dp', [(2 * a + h, 2 * a + 1 - h) for a in planes for...]
    pallas_call x0 -> x22, Pallas kernels: none -> 133 us  [the longest x15 92.3 us: piece(): pl.pallas_call(functools.partial(piece_kernel, scale, counts), grid_spec=...]
    dot_general x4 -> x0, matrix products: 50.1 us -> none  [the longest x2 26.2 us: contract_rows(): lax.dot_general(left, right, (((0,), (0,)), ((), ())), preferred_element_...]
    ppermute x0 -> x29, starting transfers between devices: none -> 39.2 us  [the longest x6 13.7 us: line_body(): across[s - 2] = lax.ppermute(out, 'dp', inner_to_inner)]
  transfers between devices with their start and end apart: 3 -> 30, of which waited for: 2 -> 14; matrix products, arithmetic and copies ran while one was open for 4% -> 3% of each run, Pallas kernels for 0% -> 33%
where the time goes in v2:
time: 381 us; the launch traced here: 380 us
  waiting for transfers between devices  173 us (45%)
  Pallas kernels  133 us (35%)
  starting transfers between devices  39.2 us (10%)
  local copies, waits for them, and re-layouts  14.5 us (4%)
  between operations  14.5 us (4%)
  other arithmetic  4.8 us (1%)
    pallas_call x15, Pallas kernels, piece(): pl.pallas_call(functools.partial(piece_kernel, scale, counts), grid_spec=...  92.3 us
    ppermute x7, waiting for transfers between devices, swap(): lax.ppermute(array, 'dp', [(2 * a + h, 2 * a + 1 - h) for a in planes for...  77.1 us
    ppermute x6, waiting for transfers between devices, line_body(): across[s - 2] = lax.ppermute(out, 'dp', inner_to_inner)  40.5 us
    ppermute x1, waiting for transfers between devices, line_body(): quarter_in = lax.ppermute(quarter, 'dp', outer_to_inner)  25.1 us
    ppermute x5, waiting for transfers between devices, line_body(): toward.append(lax.ppermute(out, 'dp', outer_to_inner))  20.6 us
    pallas_call x1, Pallas kernels, input_partial(): pl.pallas_call(input_kernel, grid=(hidden // size,), in_specs=[tokens, pl...  16.2 us
    ppermute x6, starting transfers between devices, line_body(): across[s - 2] = lax.ppermute(out, 'dp', inner_to_inner)  13.7 us
    ppermute x7, starting transfers between devices, swap(): lax.ppermute(array, 'dp', [(2 * a + h, 2 * a + 1 - h) for a in planes for...  11 us
  transfers between devices with their start and end apart: 30, of which 14 were waited for; matrix products, arithmetic and copies ran while one was open for 3% of the time, Pallas kernels for 33%

profile of v2, /device:TPU:16, one launch (start us, length us, event | category | flops | bytes accessed | tf_op | source)
XLA Modules:
  0.0 380.0 jit_solution(14315337527355430334)
XLA Ops:
  15.6 10.4 %collective-permute-done.4.refs_0_ = f32[256,512]{1,0:T(8,128)} collective-permute-done((f32[256,512]{1,0:T(8,128)}, f32[256,512]{1,0:T(8,128)}, u32[]{:S(2)}, u32[]{:S(2)}) %collective-permute-start.4) | collective-permute-done | bytes 524320 | tf_op jit(solution)/shard_map/ppermute | solution.py:309
  28.9 10.2 %collective-permute-done.6.refs_2_ = f32[256,512]{1,0:T(8,128)} collective-permute-done((f32[256,512]{1,0:T(8,128)}, f32[256,512]{1,0:T(8,128)}, u32[]{:S(2)}, u32[]{:S(2)}) %collective-permute-start.6) | collective-permute-done | bytes 524320 | tf_op jit(solution)/shard_map/ppermute | solution.py:312
  39.1 25.1 %collective-permute-done.refs_6_.refs_0_ = f32[256,512]{1,0:T(8,128)} collective-permute-done((f32[256,512]{1,0:T(8,128)}, f32[256,512]{1,0:T(8,128)}, u32[]{:S(2)}, u32[]{:S(2)}) %collective-permute-start) | collective-permute-done | bytes 524320 | tf_op jit(solution)/shard_map/ppermute | solution.py:350
  71.4 6.6 %piece.15 = (f32[2,384,512]{2,1,0:T(8,128)}, f32[1536,384]{1,0:T(8,128)}) custom-call(s32[6]{0:T(128)} %stack.159.idx_ref, bf16[512,9216]{1,0:T(8,128)(2,1)} %own_ref.31, bf16[1024,512]{1,0:T(8,128)(2,1)} %get-tuple-element.25.g_ref.refs_4_, bf16[1024,512]{1,0:T(8,128)(2,1)} %get-tuple-element.26.x_ref, bf16[9216,512]{1,0:T(8,128)(2,1)} %w_ref.31, ...), custom_call_target="tpu_custom_call" | custom-call | flops 1 | bytes 1 | tf_op jit(solution)/shard_map/piece/pallas_call | solution.py:205
  103.0 16.2 %input_partial.1.refs_5_ = f32[512,512]{1,0:T(8,128)} custom-call(bf16[512,512]{1,0:T(8,128)(2,1)} %grads_ref.7, bf16[512,9216]{1,0:T(8,128)(2,1)} %own_ref.31, bf16[9216,512]{1,0:T(8,128)(2,1)} %w_ref.31, bf16[9216,512]{1,0:T(8,128)(2,1)} %in_rows_ref.1, f32[2,384,512]{2,1,0:T(8,128)} %piece.17.refs_0_), custom_call_target="tpu_custom_call" | custom-call | flops 1 | bytes 1 | tf_op jit(solution)/shard_map/input_partial/pallas_call | solution.py:133
  120.0 12.3 %collective-permute-done.10.refs_0_.refs_1_.partner_ref = f32[1536,384]{1,0:T(8,128)S(1)} collective-permute-done((f32[1536,384]{1,0:T(8,128)}, f32[1536,384]{1,0:T(8,128)S(1)}, u32[]{:S(2)}, u32[]{:S(2)}) %collective-permute-start.10) | collective-permute-done | bytes 2359328 | tf_op jit(solution)/shard_map/ppermute | solution.py:309
  133.8 7.0 %piece.18 = (f32[2,384,512]{2,1,0:T(8,128)}, f32[1536,384]{1,0:T(8,128)}) custom-call(s32[6]{0:T(128)} %stack.175.idx_ref, bf16[512,9216]{1,0:T(8,128)(2,1)} %own_ref.31, bf16[1024,512]{1,0:T(8,128)(2,1)} %get-tuple-element.25.g_ref.refs_4_, bf16[1024,512]{1,0:T(8,128)(2,1)} %get-tuple-element.26.x_ref, bf16[9216,512]{1,0:T(8,128)(2,1)} %w_ref.31, ...), custom_call_target="tpu_custom_call" | custom-call | flops 1 | bytes 1 | tf_op jit(solution)/shard_map/piece/pallas_call | solution.py:205
  145.6 20.6 %collective-permute-done.15.refs_3_.refs_1_ = f32[2,384,512]{2,1,0:T(8,128)} collective-permute-done((f32[2,384,512]{2,1,0:T(8,128)}, f32[2,384,512]{2,1,0:T(8,128)}, u32[]{:S(2)}, u32[]{:S(2)}) %collective-permute-start.15) | collective-permute-done | bytes 1572896 | tf_op jit(solution)/shard_map/ppermute | solution.py:309
  176.2 11.3 %collective-permute-done.13.refs_4_ = f32[2,384,512]{2,1,0:T(8,128)} collective-permute-done((f32[2,384,512]{2,1,0:T(8,128)}, f32[2,384,512]{2,1,0:T(8,128)}, u32[]{:S(2)}, u32[]{:S(2)}) %collective-permute-start.13) | collective-permute-done | bytes 1572896 | tf_op jit(solution)/shard_map/ppermute | solution.py:396
  187.5 26.5 %collective-permute-done.12.refs_0_.refs_1_ = f32[1536,384]{1,0:T(8,128)S(1)} collective-permute-done((f32[1536,384]{1,0:T(8,128)}, f32[1536,384]{1,0:T(8,128)S(1)}, u32[]{:S(2)}, u32[]{:S(2)}) %collective-permute-start.12) | collective-permute-done | bytes 2359328 | tf_op jit(solution)/shard_map/ppermute | solution.py:309
  215.4 7.0 %piece.20 = (f32[2,384,512]{2,1,0:T(8,128)}, f32[1536,384]{1,0:T(8,128)}) custom-call(s32[6]{0:T(128)} %stack.170.idx_ref, bf16[512,9216]{1,0:T(8,128)(2,1)} %own_ref.31, bf16[1024,512]{1,0:T(8,128)(2,1)} %get-tuple-element.25.g_ref.refs_4_, bf16[1024,512]{1,0:T(8,128)(2,1)} %get-tuple-element.26.x_ref, bf16[9216,512]{1,0:T(8,128)(2,1)} %w_ref.31, ...), custom_call_target="tpu_custom_call" | custom-call | flops 1 | bytes 1 | tf_op jit(solution)/shard_map/piece/pallas_call | solution.py:205
  236.6 6.2 %piece.22.refs_2_ = f32[2,384,512]{2,1,0:T(8,128)} custom-call(s32[3]{0:T(128)} %fusion.1.idx_ref, bf16[512,9216]{1,0:T(8,128)(2,1)} %own_ref.31, bf16[1024,512]{1,0:T(8,128)(2,1)} %get-tuple-element.25.g_ref.refs_4_, bf16[1024,512]{1,0:T(8,128)(2,1)} %get-tuple-element.26.x_ref, bf16[9216,512]{1,0:T(8,128)(2,1)} %w_ref.31, f32[1536,384]{1,0:T(8,128)} %copy-done.1, ...), custom_call_target="tpu_custom_call" | custom-call | flops 1 | bytes 1 | tf_op jit(solution)/shard_map/piece/pallas_call | solution.py:205
  242.8 5.9 %piece.23.refs_3_ = f32[2,384,512]{2,1,0:T(8,128)} custom-call(s32[3]{0:T(128)} %stack.182.idx_ref, bf16[512,9216]{1,0:T(8,128)(2,1)} %own_ref.31, bf16[1024,512]{1,0:T(8,128)(2,1)} %get-tuple-element.25.g_ref.refs_4_, bf16[1024,512]{1,0:T(8,128)(2,1)} %get-tuple-element.26.x_ref, bf16[9216,512]{1,0:T(8,128)(2,1)} %w_ref.31, f32[1536,384]{1,0:T(8,128)} %copy-done.1, ...), custom_call_target="tpu_custom_call" | custom-call | flops 1 | bytes 1 | tf_op jit(solution)/shard_map/piece/pallas_call | solution.py:205
  256.2 8.6 %collective-permute-done.18.refs_4_.refs_3_ = f32[2,384,512]{2,1,0:T(8,128)} collective-permute-done((f32[2,384,512]{2,1,0:T(8,128)}, f32[2,384,512]{2,1,0:T(8,128)}, u32[]{:S(2)}, u32[]{:S(2)}) %collective-permute-start.18) | collective-permute-done | bytes 1572896 | tf_op jit(solution)/shard_map/ppermute | solution.py:396
  266.1 7.2 %collective-permute-done.17.refs_0_.refs_1_ = f32[1536,384]{1,0:T(8,128)S(1)} collective-permute-done((f32[1536,384]{1,0:T(8,128)}, f32[1536,384]{1,0:T(8,128)S(1)}, u32[]{:S(2)}, u32[]{:S(2)}) %collective-permute-start.17) | collective-permute-done | bytes 2359328 | tf_op jit(solution)/shard_map/ppermute | solution.py:309
  274.7 6.2 %piece.24.refs_4_ = f32[2,384,512]{2,1,0:T(8,128)} custom-call(s32[3]{0:T(128)} %fusion.idx_ref, bf16[512,9216]{1,0:T(8,128)(2,1)} %own_ref.31, bf16[1024,512]{1,0:T(8,128)(2,1)} %get-tuple-element.25.g_ref.refs_4_, bf16[1024,512]{1,0:T(8,128)(2,1)} %get-tuple-element.26.x_ref, bf16[9216,512]{1,0:T(8,128)(2,1)} %w_ref.31, f32[1536,384]{1,0:T(8,128)} %copy-done, ...), custom_call_target="tpu_custom_call" | custom-call | flops 1 | bytes 1 | tf_op jit(solution)/shard_map/piece/pallas_call | solution.py:205
  281.4 6.8 %piece.25 = (f32[2,384,512]{2,1,0:T(8,128)}, f32[1024,384]{1,0:T(8,128)}) custom-call(s32[5]{0:T(128)} %pad_add_fusion.3.idx_ref, bf16[512,9216]{1,0:T(8,128)(2,1)} %own_ref.31, bf16[1024,512]{1,0:T(8,128)(2,1)} %get-tuple-element.25.g_ref.refs_4_, bf16[1024,512]{1,0:T(8,128)(2,1)} %get-tuple-element.26.x_ref, bf16[9216,512]{1,0:T(8,128)(2,1)} %w_ref.31, ...), custom_call_target="tpu_custom_call" | custom-call | flops 1 | bytes 1 | tf_op jit(solution)/shard_map/piece/pallas_call | solution.py:205
  291.8 7.9 %collective-permute-done.24.refs_5_.refs_0_ = f32[2,384,512]{2,1,0:T(8,128)} collective-permute-done((f32[2,384,512]{2,1,0:T(8,128)}, f32[2,384,512]{2,1,0:T(8,128)}, u32[]{:S(2)}, u32[]{:S(2)}) %collective-permute-start.24) | collective-permute-done | bytes 1572896 | tf_op jit(solution)/shard_map/ppermute | solution.py:402
  299.8 6.1 %piece.26.refs_2_ = f32[2,384,512]{2,1,0:T(8,128)} custom-call(s32[3]{0:T(128)} %fusion.2.idx_ref, bf16[512,9216]{1,0:T(8,128)(2,1)} %own_ref.31, bf16[1024,512]{1,0:T(8,128)(2,1)} %get-tuple-element.25.g_ref.refs_4_, bf16[1024,512]{1,0:T(8,128)(2,1)} %get-tuple-element.26.x_ref, bf16[9216,512]{1,0:T(8,128)(2,1)} %w_ref.31, f32[1536,384]{1,0:T(8,128)} %copy-done, ...), custom_call_target="tpu_custom_call" | custom-call | flops 1 | bytes 1 | tf_op jit(solution)/shard_map/piece/pallas_call | solution.py:205
  305.9 6.0 %piece.27.refs_1_ = f32[2,384,512]{2,1,0:T(8,128)} custom-call(s32[3]{0:T(128)} %stack.187.idx_ref, bf16[512,9216]{1,0:T(8,128)(2,1)} %own_ref.31, bf16[1024,512]{1,0:T(8,128)(2,1)} %get-tuple-element.25.g_ref.refs_4_, bf16[1024,512]{1,0:T(8,128)(2,1)} %get-tuple-element.26.x_ref, bf16[9216,512]{1,0:T(8,128)(2,1)} %w_ref.31, f32[1536,384]{1,0:T(8,128)} %copy-done, ...), custom_call_target="tpu_custom_call" | custom-call | flops 1 | bytes 1 | tf_op jit(solution)/shard_map/piece/pallas_call | solution.py:205
  315.9 6.6 %final_first.1 = (f32[1152,512]{1,0:T(8,128)}, f32[1152,512]{1,0:T(8,128)}) custom-call(s32[2]{0:T(128)} %pad_add_fusion.4.idx_ref, bf16[512,9216]{1,0:T(8,128)(2,1)} %own_ref.31, bf16[1024,512]{1,0:T(8,128)(2,1)} %get-tuple-element.25.g_ref.refs_4_, bf16[1024,512]{1,0:T(8,128)(2,1)} %get-tuple-element.26.x_ref, bf16[9216,512]{1,0:T(8,128)(2,1)} %w_ref.31, ...), custom_call_target="tpu_custom_call" | custom-call | flops 1 | bytes 1 | tf_op jit(solution)/shard_map/final_first/pallas_call | solution.py:252
  322.5 11.0 %collective-permute-done.26.refs_1_ = f32[2,384,512]{2,1,0:T(8,128)} collective-permute-done((f32[2,384,512]{2,1,0:T(8,128)}, f32[2,384,512]{2,1,0:T(8,128)}, u32[]{:S(2)}, u32[]{:S(2)}) %collective-permute-start.26) | collective-permute-done | bytes 1572896 | tf_op jit(solution)/shard_map/ppermute | solution.py:402
  343.1 20.3 %collective-permute-done.25.refs_1_ = f32[2,384,512]{2,1,0:T(8,128)} collective-permute-done((f32[2,384,512]{2,1,0:T(8,128)}, f32[2,384,512]{2,1,0:T(8,128)}, u32[]{:S(2)}, u32[]{:S(2)}) %collective-permute-start.25) | collective-permute-done | bytes 1572896 | tf_op jit(solution)/shard_map/ppermute | solution.py:402
  363.4 5.9 %piece.29.a_ref = f32[2,384,512]{2,1,0:T(8,128)} custom-call(s32[3]{0:T(128)} %stack.161.idx_ref, bf16[512,9216]{1,0:T(8,128)(2,1)} %own_ref.31, bf16[1024,512]{1,0:T(8,128)(2,1)} %get-tuple-element.25.g_ref.refs_4_, bf16[1024,512]{1,0:T(8,128)(2,1)} %get-tuple-element.26.x_ref, bf16[9216,512]{1,0:T(8,128)(2,1)} %w_ref.31, ...), custom_call_target="tpu_custom_call" | custom-call | flops 1 | bytes 1 | tf_op jit(solution)/shard_map/piece/pallas_call | solution.py:205
  (96 shorter events, 107.4 us)
Async XLA Ops:
  7.2 221.9 %reduce-scatter.2.cloned.1.call-start = ((), (), s32[]{:S(2)}) async-start(), calls=%async_computation.1 | async-start | bytes 1310720 | tf_op jit(solution)/shard_map/reduce_scatter | solution.py:410
  13.6 56.2 %collective-permute-start.8 = (f32[1024,384]{1,0:T(8,128)}, f32[1024,384]{1,0:T(8,128)S(1)}, u32[]{:S(2)}, u32[]{:S(2)}) collective-permute-start(f32[1024,384]{1,0:T(8,128)} %get-tuple-element.27), channel_id=1, source_target_pairs={{0,4},{4,0},{24,28},{28,24},{1,5},{5,1},{25,29},{29,25},{2,6},{6,2... | collective-permute-start | bytes 4718600 | tf_op jit(solution)/shard_map/ppermute | solution.py:309
  14.3 55.4 %collective-permute-start.9 = (f32[1024,384]{1,0:T(8,128)}, f32[1024,384]{1,0:T(8,128)S(1)}, u32[]{:S(2)}, u32[]{:S(2)}) collective-permute-start(f32[1024,384]{1,0:T(8,128)} %get-tuple-element.28), channel_id=1, source_target_pairs={{0,8},{4,12},{24,16},{28,20},{1,9},{5,13},{25,17},{29,21},{2,10},{... | collective-permute-start | bytes 4718600 | tf_op jit(solution)/shard_map/ppermute | solution.py:351
  27.5 36.7 %collective-permute-start = (f32[256,512]{1,0:T(8,128)}, f32[256,512]{1,0:T(8,128)}, u32[]{:S(2)}, u32[]{:S(2)}) collective-permute-start(f32[256,512]{1,0:T(8,128)} %get-tuple-element.24), channel_id=1, source_target_pairs={{0,8},{4,12},{24,16},{28,20},{1,9},{5,13},{25,17},{29,21},{2,10},{... | collective-permute-start | bytes 1572872 | tf_op jit(solution)/shard_map/ppermute | solution.py:350
  28.8 37.6 %collective-permute-start.5 = (f32[256,512]{1,0:T(8,128)}, f32[256,512]{1,0:T(8,128)}, u32[]{:S(2)}, u32[]{:S(2)}) collective-permute-start(f32[256,512]{1,0:T(8,128)} %collective-permute-done.4.refs_0_), channel_id=1, source_target_pairs={{0,1},{1,0},{2,3},{3,2},{4,5},{5,4},{6,7},{7,6},{8,9},{9,8},{10,11... | collective-permute-start | bytes 1572872 | tf_op jit(solution)/shard_map/ppermute | solution.py:312
  78.0 54.4 %collective-permute-start.10 = (f32[1536,384]{1,0:T(8,128)}, f32[1536,384]{1,0:T(8,128)S(1)}, u32[]{:S(2)}, u32[]{:S(2)}) collective-permute-start(f32[1536,384]{1,0:T(8,128)} %get-tuple-element.32), channel_id=1, source_target_pairs={{0,4},{4,0},{8,12},{12,8},{16,20},{20,16},{24,28},{28,24},{1,5},{5... | collective-permute-start | bytes 7077896 | tf_op jit(solution)/shard_map/ppermute | solution.py:309
  80.6 39.5 %collective-permute-start.11 = (f32[2,384,512]{2,1,0:T(8,128)}, f32[2,384,512]{2,1,0:T(8,128)}, u32[]{:S(2)}, u32[]{:S(2)}) collective-permute-start(f32[2,384,512]{2,1,0:T(8,128)} %get-tuple-element.29.refs_1_), channel_id=1, source_target_pairs={{0,8},{4,12},{24,16},{28,20},{1,9},{5,13},{25,17},{29,21},{2,10},{... | collective-permute-start | bytes 4718600 | tf_op jit(solution)/shard_map/ppermute | solution.py:396
  98.2 68.0 %collective-permute-start.15 = (f32[2,384,512]{2,1,0:T(8,128)}, f32[2,384,512]{2,1,0:T(8,128)}, u32[]{:S(2)}, u32[]{:S(2)}) collective-permute-start(f32[2,384,512]{2,1,0:T(8,128)} %piece.17.refs_0_), channel_id=1, source_target_pairs={{8,12},{12,8},{16,20},{20,16},{9,13},{13,9},{17,21},{21,17},{10,14... | collective-permute-start | bytes 4718600 | tf_op jit(solution)/shard_map/ppermute | solution.py:309
  100.6 65.6 %collective-permute-start.14 = (f32[2,384,512]{2,1,0:T(8,128)}, f32[2,384,512]{2,1,0:T(8,128)}, u32[]{:S(2)}, u32[]{:S(2)}) collective-permute-start(f32[2,384,512]{2,1,0:T(8,128)} %piece.16.refs_4_.refs_1_), channel_id=1, source_target_pairs={{0,8},{4,12},{24,16},{28,20},{1,9},{5,13},{25,17},{29,21},{2,10},{... | collective-permute-start | bytes 4718600 | tf_op jit(solution)/shard_map/ppermute | solution.py:396
  140.8 46.6 %collective-permute-start.13 = (f32[2,384,512]{2,1,0:T(8,128)}, f32[2,384,512]{2,1,0:T(8,128)}, u32[]{:S(2)}, u32[]{:S(2)}) collective-permute-start(f32[2,384,512]{2,1,0:T(8,128)} %get-tuple-element.34.refs_2_), channel_id=1, source_target_pairs={{0,8},{4,12},{24,16},{28,20},{1,9},{5,13},{25,17},{29,21},{2,10},{... | collective-permute-start | bytes 4718600 | tf_op jit(solution)/shard_map/ppermute | solution.py:396
  142.1 45.4 %collective-permute-start.16 = (f32[2,384,512]{2,1,0:T(8,128)}, f32[2,384,512]{2,1,0:T(8,128)}, u32[]{:S(2)}, u32[]{:S(2)}) collective-permute-start(f32[2,384,512]{2,1,0:T(8,128)} %get-tuple-element.34.refs_2_), channel_id=1, source_target_pairs={{8,16},{12,20},{16,8},{20,12},{9,17},{13,21},{17,9},{21,13},{10,18... | collective-permute-start | bytes 4718600 | tf_op jit(solution)/shard_map/ppermute | solution.py:402
  144.0 69.9 %collective-permute-start.12 = (f32[1536,384]{1,0:T(8,128)}, f32[1536,384]{1,0:T(8,128)S(1)}, u32[]{:S(2)}, u32[]{:S(2)}) collective-permute-start(f32[1536,384]{1,0:T(8,128)} %get-tuple-element.33), channel_id=1, source_target_pairs={{0,4},{4,0},{8,12},{12,8},{16,20},{20,16},{24,28},{28,24},{1,5},{5... | collective-permute-start | bytes 7077896 | tf_op jit(solution)/shard_map/ppermute | solution.py:309
  172.1 64.5 %collective-permute-start.19 = (f32[2,384,512]{2,1,0:T(8,128)}, f32[2,384,512]{2,1,0:T(8,128)}, u32[]{:S(2)}, u32[]{:S(2)}) collective-permute-start(f32[2,384,512]{2,1,0:T(8,128)} %piece.19.refs_5_), channel_id=1, source_target_pairs={{8,16},{12,20},{16,8},{20,12},{9,17},{13,21},{17,9},{21,13},{10,18... | collective-permute-start | bytes 4718600 | tf_op jit(solution)/shard_map/ppermute | solution.py:402
  174.0 62.6 %collective-permute-start.20 = (f32[2,384,512]{2,1,0:T(8,128)}, f32[2,384,512]{2,1,0:T(8,128)}, u32[]{:S(2)}, u32[]{:S(2)}) collective-permute-start(f32[2,384,512]{2,1,0:T(8,128)} %piece.19.refs_5_), channel_id=1, source_target_pairs={{0,8},{4,12},{24,16},{28,20},{1,9},{5,13},{25,17},{29,21},{2,10},{... | collective-permute-start | bytes 4718600 | tf_op jit(solution)/shard_map/ppermute | solution.py:396
  222.4 50.9 %collective-permute-start.17 = (f32[1536,384]{1,0:T(8,128)}, f32[1536,384]{1,0:T(8,128)S(1)}, u32[]{:S(2)}, u32[]{:S(2)}) collective-permute-start(f32[1536,384]{1,0:T(8,128)} %get-tuple-element.35), channel_id=1, source_target_pairs={{0,4},{4,0},{8,12},{12,8},{16,20},{20,16},{24,28},{28,24},{1,5},{5... | collective-permute-start | bytes 7077896 | tf_op jit(solution)/shard_map/ppermute | solution.py:309
  225.2 39.5 %collective-permute-start.18 = (f32[2,384,512]{2,1,0:T(8,128)}, f32[2,384,512]{2,1,0:T(8,128)}, u32[]{:S(2)}, u32[]{:S(2)}) collective-permute-start(f32[2,384,512]{2,1,0:T(8,128)} %get-tuple-element.36.refs_2_), channel_id=1, source_target_pairs={{0,8},{4,12},{24,16},{28,20},{1,9},{5,13},{25,17},{29,21},{2,10},{... | collective-permute-start | bytes 4718600 | tf_op jit(solution)/shard_map/ppermute | solution.py:396
  226.5 39.5 %collective-permute-start.21 = (f32[2,384,512]{2,1,0:T(8,128)}, f32[2,384,512]{2,1,0:T(8,128)}, u32[]{:S(2)}, u32[]{:S(2)}) collective-permute-start(f32[2,384,512]{2,1,0:T(8,128)} %get-tuple-element.36.refs_2_), channel_id=1, source_target_pairs={{8,16},{12,20},{16,8},{20,12},{9,17},{13,21},{17,9},{21,13},{10,18... | collective-permute-start | bytes 4718600 | tf_op jit(solution)/shard_map/ppermute | solution.py:402
  248.7 51.0 %collective-permute-start.24 = (f32[2,384,512]{2,1,0:T(8,128)}, f32[2,384,512]{2,1,0:T(8,128)}, u32[]{:S(2)}, u32[]{:S(2)}) collective-permute-start(f32[2,384,512]{2,1,0:T(8,128)} %piece.23.refs_3_), channel_id=1, source_target_pairs={{8,16},{12,20},{16,8},{20,12},{9,17},{13,21},{17,9},{21,13},{10,18... | collective-permute-start | bytes 4718600 | tf_op jit(solution)/shard_map/ppermute | solution.py:402
  252.7 47.1 %collective-permute-start.23 = (f32[2,384,512]{2,1,0:T(8,128)}, f32[2,384,512]{2,1,0:T(8,128)}, u32[]{:S(2)}, u32[]{:S(2)}) collective-permute-start(f32[2,384,512]{2,1,0:T(8,128)} %piece.22.refs_2_), channel_id=1, source_target_pairs={{0,8},{4,12},{24,16},{28,20},{8,0},{12,4},{16,24},{20,28},{1,9},{5... | collective-permute-start | bytes 4718600 | tf_op jit(solution)/shard_map/ppermute | solution.py:391
  288.2 34.2 %collective-permute-start.22 = (f32[1024,384]{1,0:T(8,128)}, f32[1024,384]{1,0:T(8,128)}, u32[]{:S(2)}, u32[]{:S(2)}) collective-permute-start(f32[1024,384]{1,0:T(8,128)} %get-tuple-element.37), channel_id=1, source_target_pairs={{0,4},{4,0},{8,12},{12,8},{16,20},{20,16},{24,28},{28,24},{1,5},{5... | collective-permute-start | bytes 4718600 | tf_op jit(solution)/shard_map/ppermute | solution.py:309
  289.8 43.6 %collective-permute-start.26 = (f32[2,384,512]{2,1,0:T(8,128)}, f32[2,384,512]{2,1,0:T(8,128)}, u32[]{:S(2)}, u32[]{:S(2)}) collective-permute-start(f32[2,384,512]{2,1,0:T(8,128)} %get-tuple-element.38.refs_3_), channel_id=1, source_target_pairs={{8,16},{12,20},{16,8},{20,12},{9,17},{13,21},{17,9},{21,13},{10,18... | collective-permute-start | bytes 4718600 | tf_op jit(solution)/shard_map/ppermute | solution.py:402
  291.8 47.6 %collective-permute-start.27 = (f32[2,384,512]{2,1,0:T(8,128)S(1)}, f32[2,384,512]{2,1,0:T(8,128)}, u32[]{:S(2)}, u32[]{:S(2)}) collective-permute-start(f32[2,384,512]{2,1,0:T(8,128)S(1)} %copy-done.4), channel_id=1, source_target_pairs={{0,8},{4,12},{24,16},{28,20},{8,0},{12,4},{16,24},{20,28},{1,9},{5... | collective-permute-start | bytes 4718600 | tf_op jit(solution)/shard_map/ppermute | solution.py:391
  312.0 51.4 %collective-permute-start.25 = (f32[2,384,512]{2,1,0:T(8,128)}, f32[2,384,512]{2,1,0:T(8,128)}, u32[]{:S(2)}, u32[]{:S(2)}) collective-permute-start(f32[2,384,512]{2,1,0:T(8,128)} %piece.27.refs_1_), channel_id=1, source_target_pairs={{8,16},{12,20},{16,8},{20,12},{9,17},{13,21},{17,9},{21,13},{10,18... | collective-permute-start | bytes 4718600 | tf_op jit(solution)/shard_map/ppermute | solution.py:402
  314.1 55.2 %collective-permute-start.28 = (f32[2,384,512]{2,1,0:T(8,128)S(1)}, f32[2,384,512]{2,1,0:T(8,128)}, u32[]{:S(2)}, u32[]{:S(2)}) collective-permute-start(f32[2,384,512]{2,1,0:T(8,128)S(1)} %copy-done.6), channel_id=1, source_target_pairs={{0,8},{4,12},{24,16},{28,20},{8,0},{12,4},{16,24},{20,28},{1,9},{5... | collective-permute-start | bytes 4718600 | tf_op jit(solution)/shard_map/ppermute | solution.py:391
  (15 other events, 113.5 us)
Sparse Core Ops, SparseCore 0:
  119.4 27.1 reduce-scatter.1

commit v3 on v2

--- a/solution.py
+++ b/solution.py
@@ -56,48 +56,74 @@
     return [pl.BlockSpec(memory_space=pl.ANY)] * len(arrays)
 
 
+def cast_kernel(idx_ref, pre_ref, *refs):
+    refs[-1][...] = pre_ref[...].astype(jnp.float32)
+
+
+def cast_block(index, pre_act, size, after):
+    rows = pre_act.shape[0]
+    return pl.pallas_call(
+        cast_kernel,
+        grid_spec=pltpu.PrefetchScalarGridSpec(
+            num_scalar_prefetch=1,
+            grid=(1,),
+            in_specs=[pl.BlockSpec((rows, size), lambda i, idx: (0, idx[0]))] + anywhere(after),
+            out_specs=pl.BlockSpec((rows, size), lambda i, idx: (0, 0)),
+        ),
+        out_shape=jax.ShapeDtypeStruct((rows, size), jnp.float32),
+        compiler_params=params(),
+        cost_estimate=piece_cost(),
+        name="cast_block",
+    )(index.reshape(1), pre_act, *after)
+
+
 def start_kernel(idx_ref, grads_ref, inputs_ref, *refs):
-    columns, (quarter_ref, *outs) = refs[:4], refs[4:]
+    columns, (quarter_ref, *outs) = refs[:2], refs[-3:]
     quarter, rows = grads_ref.shape[0], columns[0].shape[0]
     quarter_ref[:quarter, :] = grads_ref[...].astype(jnp.float32)
     quarter_ref[quarter:, :] = inputs_ref[...].astype(jnp.float32)
-    for k, ref in enumerate(columns):
-        place = k % 2
-        outs[k // 2][place * rows : (place + 1) * rows, :] = ref[...].astype(jnp.float32)
-
-
-def start_sends(blk, out_grads, inputs, columns, pre_act, size):
+    for ref, out_ref in zip(columns, outs):
+        out_ref[...] = ref[...].astype(jnp.float32)
+
+
+def start_sends(blk, out_grads, inputs, columns, pre_act, size, after):
     rows, width = out_grads.shape
     quarter = rows // 4
     tokens = pl.BlockSpec((quarter, width), lambda i, idx: (idx[0], 0))
-    shapes = [(2 * quarter, width), (2 * rows, size), (2 * rows, size)]
+    shapes = [(2 * quarter, width)] + [(rows, size)] * 2
     return pl.pallas_call(
         start_kernel,
         grid_spec=pltpu.PrefetchScalarGridSpec(
             num_scalar_prefetch=1,
             grid=(1,),
             in_specs=[tokens, tokens]
-            + [pl.BlockSpec((rows, size), lambda i, idx, k=k: (0, idx[k])) for k in (1, 2, 3, 4)],
+            + [pl.BlockSpec((rows, size), lambda i, idx, k=k: (0, idx[k])) for k in (1, 2)]
+            + anywhere(after),
             out_specs=[pl.BlockSpec(shape, lambda i, idx: (0, 0)) for shape in shapes],
         ),
         out_shape=[jax.ShapeDtypeStruct(shape, jnp.float32) for shape in shapes],
         compiler_params=params(),
         cost_estimate=piece_cost(),
         name="start_sends",
-    )(jnp.stack([blk, *columns]), out_grads, inputs, *([pre_act] * 4))
-
-
-def join_kernel(blk_ref, grads_ref, inputs_ref, *refs):
-    quarters, (g_ref, x_ref) = refs[:4], refs[-2:]
+    )(jnp.stack([blk, *columns]), out_grads, inputs, *([pre_act] * 2), *after)
+
+
+def join_kernel(n_quarters, blk_ref, grads_ref, inputs_ref, *refs):
+    quarters, (g_ref, x_ref) = refs[:n_quarters], refs[-2:]
     rows = grads_ref.shape[0]
     quarter = rows // 4
     g_ref[:rows, :] = grads_ref[...]
     x_ref[:rows, :] = inputs_ref[...]
-    for flip, ref in enumerate(quarters):
-        where = jnp.bitwise_xor(blk_ref[0], flip)
-        place = pl.ds(pl.multiple_of(rows + where * quarter, quarter), quarter)
-        g_ref[place, :] = ref[:quarter, :].astype(jnp.bfloat16)
-        x_ref[place, :] = ref[quarter:, :].astype(jnp.bfloat16)
+    for k in range(4):
+        if n_quarters == 1:
+            place = pl.ds(rows + k * quarter, quarter)
+            ref, start = quarters[0], 2 * k * quarter
+        else:
+            where = jnp.bitwise_xor(blk_ref[0], k)
+            place = pl.ds(pl.multiple_of(rows + where * quarter, quarter), quarter)
+            ref, start = quarters[k], 0
+        g_ref[place, :] = ref[start : start + quarter, :].astype(jnp.bfloat16)
+        x_ref[place, :] = ref[start + quarter : start + 2 * quarter, :].astype(jnp.bfloat16)
 
 
 def join(blk, out_grads, inputs, quarters, after):
@@ -105,11 +131,12 @@
     shape = jax.ShapeDtypeStruct((2 * rows, width), jnp.bfloat16)
     vmem = pl.BlockSpec(memory_space=pltpu.VMEM)
     return pl.pallas_call(
-        join_kernel,
+        functools.partial(join_kernel, len(quarters)),
         out_shape=(shape, shape),
-        in_specs=[pl.BlockSpec(memory_space=pltpu.SMEM)] + [vmem] * 6 + anywhere(after),
+        in_specs=[pl.BlockSpec(memory_space=pltpu.SMEM)] + [vmem] * (2 + len(quarters)) + anywhere(after),
         out_specs=(vmem, vmem),
         compiler_params=params(),
+        cost_estimate=piece_cost(),
         name="join_tokens",
     )(blk.reshape(1), out_grads, inputs, *quarters, *after)
 
@@ -314,7 +341,7 @@
     outer_to_inner = links([(0, 1), (3, 2)])
     inner_to_inner = links([(1, 2), (2, 1)])
     inner_to_outer = links([(1, 0), (2, 3)])
-    every, outer_planes, inner_planes = (0, 1, 2, 3), (0, 3), (1, 2)
+    every, inner_planes = (0, 1, 2, 3), (1, 2)
 
     def block(q, which):
         place = q // count
@@ -336,82 +363,83 @@
     double = steps - count
     first = jnp.int32(near_inner[0])
 
-    quarter, send, raw = start_sends(
-        blk,
-        out_grads,
-        inputs,
-        [theirs(main[0]), theirs(main[1]), theirs(first), mine(first)],
-        pre_act,
-        size,
-    )
+    inner_main, outer_main = [max(s - 2, 0) for s in range(steps)], ahead
+    exchanges = [
+        [(near_outer[0], outer_main[0])],
+        [(near_outer[1], outer_main[1])],
+        [(inner_main[2], outer_main[2]), (inner_main[3], outer_main[3])],
+        [(inner_main[4], outer_main[4]), (inner_main[5], outer_main[5])],
+        [
+            (inner_main[6], outer_main[6]),
+            (inner_main[7], outer_main[7]),
+            (near_outer[2], near_outer[0]),
+        ],
+        [(near_inner[1], near_outer[1]), (near_inner[2], near_outer[2])],
+    ]
+
+    def columns_of(e):
+        return [theirs(by_role(*pair)) for pair in exchanges[e]]
+
+    raw = [cast_block(theirs(first), pre_act, size, [])]
+    quarter, send, last = start_sends(
+        blk, out_grads, inputs, columns_of(0) + [mine(first)], pre_act, size, raw
+    )
+    raw.append(last)
     pair_0 = swap(quarter, every)
-    received = swap(send, outer_planes)
-    y = {0: (received, 0), 1: (received, 1)}
+    got = [swap(send, every)]
     quarter_in = lax.ppermute(quarter, "dp", outer_to_inner)
-    raw_in = lax.ppermute(raw, "dp", outer_to_inner)
+    raw_in = [lax.ppermute(array, "dp", outer_to_inner) for array in raw]
+    last = cast_block(columns_of(1)[0], pre_act, size, [pair_0])
+    got.append(swap(last, every))
     pair_1, pair_2 = flip(pair_0, 1), flip(pair_0, 2)
+    pair_2, got[0], raw_in[0] = lax.optimization_barrier((pair_2, got[0], raw_in[0]))
     pair_3 = flip(pair_2, 1)
-    g, x = join(blk, out_grads, inputs, [pair_0, pair_1, pair_2, pair_3], [])
+    pair_3, quarter_in = lax.optimization_barrier((pair_3, quarter_in))
+    line_rows = lax.all_gather(quarter_in, "blk", tiled=True)
+    g, x = join(blk, out_grads, inputs, [pair_0, pair_1, pair_2, pair_3], [last, got[0], raw_in[0]])
     last = g
 
     def run(q, partner, **more):
         return piece(scale, mine(q), pre_act, [partner[0]], partner[1], g, x, w_out, **more)
 
-    no, own = {}, {}
     toward, across = [], {}
     for s in range(steps):
-        block_names, sends = [], []
-        if s % 2 == 0:
-            for store, key, q in (
-                (y, s + 2, main[s + 2] if s + 2 < steps else None),
-                (y, s + 3, main[s + 3] if s + 3 < steps else None),
-                (no, s // 2, jnp.int32(near_outer[s // 2]) if s // 2 < count else None),
-            ):
-                if q is not None:
-                    block_names.append((store, key))
-                    sends.append(theirs(q))
-            if s + 2 >= steps:
-                for i in range(1, count):
-                    block_names.append((own, i))
-                    sends.append(theirs(own_chunk[i]))
+        partner = (got[s], 0) if s < 2 else (got[1 + s // 2], s % 2)
+        sends = columns_of(2 + s // 2) if s % 2 == 0 else []
         sums = [toward[s - 2]] if s >= 2 else []
-        held_back = ([across[s - 4]] if s >= 4 else []) + ([raw_in, quarter_in] if s == 0 else []) + ([first_in] if s == 3 else [])
+        held_back = ([across[s - 4]] if s >= 4 else []) + ([raw_in[1]] if s == 1 else []) + ([first_in] if s == 3 else [])
         j = s - double
         if j < 0:
             after = [last] + held_back
         else:
             (last,) = run(
                 by_role(near_outer[j], ahead[s]),
-                y[s],
+                partner,
                 sums=[across[j]],
-                other=no[j],
+                other=(got[j], 0) if j < 2 else (got[4], 2),
                 is_inner=inner,
                 after=[last] + sums + held_back,
             )
             toward.append(lax.ppermute(last, "dp", outer_to_inner + inner_to_outer))
             after = [last] + ([grad_inputs] if j == 0 else [])
-        out, *blocks = run(main[s], y[s], sums=sums, sends=[sends] if sends else [], after=after, flops=FLOPS if s == 3 else 1)
+        out, *blocks = run(main[s], partner, sums=sums, sends=[sends] if sends else [], after=after, flops=FLOPS if s == 3 else 1)
         last = out
         if j < 0:
             toward.append(lax.ppermute(out, "dp", outer_to_inner))
         if blocks:
-            received = swap(blocks[0], every)
-            for place, (store, key) in enumerate(block_names):
-                store[key] = (received, place)
+            got.append(swap(blocks[0], every))
         if s >= 2:
             across[s - 2] = lax.ppermute(out, "dp", inner_to_inner)
         if s == 1:
-            in_1, in_2 = flip(quarter_in, 1), flip(quarter_in, 2)
-            in_3 = flip(in_2, 1)
-            line_g, line_x = join(blk, out_grads, inputs, [quarter_in, in_1, in_2, in_3], [last])
-            (last,) = piece(scale, theirs(first), pre_act, [raw_in], 0, line_g, line_x, w_out, after=[last])
+            line_g, line_x = join(blk, out_grads, inputs, [line_rows], [last])
+            (last,) = piece(scale, theirs(first), pre_act, [raw_in[0]], 0, line_g, line_x, w_out, after=[last])
             first_in = swap(last, inner_planes)
             last = input_partial(out_grads, pre_act, w_in, w_out, 4 * size, [last])
             grad_inputs = lax.psum_scatter(last, "blk", scatter_dimension=0, tiled=True)
             grad_inputs = grad_inputs.astype(jnp.bfloat16)
         if s == 4:
             (held_in,) = piece(
-                scale, mine(first), pre_act, [raw_in], 1, line_g, line_x, w_out, sums=[first_in], after=[last]
+                scale, mine(first), pre_act, [raw_in[1]], 0, line_g, line_x, w_out, sums=[first_in], after=[last]
             )
             last = held_in
 
@@ -421,8 +449,8 @@
         mine(jnp.int32(near_outer[0])),
         inner,
         pre_act,
-        no[0][0],
-        no[0][1],
+        got[4],
+        2,
         g,
         x,
         w_out,
@@ -432,7 +460,7 @@
         [last],
     )
     for i in range(1, count):
-        (out,) = run(own_chunk[i], own[i], sums=[across[count + i]], after=[held[0]])
+        (out,) = run(own_chunk[i], (got[5], i - 1), sums=[across[count + i]], after=[held[0]])
         held = final_add(i, out, toward[double + i], held, [])
     return (grad_inputs, held[0], held[1])
 

time: 381 us -> 352 us (0.924)
  waiting for transfers between devices: 173 us -> 149 us
  local copies, waits for them, and re-layouts: 14.5 us -> 9.07 us
    ppermute x7 -> x8, waiting for transfers between devices: 77.1 us -> 42.8 us  [swap(): lax.ppermute(array, 'dp', [(2 * a + h, 2 * a + 1 - h) for a in planes for...]
    ppermute x5, waiting for transfers between devices: 20.6 us -> 52.9 us  [line_body(): toward.append(lax.ppermute(out, 'dp', outer_to_inner))]
    ppermute x3, waiting for transfers between devices: 0.01 us -> 30.3 us  [line_body(): toward.append(lax.ppermute(last, 'dp', outer_to_inner + inner_to_outer))]
    ppermute x6, waiting for transfers between devices: 40.5 us -> 13.5 us  [line_body(): across[s - 2] = lax.ppermute(out, 'dp', inner_to_inner)]
    ppermute x1, waiting for transfers between devices: 25.1 us -> 2.83 us  [line_body(): quarter_in = lax.ppermute(quarter, 'dp', outer_to_inner)]
    ppermute x6 -> x3, waiting for transfers between devices: 10.3 us -> 0.36 us  [flip(): return lax.ppermute(array, 'blk', [(i, i ^ bit) for i in range(4)])]
    ppermute x1 -> x2, waiting for transfers between devices: 0.01 us -> 6.85 us  [line_body(): raw_in = [lax.ppermute(array, 'dp', outer_to_inner) for array in raw]]
    pallas_call x2 -> x4, Pallas kernels: 6.69 us -> 11 us  [the longest x2 7.12 us: join(): pl.pallas_call(functools.partial(join_kernel, len(quarters)), out_shape=(...]
  transfers between devices with their start and end apart: 30 -> 30, of which waited for: 14 -> 16; matrix products, arithmetic and copies ran while one was open for 3% -> 3% of each run, Pallas kernels for 33% -> 36%
where the time goes in v3:
time: 352 us; the launch traced here: 351 us
  waiting for transfers between devices  149 us (42%)
  Pallas kernels  136 us (39%)
  starting transfers between devices  36 us (10%)
  between operations  14.6 us (4%)
  local copies, waits for them, and re-layouts  9.07 us (3%)
  other arithmetic  5.26 us (1%)
    pallas_call x15, Pallas kernels, piece(): pl.pallas_call(functools.partial(piece_kernel, scale, counts), grid_spec=...  91.5 us
    ppermute x5, waiting for transfers between devices, line_body(): toward.append(lax.ppermute(out, 'dp', outer_to_inner))  52.9 us
    ppermute x8, waiting for transfers between devices, swap(): lax.ppermute(array, 'dp', [(2 * a + h, 2 * a + 1 - h) for a in planes for...  42.8 us
    ppermute x3, waiting for transfers between devices, line_body(): toward.append(lax.ppermute(last, 'dp', outer_to_inner + inner_to_outer))  30.3 us
    pallas_call x1, Pallas kernels, input_partial(): pl.pallas_call(input_kernel, grid=(hidden // size,), in_specs=[tokens, pl...  16.3 us
    ppermute x6, starting transfers between devices, line_body(): across[s - 2] = lax.ppermute(out, 'dp', inner_to_inner)  14.5 us
    ppermute x6, waiting for transfers between devices, line_body(): across[s - 2] = lax.ppermute(out, 'dp', inner_to_inner)  13.5 us
    ppermute x8, starting transfers between devices, swap(): lax.ppermute(array, 'dp', [(2 * a + h, 2 * a + 1 - h) for a in planes for...  9.36 us
  transfers between devices with their start and end apart: 30, of which 16 were waited for; matrix products, arithmetic and copies ran while one was open for 3% of the time, Pallas kernels for 36%

profile of v3, /device:TPU:16, one launch (start us, length us, event | category | flops | bytes accessed | tf_op | source)
XLA Modules:
  0.0 350.8 jit_solution(9371071591884164437)
XLA Ops:
  16.6 11.6 %collective-permute-done.refs_0_ = f32[256,512]{1,0:T(8,128)S(1)} collective-permute-done((f32[256,512]{1,0:T(8,128)}, f32[256,512]{1,0:T(8,128)S(1)}, u32[]{:S(2)}, u32[]{:S(2)}) %collective-permute-start) | collective-permute-done | bytes 524320 | tf_op jit(solution)/shard_map/ppermute | solution.py:336
  31.0 6.1 %collective-permute-done.3.refs_6_.refs_0_ = f32[512,384]{1,0:T(8,128)S(1)} collective-permute-done((f32[512,384]{1,0:T(8,128)S(1)}, f32[512,384]{1,0:T(8,128)S(1)}, u32[]{:S(2)}, u32[]{:S(2)}) %collective-permute-start.3) | collective-permute-done | bytes 786464 | tf_op jit(solution)/shard_map/ppermute | solution.py:391
  37.1 6.9 %collective-permute-done.2.refs_5_.refs_0_.refs_1_ = f32[512,384]{1,0:T(8,128)S(1)} collective-permute-done((f32[512,384]{1,0:T(8,128)}, f32[512,384]{1,0:T(8,128)S(1)}, u32[]{:S(2)}, u32[]{:S(2)}) %collective-permute-start.2) | collective-permute-done | bytes 786464 | tf_op jit(solution)/shard_map/ppermute | solution.py:336
  58.1 6.2 %piece.15 = (f32[2,384,512]{2,1,0:T(8,128)}, f32[1024,384]{1,0:T(8,128)}) custom-call(s32[5]{0:T(128)} %get-tuple-element.57.idx_ref, bf16[512,9216]{1,0:T(8,128)(2,1)} %own_ref.31, bf16[1024,512]{1,0:T(8,128)(2,1)} %get-tuple-element.36.g_ref.refs_3_, bf16[1024,512]{1,0:T(8,128)(2,1)} %get-tuple-element.37.x_ref, bf16[9216,512]{1,0:T(8,128)(2,1)} %w_ref.31, ...), custom_call_target="tpu_custom_call" | custom-call | flops 1 | bytes 1 | tf_op jit(solution)/shard_map/piece/pallas_call | solution.py:232
  91.2 16.3 %input_partial.1.refs_4_ = f32[512,512]{1,0:T(8,128)} custom-call(bf16[512,512]{1,0:T(8,128)(2,1)} %grads_ref.7, bf16[512,9216]{1,0:T(8,128)(2,1)} %own_ref.31, bf16[9216,512]{1,0:T(8,128)(2,1)} %w_ref.31, bf16[9216,512]{1,0:T(8,128)(2,1)} %in_rows_ref.1, f32[2,384,512]{2,1,0:T(8,128)} %piece.17.refs_0_), custom_call_target="tpu_custom_call" | custom-call | flops 1 | bytes 1 | tf_op jit(solution)/shard_map/input_partial/pallas_call | solution.py:160
  107.5 6.6 %piece.18 = (f32[2,384,512]{2,1,0:T(8,128)}, f32[1024,384]{1,0:T(8,128)}) custom-call(s32[5]{0:T(128)} %get-tuple-element.55.idx_ref, bf16[512,9216]{1,0:T(8,128)(2,1)} %own_ref.31, bf16[1024,512]{1,0:T(8,128)(2,1)} %get-tuple-element.36.g_ref.refs_3_, bf16[1024,512]{1,0:T(8,128)(2,1)} %get-tuple-element.37.x_ref, bf16[9216,512]{1,0:T(8,128)(2,1)} %w_ref.31, ...), custom_call_target="tpu_custom_call" | custom-call | flops 1 | bytes 1 | tf_op jit(solution)/shard_map/piece/pallas_call | solution.py:232
  119.0 20.1 %collective-permute-done.13.refs_1_ = f32[2,384,512]{2,1,0:T(8,128)} collective-permute-done((f32[2,384,512]{2,1,0:T(8,128)}, f32[2,384,512]{2,1,0:T(8,128)}, u32[]{:S(2)}, u32[]{:S(2)}) %collective-permute-start.13) | collective-permute-done | bytes 1572896 | tf_op jit(solution)/shard_map/ppermute | solution.py:428
  139.0 5.9 %piece.19.refs_5_ = f32[2,384,512]{2,1,0:T(8,128)} custom-call(s32[3]{0:T(128)} %stack.164.idx_ref, bf16[512,9216]{1,0:T(8,128)(2,1)} %own_ref.31, bf16[1024,512]{1,0:T(8,128)(2,1)} %get-tuple-element.36.g_ref.refs_3_, bf16[1024,512]{1,0:T(8,128)(2,1)} %get-tuple-element.37.x_ref, bf16[9216,512]{1,0:T(8,128)(2,1)} %w_ref.31, ...), custom_call_target="tpu_custom_call" | custom-call | flops 99999997952 | bytes 1 | tf_op jit(solution)/shard_map/piece/pallas_call | solution.py:232
  149.6 20.9 %collective-permute-done.11.refs_0_ = f32[1024,384]{1,0:T(8,128)S(1)} collective-permute-done((f32[1024,384]{1,0:T(8,128)}, f32[1024,384]{1,0:T(8,128)S(1)}, u32[]{:S(2)}, u32[]{:S(2)}) %collective-permute-start.11) | collective-permute-done | bytes 1572896 | tf_op jit(solution)/shard_map/ppermute | solution.py:336
  172.8 7.0 %piece.20 = (f32[2,384,512]{2,1,0:T(8,128)}, f32[1536,384]{1,0:T(8,128)}) custom-call(s32[6]{0:T(128)} %stack.158.idx_ref, bf16[512,9216]{1,0:T(8,128)(2,1)} %own_ref.31, bf16[1024,512]{1,0:T(8,128)(2,1)} %get-tuple-element.36.g_ref.refs_3_, bf16[1024,512]{1,0:T(8,128)(2,1)} %get-tuple-element.37.x_ref, bf16[9216,512]{1,0:T(8,128)(2,1)} %w_ref.31, ...), custom_call_target="tpu_custom_call" | custom-call | flops 1 | bytes 1 | tf_op jit(solution)/shard_map/piece/pallas_call | solution.py:232
  185.9 5.9 %piece.21.refs_3_.inner_ref = f32[2,384,512]{2,1,0:T(8,128)} custom-call(s32[3]{0:T(128)} %stack.172.idx_ref, bf16[512,9216]{1,0:T(8,128)(2,1)} %own_ref.31, bf16[1024,512]{1,0:T(8,128)(2,1)} %get-tuple-element.40.g_ref, bf16[1024,512]{1,0:T(8,128)(2,1)} %get-tuple-element.41.x_ref, bf16[9216,512]{1,0:T(8,128)(2,1)} %w_ref.31, f32[512,384]{1,0:T(8,128)} %copy-done.6, ...), custom_call_target="tpu_custom_call" | custom-call | flops 1 | bytes 1 | tf_op jit(solution)/shard_map/piece/pallas_call | solution.py:232
  193.4 13.0 %collective-permute-done.19.refs_4_.refs_1_ = f32[2,384,512]{2,1,0:T(8,128)} collective-permute-done((f32[2,384,512]{2,1,0:T(8,128)}, f32[2,384,512]{2,1,0:T(8,128)}, u32[]{:S(2)}, u32[]{:S(2)}) %collective-permute-start.19) | collective-permute-done | bytes 1572896 | tf_op jit(solution)/shard_map/ppermute | solution.py:428
  206.5 6.1 %piece.22.refs_2_ = f32[2,384,512]{2,1,0:T(8,128)} custom-call(s32[3]{0:T(128)} %fusion.1.idx_ref, bf16[512,9216]{1,0:T(8,128)(2,1)} %own_ref.31, bf16[1024,512]{1,0:T(8,128)(2,1)} %get-tuple-element.36.g_ref.refs_3_, bf16[1024,512]{1,0:T(8,128)(2,1)} %get-tuple-element.37.x_ref, bf16[9216,512]{1,0:T(8,128)(2,1)} %w_ref.31, f32[1024,384]{1,0:T(8,128)} %copy-done.1, ...), custom_call_target="tpu_custom_call" | custom-call | flops 1 | bytes 1 | tf_op jit(solution)/shard_map/piece/pallas_call | solution.py:232
  222.7 17.5 %collective-permute-done.17.refs_4_.refs_3_ = f32[2,384,512]{2,1,0:T(8,128)} collective-permute-done((f32[2,384,512]{2,1,0:T(8,128)}, f32[2,384,512]{2,1,0:T(8,128)}, u32[]{:S(2)}, u32[]{:S(2)}) %collective-permute-start.17) | collective-permute-done | bytes 1572896 | tf_op jit(solution)/shard_map/ppermute | solution.py:428
  241.6 6.1 %piece.24.refs_4_ = f32[2,384,512]{2,1,0:T(8,128)} custom-call(s32[3]{0:T(128)} %fusion.idx_ref, bf16[512,9216]{1,0:T(8,128)(2,1)} %own_ref.31, bf16[1024,512]{1,0:T(8,128)(2,1)} %get-tuple-element.36.g_ref.refs_3_, bf16[1024,512]{1,0:T(8,128)(2,1)} %get-tuple-element.37.x_ref, bf16[9216,512]{1,0:T(8,128)(2,1)} %w_ref.31, f32[1536,384]{1,0:T(8,128)} %copy-done, ...), custom_call_target="tpu_custom_call" | custom-call | flops 1 | bytes 1 | tf_op jit(solution)/shard_map/piece/pallas_call | solution.py:232
  247.7 6.7 %piece.25 = (f32[2,384,512]{2,1,0:T(8,128)}, f32[1024,384]{1,0:T(8,128)}) custom-call(s32[5]{0:T(128)} %get-tuple-element.56.idx_ref, bf16[512,9216]{1,0:T(8,128)(2,1)} %own_ref.31, bf16[1024,512]{1,0:T(8,128)(2,1)} %get-tuple-element.36.g_ref.refs_3_, bf16[1024,512]{1,0:T(8,128)(2,1)} %get-tuple-element.37.x_ref, bf16[9216,512]{1,0:T(8,128)(2,1)} %w_ref.31, ...), custom_call_target="tpu_custom_call" | custom-call | flops 1 | bytes 1 | tf_op jit(solution)/shard_map/piece/pallas_call | solution.py:232
  257.4 16.5 %collective-permute-done.22.refs_4_.refs_1_.outer_ref = f32[2,384,512]{2,1,0:T(8,128)} collective-permute-done((f32[2,384,512]{2,1,0:T(8,128)}, f32[2,384,512]{2,1,0:T(8,128)}, u32[]{:S(2)}, u32[]{:S(2)}) %collective-permute-start.22) | collective-permute-done | bytes 1572896 | tf_op jit(solution)/shard_map/ppermute | solution.py:423
  273.9 6.1 %piece.26.refs_2_ = f32[2,384,512]{2,1,0:T(8,128)} custom-call(s32[3]{0:T(128)} %fusion.2.idx_ref, bf16[512,9216]{1,0:T(8,128)(2,1)} %own_ref.31, bf16[1024,512]{1,0:T(8,128)(2,1)} %get-tuple-element.36.g_ref.refs_3_, bf16[1024,512]{1,0:T(8,128)(2,1)} %get-tuple-element.37.x_ref, bf16[9216,512]{1,0:T(8,128)(2,1)} %w_ref.31, f32[1536,384]{1,0:T(8,128)} %copy-done, ...), custom_call_target="tpu_custom_call" | custom-call | flops 1 | bytes 1 | tf_op jit(solution)/shard_map/piece/pallas_call | solution.py:232
  280.0 6.0 %piece.27.refs_1_ = f32[2,384,512]{2,1,0:T(8,128)} custom-call(s32[3]{0:T(128)} %stack.174.idx_ref, bf16[512,9216]{1,0:T(8,128)(2,1)} %own_ref.31, bf16[1024,512]{1,0:T(8,128)(2,1)} %get-tuple-element.36.g_ref.refs_3_, bf16[1024,512]{1,0:T(8,128)(2,1)} %get-tuple-element.37.x_ref, bf16[9216,512]{1,0:T(8,128)(2,1)} %w_ref.31, f32[1536,384]{1,0:T(8,128)} %copy-done, ...), custom_call_target="tpu_custom_call" | custom-call | flops 1 | bytes 1 | tf_op jit(solution)/shard_map/piece/pallas_call | solution.py:232
  290.6 6.6 %final_first.1 = (f32[1152,512]{1,0:T(8,128)}, f32[1152,512]{1,0:T(8,128)}) custom-call(s32[2]{0:T(128)} %pad_add_fusion.7.idx_ref, bf16[512,9216]{1,0:T(8,128)(2,1)} %own_ref.31, bf16[1024,512]{1,0:T(8,128)(2,1)} %get-tuple-element.36.g_ref.refs_3_, bf16[1024,512]{1,0:T(8,128)(2,1)} %get-tuple-element.37.x_ref, bf16[9216,512]{1,0:T(8,128)(2,1)} %w_ref.31, ...), custom_call_target="tpu_custom_call" | custom-call | flops 1 | bytes 1 | tf_op jit(solution)/shard_map/final_first/pallas_call | solution.py:279
  297.2 5.9 %piece.28.a_ref = f32[2,384,512]{2,1,0:T(8,128)} custom-call(s32[3]{0:T(128)} %stack.178.idx_ref, bf16[512,9216]{1,0:T(8,128)(2,1)} %own_ref.31, bf16[1024,512]{1,0:T(8,128)(2,1)} %get-tuple-element.36.g_ref.refs_3_, bf16[1024,512]{1,0:T(8,128)(2,1)} %get-tuple-element.37.x_ref, bf16[9216,512]{1,0:T(8,128)(2,1)} %w_ref.31, ...), custom_call_target="tpu_custom_call" | custom-call | flops 1 | bytes 1 | tf_op jit(solution)/shard_map/piece/pallas_call | solution.py:232
  311.3 13.5 %collective-permute-done.24.refs_1_ = f32[2,384,512]{2,1,0:T(8,128)} collective-permute-done((f32[2,384,512]{2,1,0:T(8,128)}, f32[2,384,512]{2,1,0:T(8,128)}, u32[]{:S(2)}, u32[]{:S(2)}) %collective-permute-start.24) | collective-permute-done | bytes 1572896 | tf_op jit(solution)/shard_map/ppermute | solution.py:432
  324.8 6.0 %piece.29.a_ref = f32[2,384,512]{2,1,0:T(8,128)} custom-call(s32[3]{0:T(128)} %stack.149.idx_ref, bf16[512,9216]{1,0:T(8,128)(2,1)} %own_ref.31, bf16[1024,512]{1,0:T(8,128)(2,1)} %get-tuple-element.36.g_ref.refs_3_, bf16[1024,512]{1,0:T(8,128)(2,1)} %get-tuple-element.37.x_ref, bf16[9216,512]{1,0:T(8,128)(2,1)} %w_ref.31, ...), custom_call_target="tpu_custom_call" | custom-call | flops 1 | bytes 1 | tf_op jit(solution)/shard_map/piece/pallas_call | solution.py:232
  330.8 9.4 %collective-permute-done.27.b_ref = f32[2,384,512]{2,1,0:T(8,128)} collective-permute-done((f32[2,384,512]{2,1,0:T(8,128)S(1)}, f32[2,384,512]{2,1,0:T(8,128)}, u32[]{:S(2)}, u32[]{:S(2)}) %collective-permute-start.27) | collective-permute-done | bytes 1572896 | tf_op jit(solution)/shard_map/ppermute | solution.py:423
  (111 shorter events, 103.1 us)
Async XLA Ops:
  7.2 71.8 %all-gather.2.cloned.1.call-start = ((), (), s32[]{:S(2)}) async-start(), calls=%async_computation.1 | async-start | bytes 2621440 | tf_op jit(solution)/shard_map/all_gather | solution.py:398
  14.7 22.3 %collective-permute-start.3 = (f32[512,384]{1,0:T(8,128)S(1)}, f32[512,384]{1,0:T(8,128)S(1)}, u32[]{:S(2)}, u32[]{:S(2)}) collective-permute-start(f32[512,384]{1,0:T(8,128)S(1)} %copy-done.7), channel_id=1, source_target_pairs={{0,8},{4,12},{24,16},{28,20},{1,9},{5,13},{25,17},{29,21},{2,10},{... | collective-permute-start | bytes 2359304 | tf_op jit(solution)/shard_map/ppermute | solution.py:391
  16.0 27.9 %collective-permute-start.2 = (f32[512,384]{1,0:T(8,128)}, f32[512,384]{1,0:T(8,128)S(1)}, u32[]{:S(2)}, u32[]{:S(2)}) collective-permute-start(f32[512,384]{1,0:T(8,128)} %get-tuple-element.30), channel_id=1, source_target_pairs={{0,4},{4,0},{8,12},{12,8},{16,20},{20,16},{24,28},{28,24},{1,5},{5... | collective-permute-start | bytes 2359304 | tf_op jit(solution)/shard_map/ppermute | solution.py:336
  47.7 144.1 %reduce-scatter.2.cloned.1.call-start = ((), (), s32[]{:S(2)}) async-start(), calls=%async_computation.2 | async-start | bytes 1310720 | tf_op jit(solution)/shard_map/reduce_scatter | solution.py:438
  51.0 20.3 %collective-permute-start.7 = (f32[512,384]{1,0:T(8,128)}, f32[512,384]{1,0:T(8,128)S(1)}, u32[]{:S(2)}, u32[]{:S(2)}) collective-permute-start(f32[512,384]{1,0:T(8,128)} %cast_block.3.refs_4_), channel_id=1, source_target_pairs={{0,4},{4,0},{8,12},{12,8},{16,20},{20,16},{24,28},{28,24},{1,5},{5... | collective-permute-start | bytes 2359304 | tf_op jit(solution)/shard_map/ppermute | solution.py:336
  64.3 43.2 %collective-permute-start.9 = (f32[1024,384]{1,0:T(8,128)}, f32[1024,384]{1,0:T(8,128)}, u32[]{:S(2)}, u32[]{:S(2)}) collective-permute-start(f32[1024,384]{1,0:T(8,128)} %get-tuple-element.42), channel_id=1, source_target_pairs={{0,4},{4,0},{8,12},{12,8},{16,20},{20,16},{24,28},{28,24},{1,5},{5... | collective-permute-start | bytes 4718600 | tf_op jit(solution)/shard_map/ppermute | solution.py:336
  65.9 41.7 %collective-permute-start.10 = (f32[2,384,512]{2,1,0:T(8,128)}, f32[2,384,512]{2,1,0:T(8,128)}, u32[]{:S(2)}, u32[]{:S(2)}) collective-permute-start(f32[2,384,512]{2,1,0:T(8,128)} %get-tuple-element.38.refs_1_), channel_id=1, source_target_pairs={{0,8},{4,12},{24,16},{28,20},{1,9},{5,13},{25,17},{29,21},{2,10},{... | collective-permute-start | bytes 4718600 | tf_op jit(solution)/shard_map/ppermute | solution.py:428
  77.6 61.4 %collective-permute-start.13 = (f32[2,384,512]{2,1,0:T(8,128)}, f32[2,384,512]{2,1,0:T(8,128)}, u32[]{:S(2)}, u32[]{:S(2)}) collective-permute-start(f32[2,384,512]{2,1,0:T(8,128)} %piece.16.refs_1_), channel_id=1, source_target_pairs={{0,8},{4,12},{24,16},{28,20},{1,9},{5,13},{25,17},{29,21},{2,10},{... | collective-permute-start | bytes 4718600 | tf_op jit(solution)/shard_map/ppermute | solution.py:428
  87.8 51.3 %collective-permute-start.14 = (f32[2,384,512]{2,1,0:T(8,128)}, f32[2,384,512]{2,1,0:T(8,128)}, u32[]{:S(2)}, u32[]{:S(2)}) collective-permute-start(f32[2,384,512]{2,1,0:T(8,128)} %piece.17.refs_0_), channel_id=1, source_target_pairs={{8,12},{12,8},{16,20},{20,16},{9,13},{13,9},{17,21},{21,17},{10,14... | collective-permute-start | bytes 4718600 | tf_op jit(solution)/shard_map/ppermute | solution.py:336
  114.1 56.3 %collective-permute-start.15 = (f32[2,384,512]{2,1,0:T(8,128)}, f32[2,384,512]{2,1,0:T(8,128)S(1)}, u32[]{:S(2)}, u32[]{:S(2)}) collective-permute-start(f32[2,384,512]{2,1,0:T(8,128)} %get-tuple-element.44.refs_2_), channel_id=1, source_target_pairs={{8,16},{12,20},{16,8},{20,12},{9,17},{13,21},{17,9},{21,13},{10,18... | collective-permute-start | bytes 4718600 | tf_op jit(solution)/shard_map/ppermute | solution.py:432
  116.5 56.2 %collective-permute-start.12 = (f32[2,384,512]{2,1,0:T(8,128)}, f32[2,384,512]{2,1,0:T(8,128)}, u32[]{:S(2)}, u32[]{:S(2)}) collective-permute-start(f32[2,384,512]{2,1,0:T(8,128)} %get-tuple-element.44.refs_2_), channel_id=1, source_target_pairs={{0,8},{4,12},{24,16},{28,20},{1,9},{5,13},{25,17},{29,21},{2,10},{... | collective-permute-start | bytes 4718600 | tf_op jit(solution)/shard_map/ppermute | solution.py:428
  117.8 52.6 %collective-permute-start.11 = (f32[1024,384]{1,0:T(8,128)}, f32[1024,384]{1,0:T(8,128)S(1)}, u32[]{:S(2)}, u32[]{:S(2)}) collective-permute-start(f32[1024,384]{1,0:T(8,128)} %get-tuple-element.43), channel_id=1, source_target_pairs={{0,4},{4,0},{8,12},{12,8},{16,20},{20,16},{24,28},{28,24},{1,5},{5... | collective-permute-start | bytes 4718600 | tf_op jit(solution)/shard_map/ppermute | solution.py:336
  145.0 61.5 %collective-permute-start.19 = (f32[2,384,512]{2,1,0:T(8,128)}, f32[2,384,512]{2,1,0:T(8,128)}, u32[]{:S(2)}, u32[]{:S(2)}) collective-permute-start(f32[2,384,512]{2,1,0:T(8,128)} %piece.19.refs_5_), channel_id=1, source_target_pairs={{0,8},{4,12},{24,16},{28,20},{1,9},{5,13},{25,17},{29,21},{2,10},{... | collective-permute-start | bytes 4718600 | tf_op jit(solution)/shard_map/ppermute | solution.py:428
  146.2 60.2 %collective-permute-start.18 = (f32[2,384,512]{2,1,0:T(8,128)}, f32[2,384,512]{2,1,0:T(8,128)}, u32[]{:S(2)}, u32[]{:S(2)}) collective-permute-start(f32[2,384,512]{2,1,0:T(8,128)} %piece.19.refs_5_), channel_id=1, source_target_pairs={{8,16},{12,20},{16,8},{20,12},{9,17},{13,21},{17,9},{21,13},{10,18... | collective-permute-start | bytes 4718600 | tf_op jit(solution)/shard_map/ppermute | solution.py:432
  179.7 60.4 %collective-permute-start.16 = (f32[1536,384]{1,0:T(8,128)}, f32[1536,384]{1,0:T(8,128)S(1)}, u32[]{:S(2)}, u32[]{:S(2)}) collective-permute-start(f32[1536,384]{1,0:T(8,128)} %get-tuple-element.45), channel_id=1, source_target_pairs={{0,4},{4,0},{8,12},{12,8},{16,20},{20,16},{24,28},{28,24},{1,5},{5... | collective-permute-start | bytes 7077896 | tf_op jit(solution)/shard_map/ppermute | solution.py:336
  181.7 41.0 %collective-permute-start.20 = (f32[2,384,512]{2,1,0:T(8,128)}, f32[2,384,512]{2,1,0:T(8,128)}, u32[]{:S(2)}, u32[]{:S(2)}) collective-permute-start(f32[2,384,512]{2,1,0:T(8,128)} %get-tuple-element.46.refs_2_), channel_id=1, source_target_pairs={{8,16},{12,20},{16,8},{20,12},{9,17},{13,21},{17,9},{21,13},{10,18... | collective-permute-start | bytes 4718600 | tf_op jit(solution)/shard_map/ppermute | solution.py:432
  184.1 56.1 %collective-permute-start.17 = (f32[2,384,512]{2,1,0:T(8,128)}, f32[2,384,512]{2,1,0:T(8,128)}, u32[]{:S(2)}, u32[]{:S(2)}) collective-permute-start(f32[2,384,512]{2,1,0:T(8,128)} %get-tuple-element.46.refs_2_), channel_id=1, source_target_pairs={{0,8},{4,12},{24,16},{28,20},{1,9},{5,13},{25,17},{29,21},{2,10},{... | collective-permute-start | bytes 4718600 | tf_op jit(solution)/shard_map/ppermute | solution.py:428
  218.5 38.9 %collective-permute-start.23 = (f32[2,384,512]{2,1,0:T(8,128)}, f32[2,384,512]{2,1,0:T(8,128)}, u32[]{:S(2)}, u32[]{:S(2)}) collective-permute-start(f32[2,384,512]{2,1,0:T(8,128)} %piece.23.refs_3_), channel_id=1, source_target_pairs={{8,16},{12,20},{16,8},{20,12},{9,17},{13,21},{17,9},{21,13},{10,18... | collective-permute-start | bytes 4718600 | tf_op jit(solution)/shard_map/ppermute | solution.py:432
  220.9 53.0 %collective-permute-start.22 = (f32[2,384,512]{2,1,0:T(8,128)}, f32[2,384,512]{2,1,0:T(8,128)}, u32[]{:S(2)}, u32[]{:S(2)}) collective-permute-start(f32[2,384,512]{2,1,0:T(8,128)} %piece.22.refs_2_), channel_id=1, source_target_pairs={{0,8},{4,12},{24,16},{28,20},{8,0},{12,4},{16,24},{20,28},{1,9},{5... | collective-permute-start | bytes 4718600 | tf_op jit(solution)/shard_map/ppermute | solution.py:423
  254.4 42.8 %collective-permute-start.21 = (f32[1024,384]{1,0:T(8,128)}, f32[1024,384]{1,0:T(8,128)}, u32[]{:S(2)}, u32[]{:S(2)}) collective-permute-start(f32[1024,384]{1,0:T(8,128)} %get-tuple-element.47), channel_id=1, source_target_pairs={{0,4},{4,0},{8,12},{12,8},{16,20},{20,16},{24,28},{28,24},{1,5},{5... | collective-permute-start | bytes 4718600 | tf_op jit(solution)/shard_map/ppermute | solution.py:336
  254.9 42.3 %collective-permute-start.25 = (f32[2,384,512]{2,1,0:T(8,128)}, f32[2,384,512]{2,1,0:T(8,128)}, u32[]{:S(2)}, u32[]{:S(2)}) collective-permute-start(f32[2,384,512]{2,1,0:T(8,128)} %get-tuple-element.48.refs_3_), channel_id=1, source_target_pairs={{8,16},{12,20},{16,8},{20,12},{9,17},{13,21},{17,9},{21,13},{10,18... | collective-permute-start | bytes 4718600 | tf_op jit(solution)/shard_map/ppermute | solution.py:432
  257.3 50.3 %collective-permute-start.26 = (f32[2,384,512]{2,1,0:T(8,128)S(1)}, f32[2,384,512]{2,1,0:T(8,128)}, u32[]{:S(2)}, u32[]{:S(2)}) collective-permute-start(f32[2,384,512]{2,1,0:T(8,128)S(1)} %copy-done.4), channel_id=1, source_target_pairs={{0,8},{4,12},{24,16},{28,20},{8,0},{12,4},{16,24},{20,28},{1,9},{5... | collective-permute-start | bytes 4718600 | tf_op jit(solution)/shard_map/ppermute | solution.py:423
  286.0 38.7 %collective-permute-start.24 = (f32[2,384,512]{2,1,0:T(8,128)}, f32[2,384,512]{2,1,0:T(8,128)}, u32[]{:S(2)}, u32[]{:S(2)}) collective-permute-start(f32[2,384,512]{2,1,0:T(8,128)} %piece.27.refs_1_), channel_id=1, source_target_pairs={{8,16},{12,20},{16,8},{20,12},{9,17},{13,21},{17,9},{21,13},{10,18... | collective-permute-start | bytes 4718600 | tf_op jit(solution)/shard_map/ppermute | solution.py:432
  288.6 51.5 %collective-permute-start.27 = (f32[2,384,512]{2,1,0:T(8,128)S(1)}, f32[2,384,512]{2,1,0:T(8,128)}, u32[]{:S(2)}, u32[]{:S(2)}) collective-permute-start(f32[2,384,512]{2,1,0:T(8,128)S(1)} %copy-done.5), channel_id=1, source_target_pairs={{0,8},{4,12},{24,16},{28,20},{8,0},{12,4},{16,24},{20,28},{1,9},{5... | collective-permute-start | bytes 4718600 | tf_op jit(solution)/shard_map/ppermute | solution.py:423
  (22 other events, 191.6 us)
Sparse Core Ops, SparseCore 0:
  47.8 22.0 all-gather.1
  107.6 26.5 reduce-scatter.1

commit v4 on v3

--- a/solution.py
+++ b/solution.py
@@ -9,7 +9,7 @@
 
 PIECES = 3
 FLOPS = 100_000_000_000
-VMEM_LIMIT = 56 * 1024 * 1024
+VMEM_LIMIT = 63 * 1024 * 1024
 
 
 def contract_rows(left, right):
@@ -56,56 +56,64 @@
     return [pl.BlockSpec(memory_space=pl.ANY)] * len(arrays)
 
 
-def cast_kernel(idx_ref, pre_ref, *refs):
-    refs[-1][...] = pre_ref[...].astype(jnp.float32)
-
-
-def cast_block(index, pre_act, size, after):
+def cast_kernel(shapes, idx_ref, *refs):
+    outs = refs[-len(shapes) :]
+    for (_, count), out_ref in zip(shapes, outs):
+        width = out_ref.shape[1] // count
+        for k in range(count):
+            out_ref[:, k * width : (k + 1) * width] = refs[k][...].astype(jnp.float32)
+        refs = refs[count:]
+
+
+def cast_blocks(table, groups, pre_act, after):
     rows = pre_act.shape[0]
-    return pl.pallas_call(
-        cast_kernel,
+    in_specs = [columns_spec(rows, width, at) for width, places in groups for at in places]
+    shapes = [(width * len(places), len(places)) for width, places in groups]
+    return pl.pallas_call(
+        functools.partial(cast_kernel, shapes),
         grid_spec=pltpu.PrefetchScalarGridSpec(
             num_scalar_prefetch=1,
             grid=(1,),
-            in_specs=[pl.BlockSpec((rows, size), lambda i, idx: (0, idx[0]))] + anywhere(after),
-            out_specs=pl.BlockSpec((rows, size), lambda i, idx: (0, 0)),
+            in_specs=in_specs + anywhere(after),
+            out_specs=[pl.BlockSpec((rows, width), lambda i, idx: (0, 0)) for width, _ in shapes],
         ),
-        out_shape=jax.ShapeDtypeStruct((rows, size), jnp.float32),
+        out_shape=[jax.ShapeDtypeStruct((rows, width), jnp.float32) for width, _ in shapes],
         compiler_params=params(),
         cost_estimate=piece_cost(),
-        name="cast_block",
-    )(index.reshape(1), pre_act, *after)
-
-
-def start_kernel(idx_ref, grads_ref, inputs_ref, *refs):
-    columns, (quarter_ref, *outs) = refs[:2], refs[-3:]
-    quarter, rows = grads_ref.shape[0], columns[0].shape[0]
+        name="cast_blocks",
+    )(table, *([pre_act] * len(in_specs)), *after)
+
+
+def first_kernel(idx_ref, grads_ref, inputs_ref, pre_ref, quarter_ref, raw_ref):
+    quarter = grads_ref.shape[0]
     quarter_ref[:quarter, :] = grads_ref[...].astype(jnp.float32)
     quarter_ref[quarter:, :] = inputs_ref[...].astype(jnp.float32)
-    for ref, out_ref in zip(columns, outs):
-        out_ref[...] = ref[...].astype(jnp.float32)
-
-
-def start_sends(blk, out_grads, inputs, columns, pre_act, size, after):
+    raw_ref[...] = pre_ref[...].astype(jnp.float32)
+
+
+def first_sends(indices, out_grads, inputs, pre_act, size):
     rows, width = out_grads.shape
     quarter = rows // 4
     tokens = pl.BlockSpec((quarter, width), lambda i, idx: (idx[0], 0))
-    shapes = [(2 * quarter, width)] + [(rows, size)] * 2
-    return pl.pallas_call(
-        start_kernel,
+    return pl.pallas_call(
+        first_kernel,
         grid_spec=pltpu.PrefetchScalarGridSpec(
             num_scalar_prefetch=1,
             grid=(1,),
-            in_specs=[tokens, tokens]
-            + [pl.BlockSpec((rows, size), lambda i, idx, k=k: (0, idx[k])) for k in (1, 2)]
-            + anywhere(after),
-            out_specs=[pl.BlockSpec(shape, lambda i, idx: (0, 0)) for shape in shapes],
+            in_specs=[tokens, tokens, columns_spec(rows, size, 1)],
+            out_specs=[
+                pl.BlockSpec((2 * quarter, width), lambda i, idx: (0, 0)),
+                pl.BlockSpec((rows, size), lambda i, idx: (0, 0)),
+            ],
         ),
-        out_shape=[jax.ShapeDtypeStruct(shape, jnp.float32) for shape in shapes],
+        out_shape=[
+            jax.ShapeDtypeStruct((2 * quarter, width), jnp.float32),
+            jax.ShapeDtypeStruct((rows, size), jnp.float32),
+        ],
         compiler_params=params(),
         cost_estimate=piece_cost(),
-        name="start_sends",
-    )(jnp.stack([blk, *columns]), out_grads, inputs, *([pre_act] * 2), *after)
+        name="first_sends",
+    )(indices, out_grads, inputs, pre_act)
 
 
 def join_kernel(n_quarters, blk_ref, grads_ref, inputs_ref, *refs):
@@ -164,7 +172,7 @@
         out_specs=tokens,
         out_shape=jax.ShapeDtypeStruct((rows, width), jnp.float32),
         compiler_params=params(),
-        cost_estimate=piece_cost(),
+        cost_estimate=piece_cost(FLOPS),
         name="input_partial",
     )(out_grads, pre_act, w_out, w_in, *after)
 
@@ -176,7 +184,7 @@
     return contract_rows(hidden, x) * scale, contract_rows(act, g) * scale
 
 
-def piece_kernel(scale, counts, idx_ref, own_ref, g_ref, x_ref, w_ref, *refs):
+def piece_kernel(scale, counts, inner_at, table_ref, own_ref, g_ref, x_ref, w_ref, *refs):
     groups = []
     for n in counts:
         groups.append(refs[:n])
@@ -184,7 +192,7 @@
     partners, others, columns, sums, _, (out_ref, *sends) = groups + [refs]
     partner = jnp.concatenate([ref[...] for ref in partners], axis=1)
     for ref in others:
-        partner = jnp.where(idx_ref[2] > 0, ref[...], partner)
+        partner = jnp.where(table_ref[inner_at] > 0, ref[...], partner)
     grad_in, grad_out = piece_math(scale, own_ref[...], partner, g_ref[...], x_ref[...], w_ref[...])
     for ref in sums:
         grad_in = grad_in + ref[0]
@@ -192,24 +200,26 @@
     out_ref[0], out_ref[1] = grad_in, grad_out
     rows = own_ref.shape[0]
     for ref in sends:
-        n = ref.shape[0] // rows
-        for k in range(n):
-            ref[k * rows : (k + 1) * rows, :] = columns[k][...].astype(jnp.float32)
-        columns = columns[n:]
-
-
-def piece_specs(rows, size, width):
-    tokens = pl.BlockSpec((2 * rows, width), lambda i, idx: (0, 0))
+        for k, column_ref in enumerate(columns):
+            ref[k * rows : (k + 1) * rows, :] = column_ref[...].astype(jnp.float32)
+
+
+def columns_spec(rows, size, at):
+    return pl.BlockSpec((rows, size), lambda i, table: (0, table[at]))
+
+
+def piece_specs(rows, size, width, at):
+    tokens = pl.BlockSpec((2 * rows, width), lambda i, table: (0, 0))
     return [
-        pl.BlockSpec((rows, size), lambda i, idx: (0, idx[0])),
+        columns_spec(rows, size, at),
         tokens,
         tokens,
-        pl.BlockSpec((size, width), lambda i, idx: (idx[0], 0)),
+        pl.BlockSpec((size, width), lambda i, table: (table[at], 0)),
     ]
 
 
 def partner_spec(rows, size, place):
-    return pl.BlockSpec((rows, size), lambda i, idx: (place, 0))
+    return pl.BlockSpec((rows, size), lambda i, table: (place, 0))
 
 
 def piece_cost(flops=1):
@@ -217,81 +227,69 @@
 
 
 def piece(
-    scale, index, pre_act, partners, place, g, x, w_out, sums=(), other=None, is_inner=None, sends=(), after=(), flops=1
+    scale, table, at, pre_act, partners, place, g, x, w_out, sums=(), other=None, inner_at=0, sends=(), after=(), flops=1
 ):
     rows, width = pre_act.shape[0], g.shape[1]
     size = sum(p.shape[1] for p in partners)
-    whole = pl.BlockSpec((2, size, width), lambda i, idx: (0, 0, 0))
+    whole = pl.BlockSpec((2, size, width), lambda i, table: (0, 0, 0))
     others, other_specs = [], []
     if other is not None:
         others = [other[0]]
         other_specs = [partner_spec(rows, size, other[1])]
-    columns = [column for send in sends for column in send]
-    zero = jnp.int32(0)
-    counts = (len(partners), len(others), len(columns), len(sums), len(after))
-    out, *blocks = pl.pallas_call(
-        functools.partial(piece_kernel, scale, counts),
+    counts = (len(partners), len(others), len(sends), len(sums), len(after))
+    sent = [(len(sends) * rows, size)] if sends else []
+    return pl.pallas_call(
+        functools.partial(piece_kernel, scale, counts, inner_at),
         grid_spec=pltpu.PrefetchScalarGridSpec(
             num_scalar_prefetch=1,
             grid=(1,),
-            in_specs=piece_specs(rows, size, width)
+            in_specs=piece_specs(rows, size, width, at)
             + [partner_spec(rows, p.shape[1], place) for p in partners]
             + other_specs
-            + [pl.BlockSpec((rows, size), lambda i, idx, k=k: (0, idx[3 + k])) for k in range(len(columns))]
+            + [columns_spec(rows, size, k) for k in sends]
             + [whole] * len(sums)
             + anywhere(after),
-            out_specs=[whole] + [pl.BlockSpec((len(send) * rows, size), lambda i, idx: (0, 0)) for send in sends],
+            out_specs=[whole] + [pl.BlockSpec(shape, lambda i, table: (0, 0)) for shape in sent],
         ),
-        out_shape=[jax.ShapeDtypeStruct((2, size, width), jnp.float32)]
-        + [jax.ShapeDtypeStruct((len(send) * rows, size), jnp.float32) for send in sends],
+        out_shape=[jax.ShapeDtypeStruct(shape, jnp.float32) for shape in [(2, size, width)] + sent],
         compiler_params=params(),
         cost_estimate=piece_cost(flops),
         name="piece",
-    )(
-        jnp.stack([index, zero, zero if is_inner is None else is_inner, *columns]),
-        pre_act,
-        g,
-        x,
-        w_out,
-        *partners,
-        *others,
-        *([pre_act] * len(columns)),
-        *sums,
-        *after,
-    )
-    return out, *blocks
-
-
-def final_kernel(scale, idx_ref, own_ref, g_ref, x_ref, w_ref, partner_ref, inner_ref, outer_ref, *refs):
+    )(table, pre_act, g, x, w_out, *partners, *others, *([pre_act] * len(sends)), *sums, *after)
+
+
+def final_kernel(scale, inner_at, table_ref, own_ref, g_ref, x_ref, w_ref, partner_ref, inner_ref, outer_ref, *refs):
     sum_ref, (in_ref, out_ref) = refs[0], refs[-2:]
     grad_in, grad_out = piece_math(
         scale, own_ref[...], partner_ref[...], g_ref[...], x_ref[...], w_ref[...]
     )
-    is_inner = idx_ref[1] > 0
+    is_inner = table_ref[inner_at] > 0
     in_ref[...] = jnp.where(is_inner, inner_ref[0], grad_in + outer_ref[0]) + sum_ref[0]
     out_ref[...] = jnp.where(is_inner, inner_ref[1], grad_out + outer_ref[1]) + sum_ref[1]
 
 
-def final_first(scale, count, index, is_inner, pre_act, partner, place, g, x, w_out, held, received, added, after):
+def final_first(
+    scale, count, table, at, inner_at, pre_act, partner, place, g, x, w_out, held, received, added, after
+):
     rows, size, width = pre_act.shape[0], partner.shape[1], g.shape[1]
-    whole = pl.BlockSpec((2, size, width), lambda i, idx: (0, 0, 0))
+    whole = pl.BlockSpec((2, size, width), lambda i, table: (0, 0, 0))
     shape = jax.ShapeDtypeStruct((count * size, width), jnp.float32)
     return pl.pallas_call(
-        functools.partial(final_kernel, scale),
+        functools.partial(final_kernel, scale, inner_at),
         grid_spec=pltpu.PrefetchScalarGridSpec(
             num_scalar_prefetch=1,
             grid=(1,),
-            in_specs=piece_specs(rows, size, width)
+            in_specs=piece_specs(rows, size, width, at)
             + [partner_spec(rows, size, place)]
             + [whole] * 3
             + anywhere(after),
-            out_specs=[pl.BlockSpec((size, width), lambda i, idx: (0, 0))] * 2,
+            out_specs=[pl.BlockSpec((size, width), lambda i, table: (0, 0))] * 2,
         ),
         out_shape=(shape, shape),
         compiler_params=params(),
         cost_estimate=piece_cost(),
         name="final_first",
-    )(jnp.stack([index, is_inner]), pre_act, g, x, w_out, partner, held, received, added, *after)
+    )(table, pre_act, g, x, w_out, partner, held, received, added, *after)
 
 
 def add_kernel(a_ref, b_ref, *refs):
@@ -377,77 +375,133 @@
         [(near_inner[1], near_outer[1]), (near_inner[2], near_outer[2])],
     ]
 
+    third, column = size // 3, theirs(first) * 3
+    values, places = [inner], {}
+
+    def put(name, value):
+        places[name] = len(values)
+        values.append(value)
+
+    for s in range(steps):
+        put(("main", s), mine(main[s]))
+    for j in range(count):
+        put(("out", j), mine(by_role(near_outer[j], ahead[double + j])))
+        put(("own", j), mine(own_chunk[j]))
+    for e, pairs in enumerate(exchanges):
+        for k, pair in enumerate(pairs):
+            put(("send", e, k), theirs(by_role(*pair)))
+    put("first mine", mine(first))
+    put("first theirs", theirs(first))
+    put("first part", column + 1)
+    put("second part", column + 2)
+    table = jnp.stack(values)
+
     def columns_of(e):
-        return [theirs(by_role(*pair)) for pair in exchanges[e]]
-
-    raw = [cast_block(theirs(first), pre_act, size, [])]
-    quarter, send, last = start_sends(
-        blk, out_grads, inputs, columns_of(0) + [mine(first)], pre_act, size, raw
-    )
-    raw.append(last)
+        return [places["send", e, k] for k in range(len(exchanges[e]))]
+
+    quarter, raw_0 = first_sends(jnp.stack([blk, column]), out_grads, inputs, pre_act, third)
+    raw_1, send_0, raw_2, send_1 = cast_blocks(
+        table,
+        [
+            (third, [places["first part"], places["second part"]]),
+            (size, columns_of(0)),
+            (size, [places["first mine"]]),
+            (size, columns_of(1)),
+        ],
+        pre_act,
+        [raw_0],
+    )
+
+    def send_in(array):
+        return lax.ppermute(array, "dp", outer_to_inner)
+
+    tied = lax.optimization_barrier
     pair_0 = swap(quarter, every)
-    got = [swap(send, every)]
-    quarter_in = lax.ppermute(quarter, "dp", outer_to_inner)
-    raw_in = [lax.ppermute(array, "dp", outer_to_inner) for array in raw]
-    last = cast_block(columns_of(1)[0], pre_act, size, [pair_0])
-    got.append(swap(last, every))
+    raw_0, raw_1, raw_2 = send_in(raw_0), send_in(raw_1), send_in(raw_2)
+    quarter_in = send_in(quarter)
+    got = [swap(send_0, every), swap(send_1, every)]
+    pair_0, raw_0 = tied((pair_0, raw_0))
     pair_1, pair_2 = flip(pair_0, 1), flip(pair_0, 2)
-    pair_2, got[0], raw_in[0] = lax.optimization_barrier((pair_2, got[0], raw_in[0]))
+    pair_2, pair_1, got[0], raw_1 = tied((pair_2, pair_1, got[0], raw_1))
     pair_3 = flip(pair_2, 1)
-    pair_3, quarter_in = lax.optimization_barrier((pair_3, quarter_in))
-    line_rows = lax.all_gather(quarter_in, "blk", tiled=True)
-    g, x = join(blk, out_grads, inputs, [pair_0, pair_1, pair_2, pair_3], [last, got[0], raw_in[0]])
+    g, x = join(blk, out_grads, inputs, [pair_0, pair_1, pair_2, pair_3], [got[0], raw_1])
     last = g
 
-    def run(q, partner, **more):
-        return piece(scale, mine(q), pre_act, [partner[0]], partner[1], g, x, w_out, **more)
+    def run(name, partner, **more):
+        return piece(scale, table, places[name], pre_act, [partner[0]], partner[1], g, x, w_out, **more)
 
     toward, across = [], {}
     for s in range(steps):
         partner = (got[s], 0) if s < 2 else (got[1 + s // 2], s % 2)
         sends = columns_of(2 + s // 2) if s % 2 == 0 else []
         sums = [toward[s - 2]] if s >= 2 else []
-        held_back = ([across[s - 4]] if s >= 4 else []) + ([raw_in[1]] if s == 1 else []) + ([first_in] if s == 3 else [])
+        held_back = ([across[s - 4]] if s >= 4 else []) + ([first_in] if s == 3 else [])
         j = s - double
         if j < 0:
-            after = [last] + held_back
+            after = [last] + held_back + ([raw_2] if s == 0 else [])
         else:
             (last,) = run(
-                by_role(near_outer[j], ahead[s]),
+                ("out", j),
                 partner,
                 sums=[across[j]],
                 other=(got[j], 0) if j < 2 else (got[4], 2),
-                is_inner=inner,
                 after=[last] + sums + held_back,
             )
             toward.append(lax.ppermute(last, "dp", outer_to_inner + inner_to_outer))
             after = [last] + ([grad_inputs] if j == 0 else [])
-        out, *blocks = run(main[s], partner, sums=sums, sends=[sends] if sends else [], after=after, flops=FLOPS if s == 3 else 1)
+        out, *blocks = run(
+            ("main", s), partner, sums=sums, sends=sends, after=after, flops=FLOPS if s == 3 else 1
+        )
         last = out
         if j < 0:
-            toward.append(lax.ppermute(out, "dp", outer_to_inner))
+            toward.append(send_in(out))
         if blocks:
             got.append(swap(blocks[0], every))
         if s >= 2:
             across[s - 2] = lax.ppermute(out, "dp", inner_to_inner)
+        if s == 0:
+            out, quarter_in = tied((out, quarter_in))
+            line_rows = lax.all_gather(quarter_in, "blk", tiled=True)
         if s == 1:
-            line_g, line_x = join(blk, out_grads, inputs, [line_rows], [last])
-            (last,) = piece(scale, theirs(first), pre_act, [raw_in[0]], 0, line_g, line_x, w_out, after=[last])
-            first_in = swap(last, inner_planes)
             last = input_partial(out_grads, pre_act, w_in, w_out, 4 * size, [last])
             grad_inputs = lax.psum_scatter(last, "blk", scatter_dimension=0, tiled=True)
             grad_inputs = grad_inputs.astype(jnp.bfloat16)
+            line_g, line_x = join(blk, out_grads, inputs, [line_rows], [last])
+            (last,) = piece(
+                scale,
+                table,
+                places["first theirs"],
+                pre_act,
+                [raw_0, raw_1],
+                0,
+                line_g,
+                line_x,
+                w_out,
+                after=[last],
+            )
+            first_in = swap(last, inner_planes)
         if s == 4:
             (held_in,) = piece(
-                scale, mine(first), pre_act, [raw_in[1]], 0, line_g, line_x, w_out, sums=[first_in], after=[last]
+                scale,
+                table,
+                places["first mine"],
+                pre_act,
+                [raw_2],
+                0,
+                line_g,
+                line_x,
+                w_out,
+                sums=[first_in],
+                after=[last],
             )
             last = held_in
 
     held = final_first(
         scale,
         count,
-        mine(jnp.int32(near_outer[0])),
-        inner,
+        table,
+        places["own", 0],
+        0,
         pre_act,
         got[4],
         2,
@@ -460,7 +514,7 @@
         [last],
     )
     for i in range(1, count):
-        (out,) = run(own_chunk[i], (got[5], i - 1), sums=[across[count + i]], after=[held[0]])
+        (out,) = run(("own", i), (got[5], i - 1), sums=[across[count + i]], after=[held[0]])
         held = final_add(i, out, toward[double + i], held, [])
     return (grad_inputs, held[0], held[1])
 

time: 352 us -> 344 us (0.977)
  local copies, waits for them, and re-layouts: 9.07 us -> 2.32 us
  starting transfers between devices: 36 us -> 40.3 us
    ppermute x8 -> x9, waiting for transfers between devices: 62.6 us -> 51.8 us  [send_in(): return lax.ppermute(array, 'dp', outer_to_inner)]
    another operation x10 -> x1, local copies, waits for them, and re-layouts: 5.15 us -> 0.68 us  [line_body(): table = jnp.stack(values)]
    ppermute x8, waiting for transfers between devices: 42.8 us -> 46.6 us  [swap(): lax.ppermute(array, 'dp', [(2 * a + h, 2 * a + 1 - h) for a in planes for...]
    ppermute x8 -> x9, starting transfers between devices: 10.3 us -> 11.5 us  [send_in(): return lax.ppermute(array, 'dp', outer_to_inner)]
    pallas_call x19 -> x18, Pallas kernels: 105 us -> 104 us  [the longest x15 91.6 us: piece(): pl.pallas_call(functools.partial(piece_kernel, scale, counts, inner_at),...]
  transfers between devices with their start and end apart: 30 -> 31, of which waited for: 16 -> 18; matrix products, arithmetic and copies ran while one was open for 3% -> 1% of each run, Pallas kernels for 36% -> 38%
where the time goes in v4:
time: 344 us; the launch traced here: 342 us
  waiting for transfers between devices  148 us (43%)
  Pallas kernels  135 us (39%)
  starting transfers between devices  40.3 us (12%)
  between operations  14.9 us (4%)
    pallas_call x15, Pallas kernels, piece(): pl.pallas_call(functools.partial(piece_kernel, scale, counts, inner_at),...  91.6 us
    ppermute x9, waiting for transfers between devices, send_in(): return lax.ppermute(array, 'dp', outer_to_inner)  51.8 us
    ppermute x8, waiting for transfers between devices, swap(): lax.ppermute(array, 'dp', [(2 * a + h, 2 * a + 1 - h) for a in planes for...  46.6 us
    ppermute x3, waiting for transfers between devices, line_body(): toward.append(lax.ppermute(last, 'dp', outer_to_inner + inner_to_outer))  33.4 us
    pallas_call x1, Pallas kernels, input_partial(): pl.pallas_call(input_kernel, grid=(hidden // size,), in_specs=[tokens, pl...  16.4 us
    ppermute x6, waiting for transfers between devices, line_body(): across[s - 2] = lax.ppermute(out, 'dp', inner_to_inner)  15 us
    ppermute x6, starting transfers between devices, line_body(): across[s - 2] = lax.ppermute(out, 'dp', inner_to_inner)  14.5 us
    ppermute x8, starting transfers between devices, swap(): lax.ppermute(array, 'dp', [(2 * a + h, 2 * a + 1 - h) for a in planes for...  12.4 us
  transfers between devices with their start and end apart: 31, of which 18 were waited for; matrix products, arithmetic and copies ran while one was open for 1% of the time, Pallas kernels for 38%

profile of v4, /device:TPU:16, one launch (start us, length us, event | category | flops | bytes accessed | tf_op | source)
XLA Modules:
  0.0 342.5 jit_solution(3231122093925073982)
XLA Ops:
  28.4 7.4 %collective-permute-done.5.refs_5_.refs_1_ = f32[512,256]{1,0:T(8,128)S(1)} collective-permute-done((f32[512,256]{1,0:T(8,128)}, f32[512,256]{1,0:T(8,128)S(1)}, u32[]{:S(2)}, u32[]{:S(2)}) %collective-permute-start.5) | collective-permute-done | bytes 524320 | tf_op jit(solution)/shard_map/ppermute | solution.py:416
  52.6 6.2 %piece.15 = (f32[2,384,512]{2,1,0:T(8,128)}, f32[1024,384]{1,0:T(8,128)}) custom-call(s32[30]{0:T(128)} %stack.130.idx_ref.table_ref, bf16[512,9216]{1,0:T(8,128)(2,1)} %own_ref.31, bf16[1024,512]{1,0:T(8,128)(2,1)} %get-tuple-element.43.g_ref.refs_3_, bf16[1024,512]{1,0:T(8,128)(2,1)} %get-tuple-element.44.x_ref, bf16[9216,512]{1,0:T(8,128)(2,1)} %w_ref.31, ...), custom_call_target="tpu_custom_call" | custom-call | flops 1 | bytes 1 | tf_op jit(solution)/shard_map/piece/pallas_call | solution.py:241
  71.7 16.4 %input_partial.1.refs_1_.refs_2_ = f32[512,512]{1,0:T(8,128)} custom-call(bf16[512,512]{1,0:T(8,128)(2,1)} %grads_ref.7, bf16[512,9216]{1,0:T(8,128)(2,1)} %own_ref.31, bf16[9216,512]{1,0:T(8,128)(2,1)} %w_ref.31, bf16[9216,512]{1,0:T(8,128)(2,1)} %in_rows_ref.1, f32[2,384,512]{2,1,0:T(8,128)} %piece.16.refs_0_), custom_call_target="tpu_custom_call" | custom-call | flops 99999997952 | bytes 1 | tf_op jit(solution)/shard_map/input_partial/pallas_call | solution.py:168
  99.7 8.2 %collective-permute-done.9.refs_0_ = f32[1024,384]{1,0:T(8,128)} collective-permute-done((f32[1024,384]{1,0:T(8,128)}, f32[1024,384]{1,0:T(8,128)}, u32[]{:S(2)}, u32[]{:S(2)}) %collective-permute-start.9) | collective-permute-done | bytes 1572896 | tf_op jit(solution)/shard_map/ppermute | solution.py:334
  107.9 6.8 %piece.18 = (f32[2,384,512]{2,1,0:T(8,128)}, f32[1024,384]{1,0:T(8,128)}) custom-call(s32[30]{0:T(128)} %stack.130.idx_ref.table_ref, bf16[512,9216]{1,0:T(8,128)(2,1)} %own_ref.31, bf16[1024,512]{1,0:T(8,128)(2,1)} %get-tuple-element.43.g_ref.refs_3_, bf16[1024,512]{1,0:T(8,128)(2,1)} %get-tuple-element.44.x_ref, bf16[9216,512]{1,0:T(8,128)(2,1)} %w_ref.31, ...), custom_call_target="tpu_custom_call" | custom-call | flops 1 | bytes 1 | tf_op jit(solution)/shard_map/piece/pallas_call | solution.py:241
  119.9 12.1 %collective-permute-done.14.refs_1_ = f32[2,384,512]{2,1,0:T(8,128)} collective-permute-done((f32[2,384,512]{2,1,0:T(8,128)}, f32[2,384,512]{2,1,0:T(8,128)}, u32[]{:S(2)}, u32[]{:S(2)}) %collective-permute-start.14) | collective-permute-done | bytes 1572896 | tf_op jit(solution)/shard_map/ppermute | solution.py:416
  132.1 9.5 %collective-permute-done.15.refs_3_.refs_1_ = f32[2,384,512]{2,1,0:T(8,128)} collective-permute-done((f32[2,384,512]{2,1,0:T(8,128)}, f32[2,384,512]{2,1,0:T(8,128)}, u32[]{:S(2)}, u32[]{:S(2)}) %collective-permute-start.15) | collective-permute-done | bytes 1572896 | tf_op jit(solution)/shard_map/ppermute | solution.py:334
  151.3 20.2 %collective-permute-done.12.refs_0_ = f32[1024,384]{1,0:T(8,128)} collective-permute-done((f32[1024,384]{1,0:T(8,128)}, f32[1024,384]{1,0:T(8,128)}, u32[]{:S(2)}, u32[]{:S(2)}) %collective-permute-start.12) | collective-permute-done | bytes 1572896 | tf_op jit(solution)/shard_map/ppermute | solution.py:334
  171.6 7.0 %piece.20 = (f32[2,384,512]{2,1,0:T(8,128)}, f32[1536,384]{1,0:T(8,128)}) custom-call(s32[30]{0:T(128)} %stack.130.idx_ref.table_ref, bf16[512,9216]{1,0:T(8,128)(2,1)} %own_ref.31, bf16[1024,512]{1,0:T(8,128)(2,1)} %get-tuple-element.43.g_ref.refs_3_, bf16[1024,512]{1,0:T(8,128)(2,1)} %get-tuple-element.44.x_ref, bf16[9216,512]{1,0:T(8,128)(2,1)} %w_ref.31, ...), custom_call_target="tpu_custom_call" | custom-call | flops 1 | bytes 1 | tf_op jit(solution)/shard_map/piece/pallas_call | solution.py:241
  191.3 8.2 %collective-permute-done.20.refs_4_.refs_1_ = f32[2,384,512]{2,1,0:T(8,128)} collective-permute-done((f32[2,384,512]{2,1,0:T(8,128)}, f32[2,384,512]{2,1,0:T(8,128)}, u32[]{:S(2)}, u32[]{:S(2)}) %collective-permute-start.20) | collective-permute-done | bytes 1572896 | tf_op jit(solution)/shard_map/ppermute | solution.py:416
  199.5 6.2 %piece.22.refs_2_ = f32[2,384,512]{2,1,0:T(8,128)} custom-call(s32[30]{0:T(128)} %stack.130.idx_ref.table_ref, bf16[512,9216]{1,0:T(8,128)(2,1)} %own_ref.31, bf16[1024,512]{1,0:T(8,128)(2,1)} %get-tuple-element.43.g_ref.refs_3_, bf16[1024,512]{1,0:T(8,128)(2,1)} %get-tuple-element.44.x_ref, bf16[9216,512]{1,0:T(8,128)(2,1)} %w_ref.31, ...), custom_call_target="tpu_custom_call" | custom-call | flops 1 | bytes 1 | tf_op jit(solution)/shard_map/piece/pallas_call | solution.py:241
  205.6 6.0 %piece.23.refs_3_ = f32[2,384,512]{2,1,0:T(8,128)} custom-call(s32[30]{0:T(128)} %stack.130.idx_ref.table_ref, bf16[512,9216]{1,0:T(8,128)(2,1)} %own_ref.31, bf16[1024,512]{1,0:T(8,128)(2,1)} %get-tuple-element.43.g_ref.refs_3_, bf16[1024,512]{1,0:T(8,128)(2,1)} %get-tuple-element.44.x_ref, bf16[9216,512]{1,0:T(8,128)(2,1)} %w_ref.31, ...), custom_call_target="tpu_custom_call" | custom-call | flops 1 | bytes 1 | tf_op jit(solution)/shard_map/piece/pallas_call | solution.py:241
  217.6 15.6 %collective-permute-done.18.refs_4_.refs_3_ = f32[2,384,512]{2,1,0:T(8,128)} collective-permute-done((f32[2,384,512]{2,1,0:T(8,128)}, f32[2,384,512]{2,1,0:T(8,128)}, u32[]{:S(2)}, u32[]{:S(2)}) %collective-permute-start.18) | collective-permute-done | bytes 1572896 | tf_op jit(solution)/shard_map/ppermute | solution.py:416
  233.2 6.2 %piece.24.refs_4_ = f32[2,384,512]{2,1,0:T(8,128)} custom-call(s32[30]{0:T(128)} %stack.130.idx_ref.table_ref, bf16[512,9216]{1,0:T(8,128)(2,1)} %own_ref.31, bf16[1024,512]{1,0:T(8,128)(2,1)} %get-tuple-element.43.g_ref.refs_3_, bf16[1024,512]{1,0:T(8,128)(2,1)} %get-tuple-element.44.x_ref, bf16[9216,512]{1,0:T(8,128)(2,1)} %w_ref.31, ...), custom_call_target="tpu_custom_call" | custom-call | flops 1 | bytes 1 | tf_op jit(solution)/shard_map/piece/pallas_call | solution.py:241
  239.4 6.6 %piece.25 = (f32[2,384,512]{2,1,0:T(8,128)}, f32[1024,384]{1,0:T(8,128)}) custom-call(s32[30]{0:T(128)} %stack.130.idx_ref.table_ref, bf16[512,9216]{1,0:T(8,128)(2,1)} %own_ref.31, bf16[1024,512]{1,0:T(8,128)(2,1)} %get-tuple-element.43.g_ref.refs_3_, bf16[1024,512]{1,0:T(8,128)(2,1)} %get-tuple-element.44.x_ref, bf16[9216,512]{1,0:T(8,128)(2,1)} %w_ref.31, ...), custom_call_target="tpu_custom_call" | custom-call | flops 1 | bytes 1 | tf_op jit(solution)/shard_map/piece/pallas_call | solution.py:241
  250.0 16.9 %collective-permute-done.23.refs_4_.refs_1_.outer_ref = f32[2,384,512]{2,1,0:T(8,128)} collective-permute-done((f32[2,384,512]{2,1,0:T(8,128)}, f32[2,384,512]{2,1,0:T(8,128)}, u32[]{:S(2)}, u32[]{:S(2)}) %collective-permute-start.23) | collective-permute-done | bytes 1572896 | tf_op jit(solution)/shard_map/ppermute | solution.py:450
  266.9 6.2 %piece.26.refs_2_ = f32[2,384,512]{2,1,0:T(8,128)} custom-call(s32[30]{0:T(128)} %stack.130.idx_ref.table_ref, bf16[512,9216]{1,0:T(8,128)(2,1)} %own_ref.31, bf16[1024,512]{1,0:T(8,128)(2,1)} %get-tuple-element.43.g_ref.refs_3_, bf16[1024,512]{1,0:T(8,128)(2,1)} %get-tuple-element.44.x_ref, bf16[9216,512]{1,0:T(8,128)(2,1)} %w_ref.31, ...), custom_call_target="tpu_custom_call" | custom-call | flops 1 | bytes 1 | tf_op jit(solution)/shard_map/piece/pallas_call | solution.py:241
  273.0 6.0 %piece.27.refs_1_ = f32[2,384,512]{2,1,0:T(8,128)} custom-call(s32[30]{0:T(128)} %stack.130.idx_ref.table_ref, bf16[512,9216]{1,0:T(8,128)(2,1)} %own_ref.31, bf16[1024,512]{1,0:T(8,128)(2,1)} %get-tuple-element.43.g_ref.refs_3_, bf16[1024,512]{1,0:T(8,128)(2,1)} %get-tuple-element.44.x_ref, bf16[9216,512]{1,0:T(8,128)(2,1)} %w_ref.31, ...), custom_call_target="tpu_custom_call" | custom-call | flops 1 | bytes 1 | tf_op jit(solution)/shard_map/piece/pallas_call | solution.py:241
  281.7 6.6 %final_first.1 = (f32[1152,512]{1,0:T(8,128)}, f32[1152,512]{1,0:T(8,128)}) custom-call(s32[30]{0:T(128)} %stack.130.idx_ref.table_ref, bf16[512,9216]{1,0:T(8,128)(2,1)} %own_ref.31, bf16[1024,512]{1,0:T(8,128)(2,1)} %get-tuple-element.43.g_ref.refs_3_, bf16[1024,512]{1,0:T(8,128)(2,1)} %get-tuple-element.44.x_ref, bf16[9216,512]{1,0:T(8,128)(2,1)} %w_ref.31, ...), custom_call_target="tpu_custom_call" | custom-call | flops 1 | bytes 1 | tf_op jit(solution)/shard_map/final_first/pallas_call | solution.py:277
  288.3 5.9 %piece.28.a_ref = f32[2,384,512]{2,1,0:T(8,128)} custom-call(s32[30]{0:T(128)} %stack.130.idx_ref.table_ref, bf16[512,9216]{1,0:T(8,128)(2,1)} %own_ref.31, bf16[1024,512]{1,0:T(8,128)(2,1)} %get-tuple-element.43.g_ref.refs_3_, bf16[1024,512]{1,0:T(8,128)(2,1)} %get-tuple-element.44.x_ref, bf16[9216,512]{1,0:T(8,128)(2,1)} %w_ref.31, ...), custom_call_target="tpu_custom_call" | custom-call | flops 1 | bytes 1 | tf_op jit(solution)/shard_map/piece/pallas_call | solution.py:241
  294.2 6.4 %collective-permute-done.27.b_ref = f32[2,384,512]{2,1,0:T(8,128)} collective-permute-done((f32[2,384,512]{2,1,0:T(8,128)}, f32[2,384,512]{2,1,0:T(8,128)}, u32[]{:S(2)}, u32[]{:S(2)}) %collective-permute-start.27) | collective-permute-done | bytes 1572896 | tf_op jit(solution)/shard_map/ppermute | solution.py:450
  304.3 11.5 %collective-permute-done.25.refs_1_ = f32[2,384,512]{2,1,0:T(8,128)} collective-permute-done((f32[2,384,512]{2,1,0:T(8,128)}, f32[2,384,512]{2,1,0:T(8,128)}, u32[]{:S(2)}, u32[]{:S(2)}) %collective-permute-start.25) | collective-permute-done | bytes 1572896 | tf_op jit(solution)/shard_map/ppermute | solution.py:461
  315.8 6.0 %piece.29.a_ref = f32[2,384,512]{2,1,0:T(8,128)} custom-call(s32[30]{0:T(128)} %stack.130.idx_ref.table_ref, bf16[512,9216]{1,0:T(8,128)(2,1)} %own_ref.31, bf16[1024,512]{1,0:T(8,128)(2,1)} %get-tuple-element.43.g_ref.refs_3_, bf16[1024,512]{1,0:T(8,128)(2,1)} %get-tuple-element.44.x_ref, bf16[9216,512]{1,0:T(8,128)(2,1)} %w_ref.31, ...), custom_call_target="tpu_custom_call" | custom-call | flops 1 | bytes 1 | tf_op jit(solution)/shard_map/piece/pallas_call | solution.py:241
  321.8 10.1 %collective-permute-done.28.b_ref = f32[2,384,512]{2,1,0:T(8,128)} collective-permute-done((f32[2,384,512]{2,1,0:T(8,128)}, f32[2,384,512]{2,1,0:T(8,128)}, u32[]{:S(2)}, u32[]{:S(2)}) %collective-permute-start.28) | collective-permute-done | bytes 1572896 | tf_op jit(solution)/shard_map/ppermute | solution.py:450
  (74 shorter events, 109.5 us)
Async XLA Ops:
  7.2 81.0 %all-gather.2.cloned.1.call-start = ((), (), s32[]{:S(2)}) async-start(), calls=%async_computation.2 | async-start | bytes 2621440 | tf_op jit(solution)/shard_map/all_gather | solution.py:464
  18.3 24.1 %collective-permute-start.4 = (f32[512,384]{1,0:T(8,128)}, f32[512,384]{1,0:T(8,128)S(1)}, u32[]{:S(2)}, u32[]{:S(2)}) collective-permute-start(f32[512,384]{1,0:T(8,128)} %get-tuple-element.37), channel_id=1, source_target_pairs={{0,4},{4,0},{8,12},{12,8},{16,20},{20,16},{24,28},{28,24},{1,5},{5... | collective-permute-start | bytes 2359304 | tf_op jit(solution)/shard_map/ppermute | solution.py:334
  27.1 25.5 %collective-permute-start.8 = (f32[512,384]{1,0:T(8,128)}, f32[512,384]{1,0:T(8,128)}, u32[]{:S(2)}, u32[]{:S(2)}) collective-permute-start(f32[512,384]{1,0:T(8,128)} %get-tuple-element.46), channel_id=1, source_target_pairs={{0,8},{4,12},{24,16},{28,20},{1,9},{5,13},{25,17},{29,21},{2,10},{... | collective-permute-start | bytes 2359304 | tf_op jit(solution)/shard_map/ppermute | solution.py:416
  35.8 27.7 %collective-permute-start.7 = (f32[512,384]{1,0:T(8,128)}, f32[512,384]{1,0:T(8,128)}, u32[]{:S(2)}, u32[]{:S(2)}) collective-permute-start(f32[512,384]{1,0:T(8,128)} %get-tuple-element.45), channel_id=1, source_target_pairs={{0,4},{4,0},{8,12},{12,8},{16,20},{20,16},{24,28},{28,24},{1,5},{5... | collective-permute-start | bytes 2359304 | tf_op jit(solution)/shard_map/ppermute | solution.py:334
  58.8 49.1 %collective-permute-start.10 = (f32[2,384,512]{2,1,0:T(8,128)}, f32[2,384,512]{2,1,0:T(8,128)}, u32[]{:S(2)}, u32[]{:S(2)}) collective-permute-start(f32[2,384,512]{2,1,0:T(8,128)} %get-tuple-element.47.refs_1_), channel_id=1, source_target_pairs={{0,8},{4,12},{24,16},{28,20},{1,9},{5,13},{25,17},{29,21},{2,10},{... | collective-permute-start | bytes 4718600 | tf_op jit(solution)/shard_map/ppermute | solution.py:416
  63.4 120.3 %reduce-scatter.2.cloned.1.call-start = ((), (), s32[]{:S(2)}) async-start(), calls=%async_computation.1 | async-start | bytes 1310720 | tf_op jit(solution)/shard_map/reduce_scatter | solution.py:467
  68.9 63.2 %collective-permute-start.14 = (f32[2,384,512]{2,1,0:T(8,128)}, f32[2,384,512]{2,1,0:T(8,128)}, u32[]{:S(2)}, u32[]{:S(2)}) collective-permute-start(f32[2,384,512]{2,1,0:T(8,128)} %piece.16.refs_0_), channel_id=1, source_target_pairs={{0,8},{4,12},{24,16},{28,20},{1,9},{5,13},{25,17},{29,21},{2,10},{... | collective-permute-start | bytes 4718600 | tf_op jit(solution)/shard_map/ppermute | solution.py:416
  70.2 37.7 %collective-permute-start.9 = (f32[1024,384]{1,0:T(8,128)}, f32[1024,384]{1,0:T(8,128)}, u32[]{:S(2)}, u32[]{:S(2)}) collective-permute-start(f32[1024,384]{1,0:T(8,128)} %get-tuple-element.48), channel_id=1, source_target_pairs={{0,4},{4,0},{8,12},{12,8},{16,20},{20,16},{24,28},{28,24},{1,5},{5... | collective-permute-start | bytes 4718600 | tf_op jit(solution)/shard_map/ppermute | solution.py:334
  97.0 44.6 %collective-permute-start.15 = (f32[2,384,512]{2,1,0:T(8,128)}, f32[2,384,512]{2,1,0:T(8,128)}, u32[]{:S(2)}, u32[]{:S(2)}) collective-permute-start(f32[2,384,512]{2,1,0:T(8,128)} %piece.17.refs_4_), channel_id=1, source_target_pairs={{8,12},{12,8},{16,20},{20,16},{9,13},{13,9},{17,21},{21,17},{10,14... | collective-permute-start | bytes 4718600 | tf_op jit(solution)/shard_map/ppermute | solution.py:334
  114.7 56.9 %collective-permute-start.16 = (f32[2,384,512]{2,1,0:T(8,128)}, f32[2,384,512]{2,1,0:T(8,128)}, u32[]{:S(2)}, u32[]{:S(2)}) collective-permute-start(f32[2,384,512]{2,1,0:T(8,128)} %get-tuple-element.54.refs_2_), channel_id=1, source_target_pairs={{8,16},{12,20},{16,8},{20,12},{9,17},{13,21},{17,9},{21,13},{10,18... | collective-permute-start | bytes 4718600 | tf_op jit(solution)/shard_map/ppermute | solution.py:461
  117.0 54.5 %collective-permute-start.13 = (f32[2,384,512]{2,1,0:T(8,128)}, f32[2,384,512]{2,1,0:T(8,128)}, u32[]{:S(2)}, u32[]{:S(2)}) collective-permute-start(f32[2,384,512]{2,1,0:T(8,128)} %get-tuple-element.54.refs_2_), channel_id=1, source_target_pairs={{0,8},{4,12},{24,16},{28,20},{1,9},{5,13},{25,17},{29,21},{2,10},{... | collective-permute-start | bytes 4718600 | tf_op jit(solution)/shard_map/ppermute | solution.py:416
  118.3 53.2 %collective-permute-start.12 = (f32[1024,384]{1,0:T(8,128)}, f32[1024,384]{1,0:T(8,128)}, u32[]{:S(2)}, u32[]{:S(2)}) collective-permute-start(f32[1024,384]{1,0:T(8,128)} %get-tuple-element.53), channel_id=1, source_target_pairs={{0,4},{4,0},{8,12},{12,8},{16,20},{20,16},{24,28},{28,24},{1,5},{5... | collective-permute-start | bytes 4718600 | tf_op jit(solution)/shard_map/ppermute | solution.py:334
  147.5 52.0 %collective-permute-start.20 = (f32[2,384,512]{2,1,0:T(8,128)}, f32[2,384,512]{2,1,0:T(8,128)}, u32[]{:S(2)}, u32[]{:S(2)}) collective-permute-start(f32[2,384,512]{2,1,0:T(8,128)} %piece.19.refs_5_), channel_id=1, source_target_pairs={{0,8},{4,12},{24,16},{28,20},{1,9},{5,13},{25,17},{29,21},{2,10},{... | collective-permute-start | bytes 4718600 | tf_op jit(solution)/shard_map/ppermute | solution.py:416
  148.8 50.7 %collective-permute-start.19 = (f32[2,384,512]{2,1,0:T(8,128)}, f32[2,384,512]{2,1,0:T(8,128)}, u32[]{:S(2)}, u32[]{:S(2)}) collective-permute-start(f32[2,384,512]{2,1,0:T(8,128)} %piece.19.refs_5_), channel_id=1, source_target_pairs={{8,16},{12,20},{16,8},{20,12},{9,17},{13,21},{17,9},{21,13},{10,18... | collective-permute-start | bytes 4718600 | tf_op jit(solution)/shard_map/ppermute | solution.py:461
  178.6 54.6 %collective-permute-start.17 = (f32[1536,384]{1,0:T(8,128)}, f32[1536,384]{1,0:T(8,128)}, u32[]{:S(2)}, u32[]{:S(2)}) collective-permute-start(f32[1536,384]{1,0:T(8,128)} %get-tuple-element.55), channel_id=1, source_target_pairs={{0,4},{4,0},{8,12},{12,8},{16,20},{20,16},{24,28},{28,24},{1,5},{5... | collective-permute-start | bytes 7077896 | tf_op jit(solution)/shard_map/ppermute | solution.py:334
  180.1 37.5 %collective-permute-start.21 = (f32[2,384,512]{2,1,0:T(8,128)}, f32[2,384,512]{2,1,0:T(8,128)}, u32[]{:S(2)}, u32[]{:S(2)}) collective-permute-start(f32[2,384,512]{2,1,0:T(8,128)} %get-tuple-element.56.refs_2_), channel_id=1, source_target_pairs={{8,16},{12,20},{16,8},{20,12},{9,17},{13,21},{17,9},{21,13},{10,18... | collective-permute-start | bytes 4718600 | tf_op jit(solution)/shard_map/ppermute | solution.py:461
  182.4 50.7 %collective-permute-start.18 = (f32[2,384,512]{2,1,0:T(8,128)}, f32[2,384,512]{2,1,0:T(8,128)}, u32[]{:S(2)}, u32[]{:S(2)}) collective-permute-start(f32[2,384,512]{2,1,0:T(8,128)} %get-tuple-element.56.refs_2_), channel_id=1, source_target_pairs={{0,8},{4,12},{24,16},{28,20},{1,9},{5,13},{25,17},{29,21},{2,10},{... | collective-permute-start | bytes 4718600 | tf_op jit(solution)/shard_map/ppermute | solution.py:416
  211.6 38.3 %collective-permute-start.24 = (f32[2,384,512]{2,1,0:T(8,128)}, f32[2,384,512]{2,1,0:T(8,128)}, u32[]{:S(2)}, u32[]{:S(2)}) collective-permute-start(f32[2,384,512]{2,1,0:T(8,128)} %piece.23.refs_3_), channel_id=1, source_target_pairs={{8,16},{12,20},{16,8},{20,12},{9,17},{13,21},{17,9},{21,13},{10,18... | collective-permute-start | bytes 4718600 | tf_op jit(solution)/shard_map/ppermute | solution.py:461
  214.0 52.9 %collective-permute-start.23 = (f32[2,384,512]{2,1,0:T(8,128)}, f32[2,384,512]{2,1,0:T(8,128)}, u32[]{:S(2)}, u32[]{:S(2)}) collective-permute-start(f32[2,384,512]{2,1,0:T(8,128)} %piece.22.refs_2_), channel_id=1, source_target_pairs={{0,8},{4,12},{24,16},{28,20},{8,0},{12,4},{16,24},{20,28},{1,9},{5... | collective-permute-start | bytes 4718600 | tf_op jit(solution)/shard_map/ppermute | solution.py:450
  246.0 42.2 %collective-permute-start.22 = (f32[1024,384]{1,0:T(8,128)}, f32[1024,384]{1,0:T(8,128)}, u32[]{:S(2)}, u32[]{:S(2)}) collective-permute-start(f32[1024,384]{1,0:T(8,128)} %get-tuple-element.57), channel_id=1, source_target_pairs={{0,4},{4,0},{8,12},{12,8},{16,20},{20,16},{24,28},{28,24},{1,5},{5... | collective-permute-start | bytes 4718600 | tf_op jit(solution)/shard_map/ppermute | solution.py:334
  247.5 40.7 %collective-permute-start.26 = (f32[2,384,512]{2,1,0:T(8,128)}, f32[2,384,512]{2,1,0:T(8,128)}, u32[]{:S(2)}, u32[]{:S(2)}) collective-permute-start(f32[2,384,512]{2,1,0:T(8,128)} %get-tuple-element.58.refs_3_), channel_id=1, source_target_pairs={{8,16},{12,20},{16,8},{20,12},{9,17},{13,21},{17,9},{21,13},{10,18... | collective-permute-start | bytes 4718600 | tf_op jit(solution)/shard_map/ppermute | solution.py:461
  249.9 50.7 %collective-permute-start.27 = (f32[2,384,512]{2,1,0:T(8,128)}, f32[2,384,512]{2,1,0:T(8,128)}, u32[]{:S(2)}, u32[]{:S(2)}) collective-permute-start(f32[2,384,512]{2,1,0:T(8,128)} %piece.24.refs_4_), channel_id=1, source_target_pairs={{0,8},{4,12},{24,16},{28,20},{8,0},{12,4},{16,24},{20,28},{1,9},{5... | collective-permute-start | bytes 4718600 | tf_op jit(solution)/shard_map/ppermute | solution.py:450
  279.0 36.8 %collective-permute-start.25 = (f32[2,384,512]{2,1,0:T(8,128)}, f32[2,384,512]{2,1,0:T(8,128)}, u32[]{:S(2)}, u32[]{:S(2)}) collective-permute-start(f32[2,384,512]{2,1,0:T(8,128)} %piece.27.refs_1_), channel_id=1, source_target_pairs={{8,16},{12,20},{16,8},{20,12},{9,17},{13,21},{17,9},{21,13},{10,18... | collective-permute-start | bytes 4718600 | tf_op jit(solution)/shard_map/ppermute | solution.py:461
  281.6 50.3 %collective-permute-start.28 = (f32[2,384,512]{2,1,0:T(8,128)}, f32[2,384,512]{2,1,0:T(8,128)}, u32[]{:S(2)}, u32[]{:S(2)}) collective-permute-start(f32[2,384,512]{2,1,0:T(8,128)} %piece.26.refs_2_), channel_id=1, source_target_pairs={{0,8},{4,12},{24,16},{28,20},{8,0},{12,4},{16,24},{20,28},{1,9},{5... | collective-permute-start | bytes 4718600 | tf_op jit(solution)/shard_map/ppermute | solution.py:450
  (11 other events, 109.8 us)
Sparse Core Ops, SparseCore 0:
  63.6 22.6 all-gather.1
  99.8 26.2 reduce-scatter.1

commit v5 on v4

--- a/solution.py
+++ b/solution.py
@@ -84,26 +84,26 @@
     )(table, *([pre_act] * len(in_specs)), *after)
 
 
-def first_kernel(idx_ref, grads_ref, inputs_ref, pre_ref, quarter_ref, raw_ref):
+def first_kernel(blk_ref, column_ref, grads_ref, inputs_ref, pre_ref, quarter_ref, raw_ref):
     quarter = grads_ref.shape[0]
     quarter_ref[:quarter, :] = grads_ref[...].astype(jnp.float32)
     quarter_ref[quarter:, :] = inputs_ref[...].astype(jnp.float32)
     raw_ref[...] = pre_ref[...].astype(jnp.float32)
 
 
-def first_sends(indices, out_grads, inputs, pre_act, size):
+def first_sends(blk, column, out_grads, inputs, pre_act, size):
     rows, width = out_grads.shape
     quarter = rows // 4
-    tokens = pl.BlockSpec((quarter, width), lambda i, idx: (idx[0], 0))
+    tokens = pl.BlockSpec((quarter, width), lambda i, blk, column: (blk[0], 0))
     return pl.pallas_call(
         first_kernel,
         grid_spec=pltpu.PrefetchScalarGridSpec(
-            num_scalar_prefetch=1,
+            num_scalar_prefetch=2,
             grid=(1,),
-            in_specs=[tokens, tokens, columns_spec(rows, size, 1)],
+            in_specs=[tokens, tokens, pl.BlockSpec((rows, size), lambda i, blk, column: (0, column[0]))],
             out_specs=[
-                pl.BlockSpec((2 * quarter, width), lambda i, idx: (0, 0)),
-                pl.BlockSpec((rows, size), lambda i, idx: (0, 0)),
+                pl.BlockSpec((2 * quarter, width), lambda i, blk, column: (0, 0)),
+                pl.BlockSpec((rows, size), lambda i, blk, column: (0, 0)),
             ],
         ),
         out_shape=[
@@ -113,40 +113,34 @@
         compiler_params=params(),
         cost_estimate=piece_cost(),
         name="first_sends",
-    )(indices, out_grads, inputs, pre_act)
-
-
-def join_kernel(n_quarters, blk_ref, grads_ref, inputs_ref, *refs):
-    quarters, (g_ref, x_ref) = refs[:n_quarters], refs[-2:]
+    )(blk.reshape(1), column.reshape(1), out_grads, inputs, pre_act)
+
+
+def join_kernel(grads_ref, inputs_ref, line_ref, *refs):
+    g_ref, x_ref = refs[-2:]
     rows = grads_ref.shape[0]
     quarter = rows // 4
     g_ref[:rows, :] = grads_ref[...]
     x_ref[:rows, :] = inputs_ref[...]
     for k in range(4):
-        if n_quarters == 1:
-            place = pl.ds(rows + k * quarter, quarter)
-            ref, start = quarters[0], 2 * k * quarter
-        else:
-            where = jnp.bitwise_xor(blk_ref[0], k)
-            place = pl.ds(pl.multiple_of(rows + where * quarter, quarter), quarter)
-            ref, start = quarters[k], 0
-        g_ref[place, :] = ref[start : start + quarter, :].astype(jnp.bfloat16)
-        x_ref[place, :] = ref[start + quarter : start + 2 * quarter, :].astype(jnp.bfloat16)
-
-
-def join(blk, out_grads, inputs, quarters, after):
+        place, start = pl.ds(rows + k * quarter, quarter), 2 * k * quarter
+        g_ref[place, :] = line_ref[start : start + quarter, :].astype(jnp.bfloat16)
+        x_ref[place, :] = line_ref[start + quarter : start + 2 * quarter, :].astype(jnp.bfloat16)
+
+
+def join(out_grads, inputs, line_rows, after):
     rows, width = out_grads.shape
     shape = jax.ShapeDtypeStruct((2 * rows, width), jnp.bfloat16)
     vmem = pl.BlockSpec(memory_space=pltpu.VMEM)
     return pl.pallas_call(
-        functools.partial(join_kernel, len(quarters)),
+        join_kernel,
         out_shape=(shape, shape),
-        in_specs=[pl.BlockSpec(memory_space=pltpu.SMEM)] + [vmem] * (2 + len(quarters)) + anywhere(after),
+        in_specs=[vmem] * 3 + anywhere(after),
         out_specs=(vmem, vmem),
         compiler_params=params(),
         cost_estimate=piece_cost(),
         name="join_tokens",
-    )(blk.reshape(1), out_grads, inputs, *quarters, *after)
+    )(out_grads, inputs, line_rows, *after)
 
 
 def input_kernel(grads_ref, pre_ref, out_rows_ref, in_rows_ref, *refs):
@@ -258,6 +252,65 @@
     )(table, pre_act, g, x, w_out, *partners, *others, *([pre_act] * len(sends)), *sums, *after)
 
 
+def first_piece_kernel(
+    scale, blk_at, table_ref, own_ref, w_ref, partner_ref, grads_ref, inputs_ref, q0_ref, q1_ref, q2_ref, q3_ref, a_ref, b_ref, *refs
+):
+    out_ref, g_ref, x_ref, send_ref = refs[-4:]
+    rows = grads_ref.shape[0]
+    quarter = rows // 4
+    g_ref[:rows, :] = grads_ref[...]
+    x_ref[:rows, :] = inputs_ref[...]
+    for k, ref in enumerate((q0_ref, q1_ref, q2_ref, q3_ref)):
+        where = jnp.bitwise_xor(table_ref[blk_at], k)
+        place = pl.ds(pl.multiple_of(rows + where * quarter, quarter), quarter)
+        g_ref[place, :] = ref[:quarter, :].astype(jnp.bfloat16)
+        x_ref[place, :] = ref[quarter:, :].astype(jnp.bfloat16)
+    out_ref[0], out_ref[1] = piece_math(
+        scale, own_ref[...], partner_ref[...], g_ref[...], x_ref[...], w_ref[...]
+    )
+    send_ref[:rows, :] = a_ref[...].astype(jnp.float32)
+    send_ref[rows:, :] = b_ref[...].astype(jnp.float32)
+
+
+def first_piece(scale, table, at, blk_at, pre_act, partner, out_grads, inputs, quarters, w_out, sends, after):
+    rows, width = out_grads.shape
+    size = partner.shape[1]
+    whole = lambda *shape: pl.BlockSpec(shape, lambda i, table: (0,) * len(shape))
+    tokens = jax.ShapeDtypeStruct((2 * rows, width), jnp.bfloat16)
+    return pl.pallas_call(
+        functools.partial(first_piece_kernel, scale, blk_at),
+        grid_spec=pltpu.PrefetchScalarGridSpec(
+            num_scalar_prefetch=1,
+            grid=(1,),
+            in_specs=[
+                columns_spec(rows, size, at),
+                pl.BlockSpec((size, width), lambda i, table: (table[at], 0)),
+                whole(rows, size),
+                whole(rows, width),
+                whole(rows, width),
+            ]
+            + [whole(rows // 2, width)] * 4
+            + [columns_spec(rows, size, k) for k in sends]
+            + anywhere(after),
+            out_specs=[
+                whole(2, size, width),
+                whole(2 * rows, width),
+                whole(2 * rows, width),
+                whole(2 * rows, size),
+            ],
+        ),
+        out_shape=[
+            jax.ShapeDtypeStruct((2, size, width), jnp.float32),
+            tokens,
+            tokens,
+            jax.ShapeDtypeStruct((2 * rows, size), jnp.float32),
+        ],
+        compiler_params=params(),
+        cost_estimate=piece_cost(),
+        name="first_piece",
+    )(table, pre_act, w_out, partner, out_grads, inputs, *quarters, pre_act, pre_act, *after)
+
+
 def final_kernel(scale, inner_at, table_ref, own_ref, g_ref, x_ref, w_ref, partner_ref, inner_ref, outer_ref, *refs):
     sum_ref, (in_ref, out_ref) = refs[0], refs[-2:]
     grad_in, grad_out = piece_math(
@@ -300,7 +353,7 @@
 
 def final_add(place, a, b, held, after):
     _, size, width = a.shape
-    steps = 3
+    steps = 2
     block = pl.BlockSpec((2, size // steps, width), lambda i: (0, i, 0))
     return pl.pallas_call(
         add_kernel,
@@ -390,6 +443,7 @@
     for e, pairs in enumerate(exchanges):
         for k, pair in enumerate(pairs):
             put(("send", e, k), theirs(by_role(*pair)))
+    put("blk", blk.astype(jnp.int32))
     put("first mine", mine(first))
     put("first theirs", theirs(first))
     put("first part", column + 1)
@@ -399,7 +453,7 @@
     def columns_of(e):
         return [places["send", e, k] for k in range(len(exchanges[e]))]
 
-    quarter, raw_0 = first_sends(jnp.stack([blk, column]), out_grads, inputs, pre_act, third)
+    quarter, raw_0 = first_sends(blk, column, out_grads, inputs, pre_act, third)
     raw_1, send_0, raw_2, send_1 = cast_blocks(
         table,
         [
@@ -424,9 +478,6 @@
     pair_1, pair_2 = flip(pair_0, 1), flip(pair_0, 2)
     pair_2, pair_1, got[0], raw_1 = tied((pair_2, pair_1, got[0], raw_1))
     pair_3 = flip(pair_2, 1)
-    g, x = join(blk, out_grads, inputs, [pair_0, pair_1, pair_2, pair_3], [got[0], raw_1])
-    last = g
-
     def run(name, partner, **more):
         return piece(scale, table, places[name], pre_act, [partner[0]], partner[1], g, x, w_out, **more)
 
@@ -437,21 +488,36 @@
         sums = [toward[s - 2]] if s >= 2 else []
         held_back = ([across[s - 4]] if s >= 4 else []) + ([first_in] if s == 3 else [])
         j = s - double
-        if j < 0:
-            after = [last] + held_back + ([raw_2] if s == 0 else [])
+        if s == 0:
+            out, g, x, *blocks = first_piece(
+                scale,
+                table,
+                places["main", 0],
+                places["blk"],
+                pre_act,
+                got[0],
+                out_grads,
+                inputs,
+                [pair_0, pair_1, pair_2, pair_3],
+                w_out,
+                sends,
+                [raw_2],
+            )
         else:
-            (last,) = run(
-                ("out", j),
-                partner,
-                sums=[across[j]],
-                other=(got[j], 0) if j < 2 else (got[4], 2),
-                after=[last] + sums + held_back,
+            after = [last] + held_back
+            if j >= 0:
+                (last,) = run(
+                    ("out", j),
+                    partner,
+                    sums=[across[j]],
+                    other=(got[j], 0) if j < 2 else (got[4], 2),
+                    after=after + sums,
+                )
+                toward.append(lax.ppermute(last, "dp", outer_to_inner + inner_to_outer))
+                after = [last] + ([grad_inputs] if j == 0 else [])
+            out, *blocks = run(
+                ("main", s), partner, sums=sums, sends=sends, after=after, flops=FLOPS if s == 3 else 1
             )
-            toward.append(lax.ppermute(last, "dp", outer_to_inner + inner_to_outer))
-            after = [last] + ([grad_inputs] if j == 0 else [])
-        out, *blocks = run(
-            ("main", s), partner, sums=sums, sends=sends, after=after, flops=FLOPS if s == 3 else 1
-        )
         last = out
         if j < 0:
             toward.append(send_in(out))
@@ -466,7 +532,7 @@
             last = input_partial(out_grads, pre_act, w_in, w_out, 4 * size, [last])
             grad_inputs = lax.psum_scatter(last, "blk", scatter_dimension=0, tiled=True)
             grad_inputs = grad_inputs.astype(jnp.bfloat16)
-            line_g, line_x = join(blk, out_grads, inputs, [line_rows], [last])
+            line_g, line_x = join(out_grads, inputs, line_rows, [last])
             (last,) = piece(
                 scale,
                 table,

time: 344 us -> 342 us (level)
  Pallas kernels: 135 us -> 130 us
  waiting for transfers between devices: 148 us -> 152 us
    pallas_call x15 -> x14, Pallas kernels: 91.6 us -> 85.4 us  [piece(): pl.pallas_call(functools.partial(piece_kernel, scale, counts, inner_at),...]
  transfers between devices with their start and end apart: 31 -> 31, of which waited for: 18 -> 18; matrix products, arithmetic and copies ran while one was open for 1% -> 1% of each run, Pallas kernels for 38% -> 37%
where the time goes in v5:
time: 342 us; the launch traced here: 340 us
  waiting for transfers between devices  152 us (44%)
  Pallas kernels  130 us (38%)
  starting transfers between devices  40 us (12%)
  between operations  14.9 us (4%)
    pallas_call x14, Pallas kernels, piece(): pl.pallas_call(functools.partial(piece_kernel, scale, counts, inner_at),...  85.4 us
    ppermute x9, waiting for transfers between devices, send_in(): return lax.ppermute(array, 'dp', outer_to_inner)  54.4 us
    ppermute x8, waiting for transfers between devices, swap(): lax.ppermute(array, 'dp', [(2 * a + h, 2 * a + 1 - h) for a in planes for...  47.5 us
    ppermute x3, waiting for transfers between devices, line_body(): toward.append(lax.ppermute(last, 'dp', outer_to_inner + inner_to_outer))  32.8 us
    ppermute x6, waiting for transfers between devices, line_body(): across[s - 2] = lax.ppermute(out, 'dp', inner_to_inner)  16.9 us
    pallas_call x1, Pallas kernels, input_partial(): pl.pallas_call(input_kernel, grid=(hidden // size,), in_specs=[tokens, pl...  16.4 us
    ppermute x6, starting transfers between devices, line_body(): across[s - 2] = lax.ppermute(out, 'dp', inner_to_inner)  14.5 us
    ppermute x8, starting transfers between devices, swap(): lax.ppermute(array, 'dp', [(2 * a + h, 2 * a + 1 - h) for a in planes for...  12.1 us
  transfers between devices with their start and end apart: 31, of which 18 were waited for; matrix products, arithmetic and copies ran while one was open for 1% of the time, Pallas kernels for 37%

profile of v5, /device:TPU:16, one launch (start us, length us, event | category | flops | bytes accessed | tf_op | source)
XLA Modules:
  0.0 340.2 jit_solution(4593512943269530080)
XLA Ops:
  27.1 7.3 %collective-permute-done.5.refs_1_ = f32[512,256]{1,0:T(8,128)S(1)} collective-permute-done((f32[512,256]{1,0:T(8,128)}, f32[512,256]{1,0:T(8,128)S(1)}, u32[]{:S(2)}, u32[]{:S(2)}) %collective-permute-start.5) | collective-permute-done | bytes 524320 | tf_op jit(solution)/shard_map/ppermute | solution.py:470
  43.3 8.1 %collective-permute-done.7.refs_0_ = f32[512,384]{1,0:T(8,128)} collective-permute-done((f32[512,384]{1,0:T(8,128)}, f32[512,384]{1,0:T(8,128)}, u32[]{:S(2)}, u32[]{:S(2)}) %collective-permute-start.7) | collective-permute-done | bytes 786464 | tf_op jit(solution)/shard_map/ppermute | solution.py:470
  51.5 6.5 %first_piece.1 = (f32[2,384,512]{2,1,0:T(8,128)}, bf16[1024,512]{1,0:T(8,128)(2,1)}, bf16[1024,512]{1,0:T(8,128)(2,1)}, f32[1024,384]{1,0:T(8,128)}) custom-call(s32[31]{0:T(128)} %stack.127.idx_ref.table_ref, bf16[512,9216]{1,0:T(8,128)(2,1)} %own_ref.31, bf16[9216,512]{1,0:T(8,128)(2,1)} %w_ref.31, f32[512,384]{1,0:T(8,128)} %collective-permute-done.4.partner_ref.refs_1_, ...), custom_call_target="tpu_custom_call" | custom-call | flops 1 | bytes 1 | tf_op jit(solution)/shard_map/first_piece/pallas_call | solution.py:280
  71.7 16.4 %input_partial.1.refs_0_.refs_2_ = f32[512,512]{1,0:T(8,128)} custom-call(bf16[512,512]{1,0:T(8,128)(2,1)} %grads_ref.7, bf16[512,9216]{1,0:T(8,128)(2,1)} %own_ref.31, bf16[9216,512]{1,0:T(8,128)(2,1)} %w_ref.31, bf16[9216,512]{1,0:T(8,128)(2,1)} %in_rows_ref.1, f32[2,384,512]{2,1,0:T(8,128)} %piece.14.refs_0_), custom_call_target="tpu_custom_call" | custom-call | flops 99999997952 | bytes 1 | tf_op jit(solution)/shard_map/input_partial/pallas_call | solution.py:162
  99.4 8.4 %collective-permute-done.9.refs_0_ = f32[1024,384]{1,0:T(8,128)} collective-permute-done((f32[1024,384]{1,0:T(8,128)}, f32[1024,384]{1,0:T(8,128)}, u32[]{:S(2)}, u32[]{:S(2)}) %collective-permute-start.9) | collective-permute-done | bytes 1572896 | tf_op jit(solution)/shard_map/ppermute | solution.py:387
  107.8 6.8 %piece.16 = (f32[2,384,512]{2,1,0:T(8,128)}, f32[1024,384]{1,0:T(8,128)}) custom-call(s32[31]{0:T(128)} %stack.127.idx_ref.table_ref, bf16[512,9216]{1,0:T(8,128)(2,1)} %own_ref.31, bf16[1024,512]{1,0:T(8,128)(2,1)} %get-tuple-element.43.g_ref, bf16[1024,512]{1,0:T(8,128)(2,1)} %get-tuple-element.44.x_ref, bf16[9216,512]{1,0:T(8,128)(2,1)} %w_ref.31, ...), custom_call_target="tpu_custom_call" | custom-call | flops 1 | bytes 1 | tf_op jit(solution)/shard_map/piece/pallas_call | solution.py:235
  119.9 11.4 %collective-permute-done.14.refs_1_ = f32[2,384,512]{2,1,0:T(8,128)} collective-permute-done((f32[2,384,512]{2,1,0:T(8,128)}, f32[2,384,512]{2,1,0:T(8,128)}, u32[]{:S(2)}, u32[]{:S(2)}) %collective-permute-start.14) | collective-permute-done | bytes 1572896 | tf_op jit(solution)/shard_map/ppermute | solution.py:470
  131.2 10.3 %collective-permute-done.15.refs_3_.refs_1_ = f32[2,384,512]{2,1,0:T(8,128)} collective-permute-done((f32[2,384,512]{2,1,0:T(8,128)}, f32[2,384,512]{2,1,0:T(8,128)}, u32[]{:S(2)}, u32[]{:S(2)}) %collective-permute-start.15) | collective-permute-done | bytes 1572896 | tf_op jit(solution)/shard_map/ppermute | solution.py:387
  151.3 19.8 %collective-permute-done.12.refs_0_ = f32[1024,384]{1,0:T(8,128)} collective-permute-done((f32[1024,384]{1,0:T(8,128)}, f32[1024,384]{1,0:T(8,128)}, u32[]{:S(2)}, u32[]{:S(2)}) %collective-permute-start.12) | collective-permute-done | bytes 1572896 | tf_op jit(solution)/shard_map/ppermute | solution.py:387
  171.1 7.0 %piece.18 = (f32[2,384,512]{2,1,0:T(8,128)}, f32[1536,384]{1,0:T(8,128)}) custom-call(s32[31]{0:T(128)} %stack.127.idx_ref.table_ref, bf16[512,9216]{1,0:T(8,128)(2,1)} %own_ref.31, bf16[1024,512]{1,0:T(8,128)(2,1)} %get-tuple-element.43.g_ref, bf16[1024,512]{1,0:T(8,128)(2,1)} %get-tuple-element.44.x_ref, bf16[9216,512]{1,0:T(8,128)(2,1)} %w_ref.31, ...), custom_call_target="tpu_custom_call" | custom-call | flops 1 | bytes 1 | tf_op jit(solution)/shard_map/piece/pallas_call | solution.py:235
  190.8 7.8 %collective-permute-done.20.refs_5_.refs_1_ = f32[2,384,512]{2,1,0:T(8,128)} collective-permute-done((f32[2,384,512]{2,1,0:T(8,128)}, f32[2,384,512]{2,1,0:T(8,128)}, u32[]{:S(2)}, u32[]{:S(2)}) %collective-permute-start.20) | collective-permute-done | bytes 1572896 | tf_op jit(solution)/shard_map/ppermute | solution.py:470
  198.7 6.2 %piece.20.refs_2_ = f32[2,384,512]{2,1,0:T(8,128)} custom-call(s32[31]{0:T(128)} %stack.127.idx_ref.table_ref, bf16[512,9216]{1,0:T(8,128)(2,1)} %own_ref.31, bf16[1024,512]{1,0:T(8,128)(2,1)} %get-tuple-element.43.g_ref, bf16[1024,512]{1,0:T(8,128)(2,1)} %get-tuple-element.44.x_ref, bf16[9216,512]{1,0:T(8,128)(2,1)} %w_ref.31, ...), custom_call_target="tpu_custom_call" | custom-call | flops 1 | bytes 1 | tf_op jit(solution)/shard_map/piece/pallas_call | solution.py:235
  204.8 6.0 %piece.21.refs_3_ = f32[2,384,512]{2,1,0:T(8,128)} custom-call(s32[31]{0:T(128)} %stack.127.idx_ref.table_ref, bf16[512,9216]{1,0:T(8,128)(2,1)} %own_ref.31, bf16[1024,512]{1,0:T(8,128)(2,1)} %get-tuple-element.43.g_ref, bf16[1024,512]{1,0:T(8,128)(2,1)} %get-tuple-element.44.x_ref, bf16[9216,512]{1,0:T(8,128)(2,1)} %w_ref.31, ...), custom_call_target="tpu_custom_call" | custom-call | flops 1 | bytes 1 | tf_op jit(solution)/shard_map/piece/pallas_call | solution.py:235
  217.6 14.8 %collective-permute-done.18.refs_5_.refs_3_ = f32[2,384,512]{2,1,0:T(8,128)} collective-permute-done((f32[2,384,512]{2,1,0:T(8,128)}, f32[2,384,512]{2,1,0:T(8,128)}, u32[]{:S(2)}, u32[]{:S(2)}) %collective-permute-start.18) | collective-permute-done | bytes 1572896 | tf_op jit(solution)/shard_map/ppermute | solution.py:470
  232.4 6.2 %piece.22.refs_4_ = f32[2,384,512]{2,1,0:T(8,128)} custom-call(s32[31]{0:T(128)} %stack.127.idx_ref.table_ref, bf16[512,9216]{1,0:T(8,128)(2,1)} %own_ref.31, bf16[1024,512]{1,0:T(8,128)(2,1)} %get-tuple-element.43.g_ref, bf16[1024,512]{1,0:T(8,128)(2,1)} %get-tuple-element.44.x_ref, bf16[9216,512]{1,0:T(8,128)(2,1)} %w_ref.31, ...), custom_call_target="tpu_custom_call" | custom-call | flops 1 | bytes 1 | tf_op jit(solution)/shard_map/piece/pallas_call | solution.py:235
  238.6 6.6 %piece.23 = (f32[2,384,512]{2,1,0:T(8,128)}, f32[1024,384]{1,0:T(8,128)}) custom-call(s32[31]{0:T(128)} %stack.127.idx_ref.table_ref, bf16[512,9216]{1,0:T(8,128)(2,1)} %own_ref.31, bf16[1024,512]{1,0:T(8,128)(2,1)} %get-tuple-element.43.g_ref, bf16[1024,512]{1,0:T(8,128)(2,1)} %get-tuple-element.44.x_ref, bf16[9216,512]{1,0:T(8,128)(2,1)} %w_ref.31, ...), custom_call_target="tpu_custom_call" | custom-call | flops 1 | bytes 1 | tf_op jit(solution)/shard_map/piece/pallas_call | solution.py:235
  249.4 16.7 %collective-permute-done.23.refs_5_.refs_1_.outer_ref = f32[2,384,512]{2,1,0:T(8,128)} collective-permute-done((f32[2,384,512]{2,1,0:T(8,128)}, f32[2,384,512]{2,1,0:T(8,128)}, u32[]{:S(2)}, u32[]{:S(2)}) %collective-permute-start.23) | collective-permute-done | bytes 1572896 | tf_op jit(solution)/shard_map/ppermute | solution.py:516
  266.1 6.2 %piece.24.refs_2_ = f32[2,384,512]{2,1,0:T(8,128)} custom-call(s32[31]{0:T(128)} %stack.127.idx_ref.table_ref, bf16[512,9216]{1,0:T(8,128)(2,1)} %own_ref.31, bf16[1024,512]{1,0:T(8,128)(2,1)} %get-tuple-element.43.g_ref, bf16[1024,512]{1,0:T(8,128)(2,1)} %get-tuple-element.44.x_ref, bf16[9216,512]{1,0:T(8,128)(2,1)} %w_ref.31, ...), custom_call_target="tpu_custom_call" | custom-call | flops 1 | bytes 1 | tf_op jit(solution)/shard_map/piece/pallas_call | solution.py:235
  272.2 6.0 %piece.25.refs_1_ = f32[2,384,512]{2,1,0:T(8,128)} custom-call(s32[31]{0:T(128)} %stack.127.idx_ref.table_ref, bf16[512,9216]{1,0:T(8,128)(2,1)} %own_ref.31, bf16[1024,512]{1,0:T(8,128)(2,1)} %get-tuple-element.43.g_ref, bf16[1024,512]{1,0:T(8,128)(2,1)} %get-tuple-element.44.x_ref, bf16[9216,512]{1,0:T(8,128)(2,1)} %w_ref.31, ...), custom_call_target="tpu_custom_call" | custom-call | flops 1 | bytes 1 | tf_op jit(solution)/shard_map/piece/pallas_call | solution.py:235
  280.9 6.6 %final_first.1 = (f32[1152,512]{1,0:T(8,128)}, f32[1152,512]{1,0:T(8,128)}) custom-call(s32[31]{0:T(128)} %stack.127.idx_ref.table_ref, bf16[512,9216]{1,0:T(8,128)(2,1)} %own_ref.31, bf16[1024,512]{1,0:T(8,128)(2,1)} %get-tuple-element.43.g_ref, bf16[1024,512]{1,0:T(8,128)(2,1)} %get-tuple-element.44.x_ref, bf16[9216,512]{1,0:T(8,128)(2,1)} %w_ref.31, ...), custom_call_target="tpu_custom_call" | custom-call | flops 1 | bytes 1 | tf_op jit(solution)/shard_map/final_first/pallas_call | solution.py:330
  293.4 6.4 %collective-permute-done.27.b_ref = f32[2,384,512]{2,1,0:T(8,128)} collective-permute-done((f32[2,384,512]{2,1,0:T(8,128)}, f32[2,384,512]{2,1,0:T(8,128)}, u32[]{:S(2)}, u32[]{:S(2)}) %collective-permute-start.27) | collective-permute-done | bytes 1572896 | tf_op jit(solution)/shard_map/ppermute | solution.py:516
  302.6 12.3 %collective-permute-done.25.refs_1_ = f32[2,384,512]{2,1,0:T(8,128)} collective-permute-done((f32[2,384,512]{2,1,0:T(8,128)}, f32[2,384,512]{2,1,0:T(8,128)}, u32[]{:S(2)}, u32[]{:S(2)}) %collective-permute-start.25) | collective-permute-done | bytes 1572896 | tf_op jit(solution)/shard_map/ppermute | solution.py:527
  314.9 6.0 %piece.27.a_ref = f32[2,384,512]{2,1,0:T(8,128)} custom-call(s32[31]{0:T(128)} %stack.127.idx_ref.table_ref, bf16[512,9216]{1,0:T(8,128)(2,1)} %own_ref.31, bf16[1024,512]{1,0:T(8,128)(2,1)} %get-tuple-element.43.g_ref, bf16[1024,512]{1,0:T(8,128)(2,1)} %get-tuple-element.44.x_ref, bf16[9216,512]{1,0:T(8,128)(2,1)} %w_ref.31, ...), custom_call_target="tpu_custom_call" | custom-call | flops 1 | bytes 1 | tf_op jit(solution)/shard_map/piece/pallas_call | solution.py:235
  320.9 9.7 %collective-permute-done.28.b_ref = f32[2,384,512]{2,1,0:T(8,128)} collective-permute-done((f32[2,384,512]{2,1,0:T(8,128)}, f32[2,384,512]{2,1,0:T(8,128)}, u32[]{:S(2)}, u32[]{:S(2)}) %collective-permute-start.28) | collective-permute-done | bytes 1572896 | tf_op jit(solution)/shard_map/ppermute | solution.py:516
  (72 shorter events, 105.8 us)
Async XLA Ops:
  7.2 80.9 %all-gather.2.cloned.1.call-start = ((), (), s32[]{:S(2)}) async-start(), calls=%async_computation.2 | async-start | bytes 2621440 | tf_op jit(solution)/shard_map/all_gather | solution.py:530
  17.0 24.2 %collective-permute-start.4 = (f32[512,384]{1,0:T(8,128)}, f32[512,384]{1,0:T(8,128)}, u32[]{:S(2)}, u32[]{:S(2)}) collective-permute-start(f32[512,384]{1,0:T(8,128)} %get-tuple-element.37), channel_id=1, source_target_pairs={{0,4},{4,0},{8,12},{12,8},{16,20},{20,16},{24,28},{28,24},{1,5},{5... | collective-permute-start | bytes 2359304 | tf_op jit(solution)/shard_map/ppermute | solution.py:387
  25.9 25.6 %collective-permute-start.7 = (f32[512,384]{1,0:T(8,128)}, f32[512,384]{1,0:T(8,128)}, u32[]{:S(2)}, u32[]{:S(2)}) collective-permute-start(f32[512,384]{1,0:T(8,128)} %get-tuple-element.42), channel_id=1, source_target_pairs={{0,8},{4,12},{24,16},{28,20},{1,9},{5,13},{25,17},{29,21},{2,10},{... | collective-permute-start | bytes 2359304 | tf_op jit(solution)/shard_map/ppermute | solution.py:470
  34.5 28.0 %collective-permute-start.8 = (f32[512,384]{1,0:T(8,128)}, f32[512,384]{1,0:T(8,128)S(1)}, u32[]{:S(2)}, u32[]{:S(2)}) collective-permute-start(f32[512,384]{1,0:T(8,128)} %get-tuple-element.45), channel_id=1, source_target_pairs={{0,4},{4,0},{8,12},{12,8},{16,20},{20,16},{24,28},{28,24},{1,5},{5... | collective-permute-start | bytes 2359304 | tf_op jit(solution)/shard_map/ppermute | solution.py:387
  58.0 49.8 %collective-permute-start.10 = (f32[2,384,512]{2,1,0:T(8,128)}, f32[2,384,512]{2,1,0:T(8,128)}, u32[]{:S(2)}, u32[]{:S(2)}) collective-permute-start(f32[2,384,512]{2,1,0:T(8,128)} %get-tuple-element.46.refs_1_), channel_id=1, source_target_pairs={{0,8},{4,12},{24,16},{28,20},{1,9},{5,13},{25,17},{29,21},{2,10},{... | collective-permute-start | bytes 4718600 | tf_op jit(solution)/shard_map/ppermute | solution.py:470
  62.4 120.9 %reduce-scatter.2.cloned.1.call-start = ((), (), s32[]{:S(2)}) async-start(), calls=%async_computation.1 | async-start | bytes 1310720 | tf_op jit(solution)/shard_map/reduce_scatter | solution.py:533
  68.8 62.4 %collective-permute-start.14 = (f32[2,384,512]{2,1,0:T(8,128)}, f32[2,384,512]{2,1,0:T(8,128)}, u32[]{:S(2)}, u32[]{:S(2)}) collective-permute-start(f32[2,384,512]{2,1,0:T(8,128)} %piece.14.refs_0_), channel_id=1, source_target_pairs={{0,8},{4,12},{24,16},{28,20},{1,9},{5,13},{25,17},{29,21},{2,10},{... | collective-permute-start | bytes 4718600 | tf_op jit(solution)/shard_map/ppermute | solution.py:470
  70.1 37.7 %collective-permute-start.9 = (f32[1024,384]{1,0:T(8,128)}, f32[1024,384]{1,0:T(8,128)}, u32[]{:S(2)}, u32[]{:S(2)}) collective-permute-start(f32[1024,384]{1,0:T(8,128)} %get-tuple-element.47), channel_id=1, source_target_pairs={{0,4},{4,0},{8,12},{12,8},{16,20},{20,16},{24,28},{28,24},{1,5},{5... | collective-permute-start | bytes 4718600 | tf_op jit(solution)/shard_map/ppermute | solution.py:387
  96.9 44.6 %collective-permute-start.15 = (f32[2,384,512]{2,1,0:T(8,128)}, f32[2,384,512]{2,1,0:T(8,128)}, u32[]{:S(2)}, u32[]{:S(2)}) collective-permute-start(f32[2,384,512]{2,1,0:T(8,128)} %piece.15.refs_4_), channel_id=1, source_target_pairs={{8,12},{12,8},{16,20},{20,16},{9,13},{13,9},{17,21},{21,17},{10,14... | collective-permute-start | bytes 4718600 | tf_op jit(solution)/shard_map/ppermute | solution.py:387
  114.6 56.5 %collective-permute-start.16 = (f32[2,384,512]{2,1,0:T(8,128)}, f32[2,384,512]{2,1,0:T(8,128)}, u32[]{:S(2)}, u32[]{:S(2)}) collective-permute-start(f32[2,384,512]{2,1,0:T(8,128)} %get-tuple-element.54.refs_2_), channel_id=1, source_target_pairs={{8,16},{12,20},{16,8},{20,12},{9,17},{13,21},{17,9},{21,13},{10,18... | collective-permute-start | bytes 4718600 | tf_op jit(solution)/shard_map/ppermute | solution.py:527
  117.0 54.1 %collective-permute-start.13 = (f32[2,384,512]{2,1,0:T(8,128)}, f32[2,384,512]{2,1,0:T(8,128)}, u32[]{:S(2)}, u32[]{:S(2)}) collective-permute-start(f32[2,384,512]{2,1,0:T(8,128)} %get-tuple-element.54.refs_2_), channel_id=1, source_target_pairs={{0,8},{4,12},{24,16},{28,20},{1,9},{5,13},{25,17},{29,21},{2,10},{... | collective-permute-start | bytes 4718600 | tf_op jit(solution)/shard_map/ppermute | solution.py:470
  118.3 52.8 %collective-permute-start.12 = (f32[1024,384]{1,0:T(8,128)}, f32[1024,384]{1,0:T(8,128)}, u32[]{:S(2)}, u32[]{:S(2)}) collective-permute-start(f32[1024,384]{1,0:T(8,128)} %get-tuple-element.53), channel_id=1, source_target_pairs={{0,4},{4,0},{8,12},{12,8},{16,20},{20,16},{24,28},{28,24},{1,5},{5... | collective-permute-start | bytes 4718600 | tf_op jit(solution)/shard_map/ppermute | solution.py:387
  147.5 51.2 %collective-permute-start.20 = (f32[2,384,512]{2,1,0:T(8,128)}, f32[2,384,512]{2,1,0:T(8,128)}, u32[]{:S(2)}, u32[]{:S(2)}) collective-permute-start(f32[2,384,512]{2,1,0:T(8,128)} %piece.17.refs_5_), channel_id=1, source_target_pairs={{0,8},{4,12},{24,16},{28,20},{1,9},{5,13},{25,17},{29,21},{2,10},{... | collective-permute-start | bytes 4718600 | tf_op jit(solution)/shard_map/ppermute | solution.py:470
  148.8 49.9 %collective-permute-start.19 = (f32[2,384,512]{2,1,0:T(8,128)}, f32[2,384,512]{2,1,0:T(8,128)}, u32[]{:S(2)}, u32[]{:S(2)}) collective-permute-start(f32[2,384,512]{2,1,0:T(8,128)} %piece.17.refs_5_), channel_id=1, source_target_pairs={{8,16},{12,20},{16,8},{20,12},{9,17},{13,21},{17,9},{21,13},{10,18... | collective-permute-start | bytes 4718600 | tf_op jit(solution)/shard_map/ppermute | solution.py:527
  178.1 54.3 %collective-permute-start.17 = (f32[1536,384]{1,0:T(8,128)}, f32[1536,384]{1,0:T(8,128)}, u32[]{:S(2)}, u32[]{:S(2)}) collective-permute-start(f32[1536,384]{1,0:T(8,128)} %get-tuple-element.55), channel_id=1, source_target_pairs={{0,4},{4,0},{8,12},{12,8},{16,20},{20,16},{24,28},{28,24},{1,5},{5... | collective-permute-start | bytes 7077896 | tf_op jit(solution)/shard_map/ppermute | solution.py:387
  179.6 38.0 %collective-permute-start.21 = (f32[2,384,512]{2,1,0:T(8,128)}, f32[2,384,512]{2,1,0:T(8,128)}, u32[]{:S(2)}, u32[]{:S(2)}) collective-permute-start(f32[2,384,512]{2,1,0:T(8,128)} %get-tuple-element.56.refs_2_), channel_id=1, source_target_pairs={{8,16},{12,20},{16,8},{20,12},{9,17},{13,21},{17,9},{21,13},{10,18... | collective-permute-start | bytes 4718600 | tf_op jit(solution)/shard_map/ppermute | solution.py:527
  182.0 50.4 %collective-permute-start.18 = (f32[2,384,512]{2,1,0:T(8,128)}, f32[2,384,512]{2,1,0:T(8,128)}, u32[]{:S(2)}, u32[]{:S(2)}) collective-permute-start(f32[2,384,512]{2,1,0:T(8,128)} %get-tuple-element.56.refs_2_), channel_id=1, source_target_pairs={{0,8},{4,12},{24,16},{28,20},{1,9},{5,13},{25,17},{29,21},{2,10},{... | collective-permute-start | bytes 4718600 | tf_op jit(solution)/shard_map/ppermute | solution.py:470
  210.8 38.6 %collective-permute-start.24 = (f32[2,384,512]{2,1,0:T(8,128)}, f32[2,384,512]{2,1,0:T(8,128)}, u32[]{:S(2)}, u32[]{:S(2)}) collective-permute-start(f32[2,384,512]{2,1,0:T(8,128)} %piece.21.refs_3_), channel_id=1, source_target_pairs={{8,16},{12,20},{16,8},{20,12},{9,17},{13,21},{17,9},{21,13},{10,18... | collective-permute-start | bytes 4718600 | tf_op jit(solution)/shard_map/ppermute | solution.py:527
  213.2 52.9 %collective-permute-start.23 = (f32[2,384,512]{2,1,0:T(8,128)}, f32[2,384,512]{2,1,0:T(8,128)}, u32[]{:S(2)}, u32[]{:S(2)}) collective-permute-start(f32[2,384,512]{2,1,0:T(8,128)} %piece.20.refs_2_), channel_id=1, source_target_pairs={{0,8},{4,12},{24,16},{28,20},{8,0},{12,4},{16,24},{20,28},{1,9},{5... | collective-permute-start | bytes 4718600 | tf_op jit(solution)/shard_map/ppermute | solution.py:516
  245.2 42.2 %collective-permute-start.22 = (f32[1024,384]{1,0:T(8,128)}, f32[1024,384]{1,0:T(8,128)}, u32[]{:S(2)}, u32[]{:S(2)}) collective-permute-start(f32[1024,384]{1,0:T(8,128)} %get-tuple-element.57), channel_id=1, source_target_pairs={{0,4},{4,0},{8,12},{12,8},{16,20},{20,16},{24,28},{28,24},{1,5},{5... | collective-permute-start | bytes 4718600 | tf_op jit(solution)/shard_map/ppermute | solution.py:387
  246.7 40.7 %collective-permute-start.26 = (f32[2,384,512]{2,1,0:T(8,128)}, f32[2,384,512]{2,1,0:T(8,128)}, u32[]{:S(2)}, u32[]{:S(2)}) collective-permute-start(f32[2,384,512]{2,1,0:T(8,128)} %get-tuple-element.58.refs_3_), channel_id=1, source_target_pairs={{8,16},{12,20},{16,8},{20,12},{9,17},{13,21},{17,9},{21,13},{10,18... | collective-permute-start | bytes 4718600 | tf_op jit(solution)/shard_map/ppermute | solution.py:527
  249.1 50.7 %collective-permute-start.27 = (f32[2,384,512]{2,1,0:T(8,128)}, f32[2,384,512]{2,1,0:T(8,128)}, u32[]{:S(2)}, u32[]{:S(2)}) collective-permute-start(f32[2,384,512]{2,1,0:T(8,128)} %piece.22.refs_4_), channel_id=1, source_target_pairs={{0,8},{4,12},{24,16},{28,20},{8,0},{12,4},{16,24},{20,28},{1,9},{5... | collective-permute-start | bytes 4718600 | tf_op jit(solution)/shard_map/ppermute | solution.py:516
  278.2 36.7 %collective-permute-start.25 = (f32[2,384,512]{2,1,0:T(8,128)}, f32[2,384,512]{2,1,0:T(8,128)}, u32[]{:S(2)}, u32[]{:S(2)}) collective-permute-start(f32[2,384,512]{2,1,0:T(8,128)} %piece.25.refs_1_), channel_id=1, source_target_pairs={{8,16},{12,20},{16,8},{20,12},{9,17},{13,21},{17,9},{21,13},{10,18... | collective-permute-start | bytes 4718600 | tf_op jit(solution)/shard_map/ppermute | solution.py:527
  280.8 49.8 %collective-permute-start.28 = (f32[2,384,512]{2,1,0:T(8,128)}, f32[2,384,512]{2,1,0:T(8,128)}, u32[]{:S(2)}, u32[]{:S(2)}) collective-permute-start(f32[2,384,512]{2,1,0:T(8,128)} %piece.24.refs_2_), channel_id=1, source_target_pairs={{0,8},{4,12},{24,16},{28,20},{8,0},{12,4},{16,24},{20,28},{1,9},{5... | collective-permute-start | bytes 4718600 | tf_op jit(solution)/shard_map/ppermute | solution.py:516
  (11 other events, 128.7 us)
Sparse Core Ops, SparseCore 0:
  62.6 22.7 all-gather.1
  99.5 26.5 reduce-scatter.1

commit v6 on v5

--- a/solution.py
+++ b/solution.py
@@ -116,35 +116,39 @@
     )(blk.reshape(1), column.reshape(1), out_grads, inputs, pre_act)
 
 
-def join_kernel(grads_ref, inputs_ref, line_ref, *refs):
-    g_ref, x_ref = refs[-2:]
+def fill_tokens(blk, grads_ref, inputs_ref, quarters, g_ref, x_ref):
     rows = grads_ref.shape[0]
     quarter = rows // 4
     g_ref[:rows, :] = grads_ref[...]
     x_ref[:rows, :] = inputs_ref[...]
-    for k in range(4):
-        place, start = pl.ds(rows + k * quarter, quarter), 2 * k * quarter
-        g_ref[place, :] = line_ref[start : start + quarter, :].astype(jnp.bfloat16)
-        x_ref[place, :] = line_ref[start + quarter : start + 2 * quarter, :].astype(jnp.bfloat16)
-
-
-def join(out_grads, inputs, line_rows, after):
+    for k, ref in enumerate(quarters):
+        where = jnp.bitwise_xor(blk, k)
+        place = pl.ds(pl.multiple_of(rows + where * quarter, quarter), quarter)
+        g_ref[place, :] = ref[:quarter, :].astype(jnp.bfloat16)
+        x_ref[place, :] = ref[quarter:, :].astype(jnp.bfloat16)
+
+
+def join_kernel(blk_ref, grads_ref, inputs_ref, *refs):
+    fill_tokens(blk_ref[0], grads_ref, inputs_ref, refs[:4], *refs[-2:])
+
+
+def join(blk, out_grads, inputs, quarters, after):
     rows, width = out_grads.shape
     shape = jax.ShapeDtypeStruct((2 * rows, width), jnp.bfloat16)
     vmem = pl.BlockSpec(memory_space=pltpu.VMEM)
     return pl.pallas_call(
         join_kernel,
         out_shape=(shape, shape),
-        in_specs=[vmem] * 3 + anywhere(after),
+        in_specs=[pl.BlockSpec(memory_space=pltpu.SMEM)] + [vmem] * 6 + anywhere(after),
         out_specs=(vmem, vmem),
         compiler_params=params(),
         cost_estimate=piece_cost(),
         name="join_tokens",
-    )(out_grads, inputs, line_rows, *after)
-
-
-def input_kernel(grads_ref, pre_ref, out_rows_ref, in_rows_ref, *refs):
-    total_ref = refs[-1]
+    )(blk.reshape(1), out_grads, inputs, *quarters, *after)
+
+
+def input_kernel(blk_ref, grads_ref, pre_ref, out_rows_ref, in_rows_ref, *refs):
+    keep_ref, give_ref, total_ref = refs[-3:]
 
     @pl.when(pl.program_id(0) == 0)
     def _():
@@ -153,22 +157,76 @@
     hidden = hidden_grads(grads_ref[...], pre_ref[...], out_rows_ref[...])
     total_ref[...] += jnp.dot(hidden, in_rows_ref[...], preferred_element_type=jnp.float32)
 
-
-def input_partial(out_grads, pre_act, w_in, w_out, size, after):
+    @pl.when(pl.program_id(0) == pl.num_programs(0) - 1)
+    def _():
+        half = keep_ref.shape[0]
+        x = blk_ref[0] // 2
+        keep_ref[...] = total_ref[pl.ds(pl.multiple_of(x * half, half), half), :]
+        give_ref[...] = total_ref[pl.ds(pl.multiple_of((1 - x) * half, half), half), :]
+
+
+def input_partial(blk, out_grads, pre_act, w_in, w_out, size, after):
     rows, hidden = pre_act.shape
     width = out_grads.shape[1]
-    tokens = pl.BlockSpec((rows, width), lambda i: (0, 0))
-    weights = pl.BlockSpec((size, width), lambda i: (i, 0))
+    tokens = pl.BlockSpec((rows, width), lambda i, blk: (0, 0))
+    weights = pl.BlockSpec((size, width), lambda i, blk: (i, 0))
+    half = jax.ShapeDtypeStruct((rows // 2, width), jnp.float32)
     return pl.pallas_call(
         input_kernel,
-        grid=(hidden // size,),
-        in_specs=[tokens, pl.BlockSpec((rows, size), lambda i: (0, i)), weights, weights] + anywhere(after),
-        out_specs=tokens,
-        out_shape=jax.ShapeDtypeStruct((rows, width), jnp.float32),
+        grid_spec=pltpu.PrefetchScalarGridSpec(
+            num_scalar_prefetch=1,
+            grid=(hidden // size,),
+            in_specs=[tokens, pl.BlockSpec((rows, size), lambda i, blk: (0, i)), weights, weights]
+            + anywhere(after),
+            out_specs=[pl.BlockSpec(half.shape, lambda i, blk: (0, 0))] * 2,
+            scratch_shapes=[pltpu.VMEM((rows, width), jnp.float32)],
+        ),
+        out_shape=[half, half],
         compiler_params=params(),
         cost_estimate=piece_cost(FLOPS),
         name="input_partial",
-    )(out_grads, pre_act, w_out, w_in, *after)
+    )(blk.reshape(1), out_grads, pre_act, w_out, w_in, *after)
+
+
+def fold_kernel(blk_ref, kept_ref, got_ref, *refs):
+    keep_ref, give_ref = refs[-2:]
+    rows = keep_ref.shape[0]
+    core = blk_ref[0] % 2
+    for ref, place in ((keep_ref, core), (give_ref, 1 - core)):
+        part = pl.ds(pl.multiple_of(place * rows, rows), rows)
+        ref[...] = kept_ref[part, :] + got_ref[part, :]
+
+
+def fold(blk, kept, got, after):
+    rows, width = kept.shape
+    half = jax.ShapeDtypeStruct((rows // 2, width), jnp.float32)
+    vmem = pl.BlockSpec(memory_space=pltpu.VMEM)
+    return pl.pallas_call(
+        fold_kernel,
+        out_shape=(half, half),
+        in_specs=[pl.BlockSpec(memory_space=pltpu.SMEM), vmem, vmem] + anywhere(after),
+        out_specs=(vmem, vmem),
+        compiler_params=params(),
+        cost_estimate=piece_cost(),
+        name="fold_rows",
+    )(blk.reshape(1), kept, got, *after)
+
+
+def round_kernel(kept_ref, got_ref, *refs):
+    refs[-1][...] = (kept_ref[...] + got_ref[...]).astype(jnp.bfloat16)
+
+
+def round_sum(kept, got, after):
+    vmem = pl.BlockSpec(memory_space=pltpu.VMEM)
+    return pl.pallas_call(
+        round_kernel,
+        out_shape=jax.ShapeDtypeStruct(kept.shape, jnp.bfloat16),
+        in_specs=[vmem, vmem] + anywhere(after),
+        out_specs=vmem,
+        compiler_params=params(),
+        cost_estimate=piece_cost(),
+        name="round_sum",
+    )(kept, got, *after)
 
 
 def piece_math(scale, own, partner, g, x, w):
@@ -257,14 +315,8 @@
 ):
     out_ref, g_ref, x_ref, send_ref = refs[-4:]
     rows = grads_ref.shape[0]
-    quarter = rows // 4
-    g_ref[:rows, :] = grads_ref[...]
-    x_ref[:rows, :] = inputs_ref[...]
-    for k, ref in enumerate((q0_ref, q1_ref, q2_ref, q3_ref)):
-        where = jnp.bitwise_xor(table_ref[blk_at], k)
-        place = pl.ds(pl.multiple_of(rows + where * quarter, quarter), quarter)
-        g_ref[place, :] = ref[:quarter, :].astype(jnp.bfloat16)
-        x_ref[place, :] = ref[quarter:, :].astype(jnp.bfloat16)
+    quarters = (q0_ref, q1_ref, q2_ref, q3_ref)
+    fill_tokens(table_ref[blk_at], grads_ref, inputs_ref, quarters, g_ref, x_ref)
     out_ref[0], out_ref[1] = piece_math(
         scale, own_ref[...], partner_ref[...], g_ref[...], x_ref[...], w_ref[...]
     )
@@ -504,7 +556,7 @@
                 [raw_2],
             )
         else:
-            after = [last] + held_back
+            after = [last] + held_back + ([quarter_in] if s == 1 else [])
             if j >= 0:
                 (last,) = run(
                     ("out", j),
@@ -514,9 +566,9 @@
                     after=after + sums,
                 )
                 toward.append(lax.ppermute(last, "dp", outer_to_inner + inner_to_outer))
-                after = [last] + ([grad_inputs] if j == 0 else [])
+                after = [last]
             out, *blocks = run(
-                ("main", s), partner, sums=sums, sends=sends, after=after, flops=FLOPS if s == 3 else 1
+                ("main", s), partner, sums=sums, sends=sends, after=after, flops=FLOPS
             )
         last = out
         if j < 0:
@@ -526,13 +578,11 @@
         if s >= 2:
             across[s - 2] = lax.ppermute(out, "dp", inner_to_inner)
         if s == 0:
-            out, quarter_in = tied((out, quarter_in))
-            line_rows = lax.all_gather(quarter_in, "blk", tiled=True)
+            line_quarter = tied((quarter_in, out))[0]
         if s == 1:
-            last = input_partial(out_grads, pre_act, w_in, w_out, 4 * size, [last])
-            grad_inputs = lax.psum_scatter(last, "blk", scatter_dimension=0, tiled=True)
-            grad_inputs = grad_inputs.astype(jnp.bfloat16)
-            line_g, line_x = join(out_grads, inputs, line_rows, [last])
+            in_1, in_2 = flip(line_quarter, 1), flip(line_quarter, 2)
+            in_3 = flip(in_2, 1)
+            line_g, line_x = join(blk, out_grads, inputs, [line_quarter, in_1, in_2, in_3], [last])
             (last,) = piece(
                 scale,
                 table,
@@ -546,6 +596,8 @@
                 after=[last],
             )
             first_in = swap(last, inner_planes)
+            rows_kept, last = input_partial(blk, out_grads, pre_act, w_in, w_out, 4 * size, [last, got[2]])
+            rows_given = last
         if s == 4:
             (held_in,) = piece(
                 scale,
@@ -562,6 +614,7 @@
             )
             last = held_in
 
+    rows_got = flip(tied((rows_given, last))[0], 2)
     held = final_first(
         scale,
         count,
@@ -579,9 +632,17 @@
         across[count],
         [last],
     )
+    last = held[0]
     for i in range(1, count):
-        (out,) = run(("own", i), (got[5], i - 1), sums=[across[count + i]], after=[held[0]])
-        held = final_add(i, out, toward[double + i], held, [])
+        (out,) = run(("own", i), (got[5], i - 1), sums=[across[count + i]], after=[last])
+        if i == 1:
+            rows_kept, rows_given = fold(blk, rows_kept, rows_got, [out])
+            rows_got = flip(rows_given, 1)
+            held = final_add(i, out, toward[double + i], held, [rows_given])
+            grad_inputs = round_sum(rows_kept, rows_got, [held[0]])
+            last = grad_inputs
+        else:
+            held = final_add(i, out, toward[double + i], held, [])
     return (grad_inputs, held[0], held[1])
 
 

time: 342 us -> 335 us (0.980)
  between operations: 14.9 us -> 1.54 us
    ppermute x3, waiting for transfers between devices: 32.8 us -> 6.16 us  [line_body(): toward.append(lax.ppermute(last, 'dp', outer_to_inner + inner_to_outer))]
    ppermute x6, waiting for transfers between devices: 16.9 us -> 35.8 us  [line_body(): across[s - 2] = lax.ppermute(out, 'dp', inner_to_inner)]
    ppermute x3 -> x8, waiting for transfers between devices: 0.01 us -> 8.04 us  [flip(): return lax.ppermute(array, 'blk', [(i, i ^ bit) for i in range(4)])]
    ppermute x9, waiting for transfers between devices: 54.4 us -> 61.2 us  [send_in(): return lax.ppermute(array, 'dp', outer_to_inner)]
    ppermute x8, waiting for transfers between devices: 47.5 us -> 41.7 us  [swap(): lax.ppermute(array, 'dp', [(2 * a + h, 2 * a + 1 - h) for a in planes for...]
    pallas_call x2 -> x4, Pallas kernels: 19.8 us -> 23.5 us  [the longest x1 16.4 us: input_partial(): pl.pallas_call(input_kernel, grid_spec=pltpu.PrefetchScalarGridSpec(num_s...]
  transfers between devices with their start and end apart: 31 -> 34, of which waited for: 18 -> 19; matrix products, arithmetic and copies ran while one was open for 1% -> 0% of each run, Pallas kernels for 37% -> 38%
where the time goes in v6:
time: 335 us; the launch traced here: 334 us
  waiting for transfers between devices  153 us (46%)
  Pallas kernels  133 us (40%)
  starting transfers between devices  43 us (13%)
    pallas_call x14, Pallas kernels, piece(): pl.pallas_call(functools.partial(piece_kernel, scale, counts, inner_at),...  85 us
    ppermute x9, waiting for transfers between devices, send_in(): return lax.ppermute(array, 'dp', outer_to_inner)  61.2 us
    ppermute x8, waiting for transfers between devices, swap(): lax.ppermute(array, 'dp', [(2 * a + h, 2 * a + 1 - h) for a in planes for...  41.7 us
    ppermute x6, waiting for transfers between devices, line_body(): across[s - 2] = lax.ppermute(out, 'dp', inner_to_inner)  35.8 us
    pallas_call x1, Pallas kernels, input_partial(): pl.pallas_call(input_kernel, grid_spec=pltpu.PrefetchScalarGridSpec(num_s...  16.4 us
    ppermute x6, starting transfers between devices, line_body(): across[s - 2] = lax.ppermute(out, 'dp', inner_to_inner)  14.5 us
    ppermute x8, starting transfers between devices, swap(): lax.ppermute(array, 'dp', [(2 * a + h, 2 * a + 1 - h) for a in planes for...  13.3 us
    ppermute x9, starting transfers between devices, send_in(): return lax.ppermute(array, 'dp', outer_to_inner)  11.5 us
  transfers between devices with their start and end apart: 34, of which 19 were waited for; matrix products, arithmetic and copies ran while one was open for 0% of the time, Pallas kernels for 38%

profile of v6, /device:TPU:16, one launch (start us, length us, event | category | flops | bytes accessed | tf_op | source)
XLA Modules:
  0.0 333.5 jit_solution(5021494543881912114)
XLA Ops:
  20.6 7.3 %collective-permute-done.6.refs_1_ = f32[512,256]{1,0:T(8,128)S(1)} collective-permute-done((f32[512,256]{1,0:T(8,128)}, f32[512,256]{1,0:T(8,128)S(1)}, u32[]{:S(2)}, u32[]{:S(2)}) %collective-permute-start.6) | collective-permute-done | bytes 524320 | tf_op jit(solution)/shard_map/ppermute | solution.py:522
  36.4 8.3 %collective-permute-done.8.refs_0_ = f32[512,384]{1,0:T(8,128)S(1)} collective-permute-done((f32[512,384]{1,0:T(8,128)}, f32[512,384]{1,0:T(8,128)S(1)}, u32[]{:S(2)}, u32[]{:S(2)}) %collective-permute-start.8) | collective-permute-done | bytes 786464 | tf_op jit(solution)/shard_map/ppermute | solution.py:522
  45.6 6.5 %first_piece.1 = (f32[2,384,512]{2,1,0:T(8,128)}, bf16[1024,512]{1,0:T(8,128)(2,1)}, bf16[1024,512]{1,0:T(8,128)(2,1)}, f32[1024,384]{1,0:T(8,128)}) custom-call(s32[31]{0:T(128)} %stack.124.idx_ref.table_ref, bf16[512,9216]{1,0:T(8,128)(2,1)} %own_ref.31, bf16[9216,512]{1,0:T(8,128)(2,1)} %w_ref.31, f32[512,384]{1,0:T(8,128)} %copy-done.1, ...), custom_call_target="tpu_custom_call" | custom-call | flops 1 | bytes 1 | tf_op jit(solution)/shard_map/first_piece/pallas_call | solution.py:332
  58.7 8.0 %collective-permute-done.10.refs_2_ = f32[256,512]{1,0:T(8,128)S(1)} collective-permute-done((f32[256,512]{1,0:T(8,128)}, f32[256,512]{1,0:T(8,128)S(1)}, u32[]{:S(2)}, u32[]{:S(2)}) %collective-permute-start.10) | collective-permute-done | bytes 524320 | tf_op jit(solution)/shard_map/ppermute | solution.py:442
  85.6 9.0 %collective-permute-done.13.refs_1_.refs_0_ = f32[1024,384]{1,0:T(8,128)} collective-permute-done((f32[1024,384]{1,0:T(8,128)}, f32[1024,384]{1,0:T(8,128)}, u32[]{:S(2)}, u32[]{:S(2)}) %collective-permute-start.13) | collective-permute-done | bytes 1572896 | tf_op jit(solution)/shard_map/ppermute | solution.py:439
  94.7 16.4 %input_partial.1 = (f32[256,512]{1,0:T(8,128)}, f32[256,512]{1,0:T(8,128)}) custom-call(s32[1]{0:T(128)} %bitcast.blk_ref, bf16[512,512]{1,0:T(8,128)(2,1)} %grads_ref.7, bf16[512,9216]{1,0:T(8,128)(2,1)} %own_ref.31, bf16[9216,512]{1,0:T(8,128)(2,1)} %w_ref.31, bf16[9216,512]{1,0:T(8,128)(2,1)} %in_rows_ref.1, f32[2,384,512]{2,1,0:T(8,128)} %piece.15.refs_0_, ...), custom_call_target="tpu_custom_call" | custom-call | flops 99999997952 | bytes 1 | tf_op jit(solution)/shard_map/input_partial/pallas_call | solution.py:174
  111.1 6.6 %piece.16 = (f32[2,384,512]{2,1,0:T(8,128)}, f32[1024,384]{1,0:T(8,128)}) custom-call(s32[31]{0:T(128)} %stack.124.idx_ref.table_ref, bf16[512,9216]{1,0:T(8,128)(2,1)} %own_ref.31, bf16[1024,512]{1,0:T(8,128)(2,1)} %get-tuple-element.50.g_ref, bf16[1024,512]{1,0:T(8,128)(2,1)} %get-tuple-element.51.x_ref, bf16[9216,512]{1,0:T(8,128)(2,1)} %w_ref.31, ...), custom_call_target="tpu_custom_call" | custom-call | flops 99999997952 | bytes 1 | tf_op jit(solution)/shard_map/piece/pallas_call | solution.py:293
  122.9 6.0 %collective-permute-done.17.refs_1_ = f32[2,384,512]{2,1,0:T(8,128)} collective-permute-done((f32[2,384,512]{2,1,0:T(8,128)}, f32[2,384,512]{2,1,0:T(8,128)}, u32[]{:S(2)}, u32[]{:S(2)}) %collective-permute-start.17) | collective-permute-done | bytes 1572896 | tf_op jit(solution)/shard_map/ppermute | solution.py:522
  138.6 23.1 %collective-permute-done.15.refs_0_ = f32[1024,384]{1,0:T(8,128)} collective-permute-done((f32[1024,384]{1,0:T(8,128)}, f32[1024,384]{1,0:T(8,128)}, u32[]{:S(2)}, u32[]{:S(2)}) %collective-permute-start.15) | collective-permute-done | bytes 1572896 | tf_op jit(solution)/shard_map/ppermute | solution.py:439
  162.6 7.0 %piece.18 = (f32[2,384,512]{2,1,0:T(8,128)}, f32[1536,384]{1,0:T(8,128)}) custom-call(s32[31]{0:T(128)} %stack.124.idx_ref.table_ref, bf16[512,9216]{1,0:T(8,128)(2,1)} %own_ref.31, bf16[1024,512]{1,0:T(8,128)(2,1)} %get-tuple-element.50.g_ref, bf16[1024,512]{1,0:T(8,128)(2,1)} %get-tuple-element.51.x_ref, bf16[9216,512]{1,0:T(8,128)(2,1)} %w_ref.31, ...), custom_call_target="tpu_custom_call" | custom-call | flops 99999997952 | bytes 1 | tf_op jit(solution)/shard_map/piece/pallas_call | solution.py:293
  180.7 15.6 %collective-permute-done.22.refs_5_.refs_1_ = f32[2,384,512]{2,1,0:T(8,128)} collective-permute-done((f32[2,384,512]{2,1,0:T(8,128)}, f32[2,384,512]{2,1,0:T(8,128)}, u32[]{:S(2)}, u32[]{:S(2)}) %collective-permute-start.22) | collective-permute-done | bytes 1572896 | tf_op jit(solution)/shard_map/ppermute | solution.py:522
  196.3 6.2 %piece.20.refs_2_ = f32[2,384,512]{2,1,0:T(8,128)} custom-call(s32[31]{0:T(128)} %stack.124.idx_ref.table_ref, bf16[512,9216]{1,0:T(8,128)(2,1)} %own_ref.31, bf16[1024,512]{1,0:T(8,128)(2,1)} %get-tuple-element.50.g_ref, bf16[1024,512]{1,0:T(8,128)(2,1)} %get-tuple-element.51.x_ref, bf16[9216,512]{1,0:T(8,128)(2,1)} %w_ref.31, ...), custom_call_target="tpu_custom_call" | custom-call | flops 1 | bytes 1 | tf_op jit(solution)/shard_map/piece/pallas_call | solution.py:293
  202.5 6.0 %piece.21.refs_3_ = f32[2,384,512]{2,1,0:T(8,128)} custom-call(s32[31]{0:T(128)} %stack.124.idx_ref.table_ref, bf16[512,9216]{1,0:T(8,128)(2,1)} %own_ref.31, bf16[1024,512]{1,0:T(8,128)(2,1)} %get-tuple-element.50.g_ref, bf16[1024,512]{1,0:T(8,128)(2,1)} %get-tuple-element.51.x_ref, bf16[9216,512]{1,0:T(8,128)(2,1)} %w_ref.31, ...), custom_call_target="tpu_custom_call" | custom-call | flops 99999997952 | bytes 1 | tf_op jit(solution)/shard_map/piece/pallas_call | solution.py:293
  210.8 19.2 %collective-permute-done.25.refs_5_.refs_3_ = f32[2,384,512]{2,1,0:T(8,128)} collective-permute-done((f32[2,384,512]{2,1,0:T(8,128)}, f32[2,384,512]{2,1,0:T(8,128)}, u32[]{:S(2)}, u32[]{:S(2)}) %collective-permute-start.25) | collective-permute-done | bytes 1572896 | tf_op jit(solution)/shard_map/ppermute | solution.py:522
  230.0 6.2 %piece.22.refs_4_ = f32[2,384,512]{2,1,0:T(8,128)} custom-call(s32[31]{0:T(128)} %stack.124.idx_ref.table_ref, bf16[512,9216]{1,0:T(8,128)(2,1)} %own_ref.31, bf16[1024,512]{1,0:T(8,128)(2,1)} %get-tuple-element.50.g_ref, bf16[1024,512]{1,0:T(8,128)(2,1)} %get-tuple-element.51.x_ref, bf16[9216,512]{1,0:T(8,128)(2,1)} %w_ref.31, ...), custom_call_target="tpu_custom_call" | custom-call | flops 1 | bytes 1 | tf_op jit(solution)/shard_map/piece/pallas_call | solution.py:293
  236.2 6.6 %piece.23 = (f32[2,384,512]{2,1,0:T(8,128)}, f32[1024,384]{1,0:T(8,128)}) custom-call(s32[31]{0:T(128)} %stack.124.idx_ref.table_ref, bf16[512,9216]{1,0:T(8,128)(2,1)} %own_ref.31, bf16[1024,512]{1,0:T(8,128)(2,1)} %get-tuple-element.50.g_ref, bf16[1024,512]{1,0:T(8,128)(2,1)} %get-tuple-element.51.x_ref, bf16[9216,512]{1,0:T(8,128)(2,1)} %w_ref.31, ...), custom_call_target="tpu_custom_call" | custom-call | flops 99999997952 | bytes 1 | tf_op jit(solution)/shard_map/piece/pallas_call | solution.py:293
  246.7 11.7 %collective-permute-done.26.refs_4_.refs_0_ = f32[2,384,512]{2,1,0:T(8,128)} collective-permute-done((f32[2,384,512]{2,1,0:T(8,128)}, f32[2,384,512]{2,1,0:T(8,128)}, u32[]{:S(2)}, u32[]{:S(2)}) %collective-permute-start.26) | collective-permute-done | bytes 1572896 | tf_op jit(solution)/shard_map/ppermute | solution.py:579
  263.7 6.2 %piece.24.refs_2_ = f32[2,384,512]{2,1,0:T(8,128)} custom-call(s32[31]{0:T(128)} %stack.124.idx_ref.table_ref, bf16[512,9216]{1,0:T(8,128)(2,1)} %own_ref.31, bf16[1024,512]{1,0:T(8,128)(2,1)} %get-tuple-element.50.g_ref, bf16[1024,512]{1,0:T(8,128)(2,1)} %get-tuple-element.51.x_ref, bf16[9216,512]{1,0:T(8,128)(2,1)} %w_ref.31, ...), custom_call_target="tpu_custom_call" | custom-call | flops 1 | bytes 1 | tf_op jit(solution)/shard_map/piece/pallas_call | solution.py:293
  269.9 5.9 %piece.25.refs_1_ = f32[2,384,512]{2,1,0:T(8,128)} custom-call(s32[31]{0:T(128)} %stack.124.idx_ref.table_ref, bf16[512,9216]{1,0:T(8,128)(2,1)} %own_ref.31, bf16[1024,512]{1,0:T(8,128)(2,1)} %get-tuple-element.50.g_ref, bf16[1024,512]{1,0:T(8,128)(2,1)} %get-tuple-element.51.x_ref, bf16[9216,512]{1,0:T(8,128)(2,1)} %w_ref.31, ...), custom_call_target="tpu_custom_call" | custom-call | flops 99999997952 | bytes 1 | tf_op jit(solution)/shard_map/piece/pallas_call | solution.py:293
  279.3 6.6 %final_first.1 = (f32[1152,512]{1,0:T(8,128)}, f32[1152,512]{1,0:T(8,128)}) custom-call(s32[31]{0:T(128)} %stack.124.idx_ref.table_ref, bf16[512,9216]{1,0:T(8,128)(2,1)} %own_ref.31, bf16[1024,512]{1,0:T(8,128)(2,1)} %get-tuple-element.50.g_ref, bf16[1024,512]{1,0:T(8,128)(2,1)} %get-tuple-element.51.x_ref, bf16[9216,512]{1,0:T(8,128)(2,1)} %w_ref.31, ...), custom_call_target="tpu_custom_call" | custom-call | flops 1 | bytes 1 | tf_op jit(solution)/shard_map/final_first/pallas_call | solution.py:382
  285.9 6.2 %collective-permute-done.29.refs_1_ = f32[2,384,512]{2,1,0:T(8,128)} collective-permute-done((f32[2,384,512]{2,1,0:T(8,128)}, f32[2,384,512]{2,1,0:T(8,128)}, u32[]{:S(2)}, u32[]{:S(2)}) %collective-permute-start.29) | collective-permute-done | bytes 1572896 | tf_op jit(solution)/shard_map/ppermute | solution.py:579
  292.0 5.9 %piece.26.refs_0_.a_ref = f32[2,384,512]{2,1,0:T(8,128)} custom-call(s32[31]{0:T(128)} %stack.124.idx_ref.table_ref, bf16[512,9216]{1,0:T(8,128)(2,1)} %own_ref.31, bf16[1024,512]{1,0:T(8,128)(2,1)} %get-tuple-element.50.g_ref, bf16[1024,512]{1,0:T(8,128)(2,1)} %get-tuple-element.51.x_ref, bf16[9216,512]{1,0:T(8,128)(2,1)} %w_ref.31, ...), custom_call_target="tpu_custom_call" | custom-call | flops 1 | bytes 1 | tf_op jit(solution)/shard_map/piece/pallas_call | solution.py:293
  306.0 18.0 %collective-permute-done.32.refs_1_ = f32[2,384,512]{2,1,0:T(8,128)} collective-permute-done((f32[2,384,512]{2,1,0:T(8,128)}, f32[2,384,512]{2,1,0:T(8,128)}, u32[]{:S(2)}, u32[]{:S(2)}) %collective-permute-start.32) | collective-permute-done | bytes 1572896 | tf_op jit(solution)/shard_map/ppermute | solution.py:579
  324.1 5.9 %piece.27.a_ref = f32[2,384,512]{2,1,0:T(8,128)} custom-call(s32[31]{0:T(128)} %stack.124.idx_ref.table_ref, bf16[512,9216]{1,0:T(8,128)(2,1)} %own_ref.31, bf16[1024,512]{1,0:T(8,128)(2,1)} %get-tuple-element.50.g_ref, bf16[1024,512]{1,0:T(8,128)(2,1)} %get-tuple-element.51.x_ref, bf16[9216,512]{1,0:T(8,128)(2,1)} %w_ref.31, ...), custom_call_target="tpu_custom_call" | custom-call | flops 1 | bytes 1 | tf_op jit(solution)/shard_map/piece/pallas_call | solution.py:293
  (87 shorter events, 107.8 us)
Async XLA Ops:
  10.4 23.0 %collective-permute-start.5 = (f32[512,384]{1,0:T(8,128)}, f32[512,384]{1,0:T(8,128)S(1)}, u32[]{:S(2)}, u32[]{:S(2)}) collective-permute-start(f32[512,384]{1,0:T(8,128)} %get-tuple-element.42), channel_id=1, source_target_pairs={{0,4},{4,0},{8,12},{12,8},{16,20},{20,16},{24,28},{28,24},{1,5},{5... | collective-permute-start | bytes 2359304 | tf_op jit(solution)/shard_map/ppermute | solution.py:439
  19.3 25.4 %collective-permute-start.8 = (f32[512,384]{1,0:T(8,128)}, f32[512,384]{1,0:T(8,128)S(1)}, u32[]{:S(2)}, u32[]{:S(2)}) collective-permute-start(f32[512,384]{1,0:T(8,128)} %get-tuple-element.47), channel_id=1, source_target_pairs={{0,8},{4,12},{24,16},{28,20},{1,9},{5,13},{25,17},{29,21},{2,10},{... | collective-permute-start | bytes 2359304 | tf_op jit(solution)/shard_map/ppermute | solution.py:522
  33.5 20.8 %collective-permute-start = (f32[256,512]{1,0:T(8,128)}, f32[256,512]{1,0:T(8,128)}, u32[]{:S(2)}, u32[]{:S(2)}) collective-permute-start(f32[256,512]{1,0:T(8,128)} %get-tuple-element.39), channel_id=1, source_target_pairs={{0,8},{4,12},{24,16},{28,20},{1,9},{5,13},{25,17},{29,21},{2,10},{... | collective-permute-start | bytes 1572872 | tf_op jit(solution)/shard_map/ppermute | solution.py:522
  34.8 31.9 %collective-permute-start.12 = (f32[512,384]{1,0:T(8,128)}, f32[512,384]{1,0:T(8,128)}, u32[]{:S(2)}, u32[]{:S(2)}) collective-permute-start(f32[512,384]{1,0:T(8,128)} %get-tuple-element.52), channel_id=1, source_target_pairs={{0,4},{4,0},{8,12},{12,8},{16,20},{20,16},{24,28},{28,24},{1,5},{5... | collective-permute-start | bytes 2359304 | tf_op jit(solution)/shard_map/ppermute | solution.py:439
  55.8 55.3 %collective-permute-start.14 = (f32[2,384,512]{2,1,0:T(8,128)}, f32[2,384,512]{2,1,0:T(8,128)}, u32[]{:S(2)}, u32[]{:S(2)}) collective-permute-start(f32[2,384,512]{2,1,0:T(8,128)} %get-tuple-element.48.refs_1_), channel_id=1, source_target_pairs={{0,8},{4,12},{24,16},{28,20},{1,9},{5,13},{25,17},{29,21},{2,10},{... | collective-permute-start | bytes 4718600 | tf_op jit(solution)/shard_map/ppermute | solution.py:522
  57.1 37.6 %collective-permute-start.13 = (f32[1024,384]{1,0:T(8,128)}, f32[1024,384]{1,0:T(8,128)}, u32[]{:S(2)}, u32[]{:S(2)}) collective-permute-start(f32[1024,384]{1,0:T(8,128)} %get-tuple-element.57), channel_id=1, source_target_pairs={{0,4},{4,0},{8,12},{12,8},{16,20},{20,16},{24,28},{28,24},{1,5},{5... | collective-permute-start | bytes 4718600 | tf_op jit(solution)/shard_map/ppermute | solution.py:439
  72.2 56.7 %collective-permute-start.17 = (f32[2,384,512]{2,1,0:T(8,128)}, f32[2,384,512]{2,1,0:T(8,128)}, u32[]{:S(2)}, u32[]{:S(2)}) collective-permute-start(f32[2,384,512]{2,1,0:T(8,128)} %piece.14.refs_4_.refs_2_), channel_id=1, source_target_pairs={{0,8},{4,12},{24,16},{28,20},{1,9},{5,13},{25,17},{29,21},{2,10},{... | collective-permute-start | bytes 4718600 | tf_op jit(solution)/shard_map/ppermute | solution.py:522
  82.2 46.7 %collective-permute-start.18 = (f32[2,384,512]{2,1,0:T(8,128)}, f32[2,384,512]{2,1,0:T(8,128)}, u32[]{:S(2)}, u32[]{:S(2)}) collective-permute-start(f32[2,384,512]{2,1,0:T(8,128)} %piece.15.refs_0_), channel_id=1, source_target_pairs={{8,12},{12,8},{16,20},{20,16},{9,13},{13,9},{17,21},{21,17},{10,14... | collective-permute-start | bytes 4718600 | tf_op jit(solution)/shard_map/ppermute | solution.py:439
  117.7 44.0 %collective-permute-start.19 = (f32[2,384,512]{2,1,0:T(8,128)}, f32[2,384,512]{2,1,0:T(8,128)}, u32[]{:S(2)}, u32[]{:S(2)}) collective-permute-start(f32[2,384,512]{2,1,0:T(8,128)} %get-tuple-element.61.refs_2_), channel_id=1, source_target_pairs={{8,16},{12,20},{16,8},{20,12},{9,17},{13,21},{17,9},{21,13},{10,18... | collective-permute-start | bytes 4718600 | tf_op jit(solution)/shard_map/ppermute | solution.py:579
  120.0 42.6 %collective-permute-start.16 = (f32[2,384,512]{2,1,0:T(8,128)}, f32[2,384,512]{2,1,0:T(8,128)}, u32[]{:S(2)}, u32[]{:S(2)}) collective-permute-start(f32[2,384,512]{2,1,0:T(8,128)} %get-tuple-element.61.refs_2_), channel_id=1, source_target_pairs={{0,8},{4,12},{24,16},{28,20},{1,9},{5,13},{25,17},{29,21},{2,10},{... | collective-permute-start | bytes 4718600 | tf_op jit(solution)/shard_map/ppermute | solution.py:522
  121.3 40.3 %collective-permute-start.15 = (f32[1024,384]{1,0:T(8,128)}, f32[1024,384]{1,0:T(8,128)}, u32[]{:S(2)}, u32[]{:S(2)}) collective-permute-start(f32[1024,384]{1,0:T(8,128)} %get-tuple-element.60), channel_id=1, source_target_pairs={{0,4},{4,0},{8,12},{12,8},{16,20},{20,16},{24,28},{28,24},{1,5},{5... | collective-permute-start | bytes 4718600 | tf_op jit(solution)/shard_map/ppermute | solution.py:439
  134.8 61.5 %collective-permute-start.22 = (f32[2,384,512]{2,1,0:T(8,128)}, f32[2,384,512]{2,1,0:T(8,128)}, u32[]{:S(2)}, u32[]{:S(2)}) collective-permute-start(f32[2,384,512]{2,1,0:T(8,128)} %piece.17.refs_5_), channel_id=1, source_target_pairs={{0,8},{4,12},{24,16},{28,20},{1,9},{5,13},{25,17},{29,21},{2,10},{... | collective-permute-start | bytes 4718600 | tf_op jit(solution)/shard_map/ppermute | solution.py:522
  136.1 60.2 %collective-permute-start.21 = (f32[2,384,512]{2,1,0:T(8,128)}, f32[2,384,512]{2,1,0:T(8,128)}, u32[]{:S(2)}, u32[]{:S(2)}) collective-permute-start(f32[2,384,512]{2,1,0:T(8,128)} %piece.17.refs_5_), channel_id=1, source_target_pairs={{8,16},{12,20},{16,8},{20,12},{9,17},{13,21},{17,9},{21,13},{10,18... | collective-permute-start | bytes 4718600 | tf_op jit(solution)/shard_map/ppermute | solution.py:579
  169.6 60.4 %collective-permute-start.25 = (f32[2,384,512]{2,1,0:T(8,128)}, f32[2,384,512]{2,1,0:T(8,128)}, u32[]{:S(2)}, u32[]{:S(2)}) collective-permute-start(f32[2,384,512]{2,1,0:T(8,128)} %get-tuple-element.63.refs_2_), channel_id=1, source_target_pairs={{0,8},{4,12},{24,16},{28,20},{1,9},{5,13},{25,17},{29,21},{2,10},{... | collective-permute-start | bytes 4718600 | tf_op jit(solution)/shard_map/ppermute | solution.py:522
  170.9 59.1 %collective-permute-start.24 = (f32[2,384,512]{2,1,0:T(8,128)}, f32[2,384,512]{2,1,0:T(8,128)}, u32[]{:S(2)}, u32[]{:S(2)}) collective-permute-start(f32[2,384,512]{2,1,0:T(8,128)} %get-tuple-element.63.refs_2_), channel_id=1, source_target_pairs={{8,16},{12,20},{16,8},{20,12},{9,17},{13,21},{17,9},{21,13},{10,18... | collective-permute-start | bytes 4718600 | tf_op jit(solution)/shard_map/ppermute | solution.py:579
  173.2 56.8 %collective-permute-start.20 = (f32[1536,384]{1,0:T(8,128)}, f32[1536,384]{1,0:T(8,128)}, u32[]{:S(2)}, u32[]{:S(2)}) collective-permute-start(f32[1536,384]{1,0:T(8,128)} %get-tuple-element.62), channel_id=1, source_target_pairs={{0,4},{4,0},{8,12},{12,8},{16,20},{20,16},{24,28},{28,24},{1,5},{5... | collective-permute-start | bytes 7077896 | tf_op jit(solution)/shard_map/ppermute | solution.py:439
  202.5 61.2 %collective-permute-start.23 = (f32[2,384,512]{2,1,0:T(8,128)}, f32[2,384,512]{2,1,0:T(8,128)}, u32[]{:S(2)}, u32[]{:S(2)}) collective-permute-start(f32[2,384,512]{2,1,0:T(8,128)} %piece.20.refs_2_), channel_id=1, source_target_pairs={{0,8},{4,12},{24,16},{28,20},{8,0},{12,4},{16,24},{20,28},{1,9},{5... | collective-permute-start | bytes 4718600 | tf_op jit(solution)/shard_map/ppermute | solution.py:568
  208.4 49.9 %collective-permute-start.26 = (f32[2,384,512]{2,1,0:T(8,128)}, f32[2,384,512]{2,1,0:T(8,128)}, u32[]{:S(2)}, u32[]{:S(2)}) collective-permute-start(f32[2,384,512]{2,1,0:T(8,128)} %piece.21.refs_3_), channel_id=1, source_target_pairs={{8,16},{12,20},{16,8},{20,12},{9,17},{13,21},{17,9},{21,13},{10,18... | collective-permute-start | bytes 4718600 | tf_op jit(solution)/shard_map/ppermute | solution.py:579
  236.2 64.6 %collective-permute-start.31 = (f32[2,384,512]{2,1,0:T(8,128)}, f32[2,384,512]{2,1,0:T(8,128)}, u32[]{:S(2)}, u32[]{:S(2)}) collective-permute-start(f32[2,384,512]{2,1,0:T(8,128)} %piece.22.refs_4_), channel_id=1, source_target_pairs={{0,8},{4,12},{24,16},{28,20},{8,0},{12,4},{16,24},{20,28},{1,9},{5... | collective-permute-start | bytes 4718600 | tf_op jit(solution)/shard_map/ppermute | solution.py:568
  242.8 36.0 %collective-permute-start.28 = (f32[1024,384]{1,0:T(8,128)}, f32[1024,384]{1,0:T(8,128)}, u32[]{:S(2)}, u32[]{:S(2)}) collective-permute-start(f32[1024,384]{1,0:T(8,128)} %get-tuple-element.66), channel_id=1, source_target_pairs={{0,4},{4,0},{8,12},{12,8},{16,20},{20,16},{24,28},{28,24},{1,5},{5... | collective-permute-start | bytes 4718600 | tf_op jit(solution)/shard_map/ppermute | solution.py:439
  244.3 47.7 %collective-permute-start.29 = (f32[2,384,512]{2,1,0:T(8,128)}, f32[2,384,512]{2,1,0:T(8,128)}, u32[]{:S(2)}, u32[]{:S(2)}) collective-permute-start(f32[2,384,512]{2,1,0:T(8,128)} %get-tuple-element.64.refs_3_), channel_id=1, source_target_pairs={{8,16},{12,20},{16,8},{20,12},{9,17},{13,21},{17,9},{21,13},{10,18... | collective-permute-start | bytes 4718600 | tf_op jit(solution)/shard_map/ppermute | solution.py:579
  275.8 48.3 %collective-permute-start.32 = (f32[2,384,512]{2,1,0:T(8,128)}, f32[2,384,512]{2,1,0:T(8,128)}, u32[]{:S(2)}, u32[]{:S(2)}) collective-permute-start(f32[2,384,512]{2,1,0:T(8,128)} %piece.25.refs_1_), channel_id=1, source_target_pairs={{8,16},{12,20},{16,8},{20,12},{9,17},{13,21},{17,9},{21,13},{10,18... | collective-permute-start | bytes 4718600 | tf_op jit(solution)/shard_map/ppermute | solution.py:579
  278.4 52.4 %collective-permute-start.33 = (f32[2,384,512]{2,1,0:T(8,128)}, f32[2,384,512]{2,1,0:T(8,128)}, u32[]{:S(2)}, u32[]{:S(2)}) collective-permute-start(f32[2,384,512]{2,1,0:T(8,128)} %piece.24.refs_2_), channel_id=1, source_target_pairs={{0,8},{4,12},{24,16},{28,20},{8,0},{12,4},{16,24},{20,28},{1,9},{5... | collective-permute-start | bytes 4718600 | tf_op jit(solution)/shard_map/ppermute | solution.py:568
  278.8 19.2 %collective-permute-start.27 = (f32[256,512]{1,0:T(8,128)}, f32[256,512]{1,0:T(8,128)S(1)}, u32[]{:S(2)}, u32[]{:S(2)}) collective-permute-start(f32[256,512]{1,0:T(8,128)} %get-tuple-element.65.refs_4_), channel_id=1, source_target_pairs={{0,2},{1,3},{2,0},{3,1},{4,6},{5,7},{6,4},{7,5},{8,10},{9,11},{10,... | collective-permute-start | bytes 1572872 | tf_op jit(solution)/shard_map/ppermute | solution.py:442
  (19 other events, 188.1 us)

commit v7 on v6

--- a/solution.py
+++ b/solution.py
@@ -183,7 +183,7 @@
         ),
         out_shape=[half, half],
         compiler_params=params(),
-        cost_estimate=piece_cost(FLOPS),
+        cost_estimate=piece_cost(),
         name="input_partial",
     )(blk.reshape(1), out_grads, pre_act, w_out, w_in, *after)
 
@@ -577,12 +577,11 @@
             got.append(swap(blocks[0], every))
         if s >= 2:
             across[s - 2] = lax.ppermute(out, "dp", inner_to_inner)
-        if s == 0:
+        if s == 1:
             line_quarter = tied((quarter_in, out))[0]
-        if s == 1:
             in_1, in_2 = flip(line_quarter, 1), flip(line_quarter, 2)
             in_3 = flip(in_2, 1)
-            line_g, line_x = join(blk, out_grads, inputs, [line_quarter, in_1, in_2, in_3], [last])
+            line_g, line_x = join(blk, out_grads, inputs, [line_quarter, in_1, in_2, in_3], [last, got[2]])
             (last,) = piece(
                 scale,
                 table,
@@ -596,8 +595,9 @@
                 after=[last],
             )
             first_in = swap(last, inner_planes)
-            rows_kept, last = input_partial(blk, out_grads, pre_act, w_in, w_out, 4 * size, [last, got[2]])
-            rows_given = last
+        if s == 3:
+            rows_kept, rows_given = input_partial(blk, out_grads, pre_act, w_in, w_out, 4 * size, [last])
+            last = rows_given
         if s == 4:
             (held_in,) = piece(
                 scale,

time: 335 us -> 329 us (0.982)
  waiting for transfers between devices: 153 us -> 147 us
    ppermute x6, waiting for transfers between devices: 35.8 us -> 6.17 us  [line_body(): across[s - 2] = lax.ppermute(out, 'dp', inner_to_inner)]
    ppermute x3, waiting for transfers between devices: 6.16 us -> 31.8 us  [line_body(): toward.append(lax.ppermute(last, 'dp', outer_to_inner + inner_to_outer))]
    ppermute x8, waiting for transfers between devices: 41.7 us -> 28.9 us  [swap(): lax.ppermute(array, 'dp', [(2 * a + h, 2 * a + 1 - h) for a in planes for...]
    ppermute x9, waiting for transfers between devices: 61.2 us -> 69.5 us  [send_in(): return lax.ppermute(array, 'dp', outer_to_inner)]
  transfers between devices with their start and end apart: 34 -> 34, of which waited for: 19 -> 17; matrix products, arithmetic and copies ran while one was open for 0% -> 0% of each run, Pallas kernels for 38% -> 39%
where the time goes in v7:
time: 329 us; the launch traced here: 327 us
  waiting for transfers between devices  147 us (45%)
  Pallas kernels  133 us (40%)
  starting transfers between devices  41.3 us (13%)
  local copies, waits for them, and re-layouts  4.13 us (1%)
    pallas_call x14, Pallas kernels, piece(): pl.pallas_call(functools.partial(piece_kernel, scale, counts, inner_at),...  85.2 us
    ppermute x9, waiting for transfers between devices, send_in(): return lax.ppermute(array, 'dp', outer_to_inner)  69.5 us
    ppermute x3, waiting for transfers between devices, line_body(): toward.append(lax.ppermute(last, 'dp', outer_to_inner + inner_to_outer))  31.8 us
    ppermute x8, waiting for transfers between devices, swap(): lax.ppermute(array, 'dp', [(2 * a + h, 2 * a + 1 - h) for a in planes for...  28.9 us
    pallas_call x1, Pallas kernels, input_partial(): pl.pallas_call(input_kernel, grid_spec=pltpu.PrefetchScalarGridSpec(num_s...  16.4 us
    ppermute x6, starting transfers between devices, line_body(): across[s - 2] = lax.ppermute(out, 'dp', inner_to_inner)  14 us
    ppermute x9, starting transfers between devices, send_in(): return lax.ppermute(array, 'dp', outer_to_inner)  11.5 us
    ppermute x8, starting transfers between devices, swap(): lax.ppermute(array, 'dp', [(2 * a + h, 2 * a + 1 - h) for a in planes for...  11.1 us
  transfers between devices with their start and end apart: 34, of which 17 were waited for; matrix products, arithmetic and copies ran while one was open for 0% of the time, Pallas kernels for 39%

profile of v7, /device:TPU:16, one launch (start us, length us, event | category | flops | bytes accessed | tf_op | source)
XLA Modules:
  0.0 327.4 jit_solution(7583761720541399295)
XLA Ops:
  20.5 7.3 %collective-permute-done.5.refs_1_ = f32[512,256]{1,0:T(8,128)S(1)} collective-permute-done((f32[512,256]{1,0:T(8,128)}, f32[512,256]{1,0:T(8,128)S(1)}, u32[]{:S(2)}, u32[]{:S(2)}) %collective-permute-start.5) | collective-permute-done | bytes 524320 | tf_op jit(solution)/shard_map/ppermute | solution.py:522
  35.9 8.8 %collective-permute-done.7.refs_0_ = f32[512,384]{1,0:T(8,128)S(1)} collective-permute-done((f32[512,384]{1,0:T(8,128)}, f32[512,384]{1,0:T(8,128)S(1)}, u32[]{:S(2)}, u32[]{:S(2)}) %collective-permute-start.7) | collective-permute-done | bytes 786464 | tf_op jit(solution)/shard_map/ppermute | solution.py:522
  45.6 6.7 %first_piece.1 = (f32[2,384,512]{2,1,0:T(8,128)}, bf16[1024,512]{1,0:T(8,128)(2,1)}, bf16[1024,512]{1,0:T(8,128)(2,1)}, f32[1024,384]{1,0:T(8,128)}) custom-call(s32[31]{0:T(128)} %stack.124.idx_ref.table_ref, bf16[512,9216]{1,0:T(8,128)(2,1)} %own_ref.31, bf16[9216,512]{1,0:T(8,128)(2,1)} %w_ref.31, f32[512,384]{1,0:T(8,128)} %copy-done.1, ...), custom_call_target="tpu_custom_call" | custom-call | flops 1 | bytes 1 | tf_op jit(solution)/shard_map/first_piece/pallas_call | solution.py:332
  61.9 10.2 %collective-permute-done.14.refs_2_ = f32[256,512]{1,0:T(8,128)S(1)} collective-permute-done((f32[256,512]{1,0:T(8,128)}, f32[256,512]{1,0:T(8,128)S(1)}, u32[]{:S(2)}, u32[]{:S(2)}) %collective-permute-start.14) | collective-permute-done | bytes 524320 | tf_op jit(solution)/shard_map/ppermute | solution.py:442
  75.0 10.6 %collective-permute-done.8.refs_5_.refs_0_ = f32[1024,384]{1,0:T(8,128)} collective-permute-done((f32[1024,384]{1,0:T(8,128)}, f32[1024,384]{1,0:T(8,128)}, u32[]{:S(2)}, u32[]{:S(2)}) %collective-permute-start.8) | collective-permute-done | bytes 1572896 | tf_op jit(solution)/shard_map/ppermute | solution.py:439
  97.7 6.7 %piece.16 = (f32[2,384,512]{2,1,0:T(8,128)}, f32[1024,384]{1,0:T(8,128)}) custom-call(s32[31]{0:T(128)} %stack.124.idx_ref.table_ref, bf16[512,9216]{1,0:T(8,128)(2,1)} %own_ref.31, bf16[1024,512]{1,0:T(8,128)(2,1)} %get-tuple-element.48.g_ref, bf16[1024,512]{1,0:T(8,128)(2,1)} %get-tuple-element.49.x_ref, bf16[9216,512]{1,0:T(8,128)(2,1)} %w_ref.31, ...), custom_call_target="tpu_custom_call" | custom-call | flops 99999997952 | bytes 1 | tf_op jit(solution)/shard_map/piece/pallas_call | solution.py:293
  108.5 18.4 %collective-permute-done.11.refs_1_ = f32[2,384,512]{2,1,0:T(8,128)} collective-permute-done((f32[2,384,512]{2,1,0:T(8,128)}, f32[2,384,512]{2,1,0:T(8,128)}, u32[]{:S(2)}, u32[]{:S(2)}) %collective-permute-start.11) | collective-permute-done | bytes 1572896 | tf_op jit(solution)/shard_map/ppermute | solution.py:522
  126.9 6.9 %collective-permute-done.16.refs_3_.refs_1_ = f32[2,384,512]{2,1,0:T(8,128)} collective-permute-done((f32[2,384,512]{2,1,0:T(8,128)}, f32[2,384,512]{2,1,0:T(8,128)}, u32[]{:S(2)}, u32[]{:S(2)}) %collective-permute-start.16) | collective-permute-done | bytes 1572896 | tf_op jit(solution)/shard_map/ppermute | solution.py:439
  143.5 16.4 %input_partial.1 = (f32[256,512]{1,0:T(8,128)}, f32[256,512]{1,0:T(8,128)}) custom-call(s32[1]{0:T(128)} %bitcast.blk_ref, bf16[512,512]{1,0:T(8,128)(2,1)} %grads_ref.7, bf16[512,9216]{1,0:T(8,128)(2,1)} %own_ref.31, bf16[9216,512]{1,0:T(8,128)(2,1)} %w_ref.31, bf16[9216,512]{1,0:T(8,128)(2,1)} %in_rows_ref.1, f32[2,384,512]{2,1,0:T(8,128)} %piece.17.refs_0_), custom_call_target="tpu_custom_call" | custom-call | flops 1 | bytes 1 | tf_op jit(solution)/shard_map/input_partial/pallas_call | solution.py:174
  162.3 7.1 %piece.18 = (f32[2,384,512]{2,1,0:T(8,128)}, f32[1536,384]{1,0:T(8,128)}) custom-call(s32[31]{0:T(128)} %stack.124.idx_ref.table_ref, bf16[512,9216]{1,0:T(8,128)(2,1)} %own_ref.31, bf16[1024,512]{1,0:T(8,128)(2,1)} %get-tuple-element.48.g_ref, bf16[1024,512]{1,0:T(8,128)(2,1)} %get-tuple-element.49.x_ref, bf16[9216,512]{1,0:T(8,128)(2,1)} %w_ref.31, ...), custom_call_target="tpu_custom_call" | custom-call | flops 99999997952 | bytes 1 | tf_op jit(solution)/shard_map/piece/pallas_call | solution.py:293
  174.5 6.0 %piece.19.refs_3_.inner_ref = f32[2,384,512]{2,1,0:T(8,128)} custom-call(s32[31]{0:T(128)} %stack.124.idx_ref.table_ref, bf16[512,9216]{1,0:T(8,128)(2,1)} %own_ref.31, bf16[1024,512]{1,0:T(8,128)(2,1)} %get-tuple-element.54.g_ref, bf16[1024,512]{1,0:T(8,128)(2,1)} %get-tuple-element.55.x_ref, bf16[9216,512]{1,0:T(8,128)(2,1)} %w_ref.31, ...), custom_call_target="tpu_custom_call" | custom-call | flops 1 | bytes 1 | tf_op jit(solution)/shard_map/piece/pallas_call | solution.py:293
  180.5 13.9 %collective-permute-done.22.refs_5_.refs_1_ = f32[2,384,512]{2,1,0:T(8,128)} collective-permute-done((f32[2,384,512]{2,1,0:T(8,128)}, f32[2,384,512]{2,1,0:T(8,128)}, u32[]{:S(2)}, u32[]{:S(2)}) %collective-permute-start.22) | collective-permute-done | bytes 1572896 | tf_op jit(solution)/shard_map/ppermute | solution.py:522
  194.4 6.1 %piece.20.refs_2_ = f32[2,384,512]{2,1,0:T(8,128)} custom-call(s32[31]{0:T(128)} %stack.124.idx_ref.table_ref, bf16[512,9216]{1,0:T(8,128)(2,1)} %own_ref.31, bf16[1024,512]{1,0:T(8,128)(2,1)} %get-tuple-element.48.g_ref, bf16[1024,512]{1,0:T(8,128)(2,1)} %get-tuple-element.49.x_ref, bf16[9216,512]{1,0:T(8,128)(2,1)} %w_ref.31, ...), custom_call_target="tpu_custom_call" | custom-call | flops 1 | bytes 1 | tf_op jit(solution)/shard_map/piece/pallas_call | solution.py:293
  200.5 5.9 %piece.21.refs_3_ = f32[2,384,512]{2,1,0:T(8,128)} custom-call(s32[31]{0:T(128)} %stack.124.idx_ref.table_ref, bf16[512,9216]{1,0:T(8,128)(2,1)} %own_ref.31, bf16[1024,512]{1,0:T(8,128)(2,1)} %get-tuple-element.48.g_ref, bf16[1024,512]{1,0:T(8,128)(2,1)} %get-tuple-element.49.x_ref, bf16[9216,512]{1,0:T(8,128)(2,1)} %w_ref.31, ...), custom_call_target="tpu_custom_call" | custom-call | flops 99999997952 | bytes 1 | tf_op jit(solution)/shard_map/piece/pallas_call | solution.py:293
  208.8 19.3 %collective-permute-done.25.refs_5_.refs_3_ = f32[2,384,512]{2,1,0:T(8,128)} collective-permute-done((f32[2,384,512]{2,1,0:T(8,128)}, f32[2,384,512]{2,1,0:T(8,128)}, u32[]{:S(2)}, u32[]{:S(2)}) %collective-permute-start.25) | collective-permute-done | bytes 1572896 | tf_op jit(solution)/shard_map/ppermute | solution.py:522
  228.1 6.2 %piece.22.refs_4_ = f32[2,384,512]{2,1,0:T(8,128)} custom-call(s32[31]{0:T(128)} %stack.124.idx_ref.table_ref, bf16[512,9216]{1,0:T(8,128)(2,1)} %own_ref.31, bf16[1024,512]{1,0:T(8,128)(2,1)} %get-tuple-element.48.g_ref, bf16[1024,512]{1,0:T(8,128)(2,1)} %get-tuple-element.49.x_ref, bf16[9216,512]{1,0:T(8,128)(2,1)} %w_ref.31, ...), custom_call_target="tpu_custom_call" | custom-call | flops 1 | bytes 1 | tf_op jit(solution)/shard_map/piece/pallas_call | solution.py:293
  234.2 6.6 %piece.23 = (f32[2,384,512]{2,1,0:T(8,128)}, f32[1024,384]{1,0:T(8,128)}) custom-call(s32[31]{0:T(128)} %stack.124.idx_ref.table_ref, bf16[512,9216]{1,0:T(8,128)(2,1)} %own_ref.31, bf16[1024,512]{1,0:T(8,128)(2,1)} %get-tuple-element.48.g_ref, bf16[1024,512]{1,0:T(8,128)(2,1)} %get-tuple-element.49.x_ref, bf16[9216,512]{1,0:T(8,128)(2,1)} %w_ref.31, ...), custom_call_target="tpu_custom_call" | custom-call | flops 99999997952 | bytes 1 | tf_op jit(solution)/shard_map/piece/pallas_call | solution.py:293
  243.9 17.8 %collective-permute-done.23.refs_5_.refs_1_.outer_ref = f32[2,384,512]{2,1,0:T(8,128)} collective-permute-done((f32[2,384,512]{2,1,0:T(8,128)}, f32[2,384,512]{2,1,0:T(8,128)}, u32[]{:S(2)}, u32[]{:S(2)}) %collective-permute-start.23) | collective-permute-done | bytes 1572896 | tf_op jit(solution)/shard_map/ppermute | solution.py:568
  261.8 6.2 %piece.24.refs_2_ = f32[2,384,512]{2,1,0:T(8,128)} custom-call(s32[31]{0:T(128)} %stack.124.idx_ref.table_ref, bf16[512,9216]{1,0:T(8,128)(2,1)} %own_ref.31, bf16[1024,512]{1,0:T(8,128)(2,1)} %get-tuple-element.48.g_ref, bf16[1024,512]{1,0:T(8,128)(2,1)} %get-tuple-element.49.x_ref, bf16[9216,512]{1,0:T(8,128)(2,1)} %w_ref.31, ...), custom_call_target="tpu_custom_call" | custom-call | flops 1 | bytes 1 | tf_op jit(solution)/shard_map/piece/pallas_call | solution.py:293
  267.9 5.9 %piece.25.refs_1_ = f32[2,384,512]{2,1,0:T(8,128)} custom-call(s32[31]{0:T(128)} %stack.124.idx_ref.table_ref, bf16[512,9216]{1,0:T(8,128)(2,1)} %own_ref.31, bf16[1024,512]{1,0:T(8,128)(2,1)} %get-tuple-element.48.g_ref, bf16[1024,512]{1,0:T(8,128)(2,1)} %get-tuple-element.49.x_ref, bf16[9216,512]{1,0:T(8,128)(2,1)} %w_ref.31, ...), custom_call_target="tpu_custom_call" | custom-call | flops 99999997952 | bytes 1 | tf_op jit(solution)/shard_map/piece/pallas_call | solution.py:293
  277.9 6.6 %final_first.1 = (f32[1152,512]{1,0:T(8,128)}, f32[1152,512]{1,0:T(8,128)}) custom-call(s32[31]{0:T(128)} %stack.124.idx_ref.table_ref, bf16[512,9216]{1,0:T(8,128)(2,1)} %own_ref.31, bf16[1024,512]{1,0:T(8,128)(2,1)} %get-tuple-element.48.g_ref, bf16[1024,512]{1,0:T(8,128)(2,1)} %get-tuple-element.49.x_ref, bf16[9216,512]{1,0:T(8,128)(2,1)} %w_ref.31, ...), custom_call_target="tpu_custom_call" | custom-call | flops 1 | bytes 1 | tf_op jit(solution)/shard_map/final_first/pallas_call | solution.py:382
  300.7 6.2 %collective-permute-done.32.refs_1_ = f32[2,384,512]{2,1,0:T(8,128)} collective-permute-done((f32[2,384,512]{2,1,0:T(8,128)}, f32[2,384,512]{2,1,0:T(8,128)}, u32[]{:S(2)}, u32[]{:S(2)}) %collective-permute-start.32) | collective-permute-done | bytes 1572896 | tf_op jit(solution)/shard_map/ppermute | solution.py:579
  306.8 5.9 %piece.27.a_ref = f32[2,384,512]{2,1,0:T(8,128)} custom-call(s32[31]{0:T(128)} %stack.124.idx_ref.table_ref, bf16[512,9216]{1,0:T(8,128)(2,1)} %own_ref.31, bf16[1024,512]{1,0:T(8,128)(2,1)} %get-tuple-element.48.g_ref, bf16[1024,512]{1,0:T(8,128)(2,1)} %get-tuple-element.49.x_ref, bf16[9216,512]{1,0:T(8,128)(2,1)} %w_ref.31, ...), custom_call_target="tpu_custom_call" | custom-call | flops 1 | bytes 1 | tf_op jit(solution)/shard_map/piece/pallas_call | solution.py:293
  312.8 11.8 %collective-permute-done.33.b_ref = f32[2,384,512]{2,1,0:T(8,128)} collective-permute-done((f32[2,384,512]{2,1,0:T(8,128)}, f32[2,384,512]{2,1,0:T(8,128)}, u32[]{:S(2)}, u32[]{:S(2)}) %collective-permute-start.33) | collective-permute-done | bytes 1572896 | tf_op jit(solution)/shard_map/ppermute | solution.py:568
  (91 shorter events, 102.3 us)
Async XLA Ops:
  10.4 24.1 %collective-permute-start.4 = (f32[512,384]{1,0:T(8,128)}, f32[512,384]{1,0:T(8,128)S(1)}, u32[]{:S(2)}, u32[]{:S(2)}) collective-permute-start(f32[512,384]{1,0:T(8,128)} %get-tuple-element.42), channel_id=1, source_target_pairs={{0,4},{4,0},{8,12},{12,8},{16,20},{20,16},{24,28},{28,24},{1,5},{5... | collective-permute-start | bytes 2359304 | tf_op jit(solution)/shard_map/ppermute | solution.py:439
  10.9 17.0 %collective-permute-start.5 = (f32[512,256]{1,0:T(8,128)}, f32[512,256]{1,0:T(8,128)S(1)}, u32[]{:S(2)}, u32[]{:S(2)}) collective-permute-start(f32[512,256]{1,0:T(8,128)} %get-tuple-element.43), channel_id=1, source_target_pairs={{0,8},{4,12},{24,16},{28,20},{1,9},{5,13},{25,17},{29,21},{2,10},{... | collective-permute-start | bytes 1572872 | tf_op jit(solution)/shard_map/ppermute | solution.py:522
  19.3 25.5 %collective-permute-start.7 = (f32[512,384]{1,0:T(8,128)}, f32[512,384]{1,0:T(8,128)S(1)}, u32[]{:S(2)}, u32[]{:S(2)}) collective-permute-start(f32[512,384]{1,0:T(8,128)} %get-tuple-element.47), channel_id=1, source_target_pairs={{0,8},{4,12},{24,16},{28,20},{1,9},{5,13},{25,17},{29,21},{2,10},{... | collective-permute-start | bytes 2359304 | tf_op jit(solution)/shard_map/ppermute | solution.py:522
  27.9 27.1 %collective-permute-start.9 = (f32[512,384]{1,0:T(8,128)}, f32[512,384]{1,0:T(8,128)}, u32[]{:S(2)}, u32[]{:S(2)}) collective-permute-start(f32[512,384]{1,0:T(8,128)} %get-tuple-element.51), channel_id=1, source_target_pairs={{0,4},{4,0},{8,12},{12,8},{16,20},{20,16},{24,28},{28,24},{1,5},{5... | collective-permute-start | bytes 2359304 | tf_op jit(solution)/shard_map/ppermute | solution.py:439
  34.6 20.4 %collective-permute-start.10 = (f32[256,512]{1,0:T(8,128)}, f32[256,512]{1,0:T(8,128)}, u32[]{:S(2)}, u32[]{:S(2)}) collective-permute-start(f32[256,512]{1,0:T(8,128)} %get-tuple-element.39), channel_id=1, source_target_pairs={{0,8},{4,12},{24,16},{28,20},{1,9},{5,13},{25,17},{29,21},{2,10},{... | collective-permute-start | bytes 1572872 | tf_op jit(solution)/shard_map/ppermute | solution.py:522
  52.3 33.3 %collective-permute-start.8 = (f32[1024,384]{1,0:T(8,128)}, f32[1024,384]{1,0:T(8,128)}, u32[]{:S(2)}, u32[]{:S(2)}) collective-permute-start(f32[1024,384]{1,0:T(8,128)} %get-tuple-element.50), channel_id=1, source_target_pairs={{0,4},{4,0},{8,12},{12,8},{16,20},{20,16},{24,28},{28,24},{1,5},{5... | collective-permute-start | bytes 4718600 | tf_op jit(solution)/shard_map/ppermute | solution.py:439
  53.7 44.0 %collective-permute-start.12 = (f32[2,384,512]{2,1,0:T(8,128)}, f32[2,384,512]{2,1,0:T(8,128)}, u32[]{:S(2)}, u32[]{:S(2)}) collective-permute-start(f32[2,384,512]{2,1,0:T(8,128)} %get-tuple-element.52.refs_1_), channel_id=1, source_target_pairs={{0,8},{4,12},{24,16},{28,20},{1,9},{5,13},{25,17},{29,21},{2,10},{... | collective-permute-start | bytes 4718600 | tf_op jit(solution)/shard_map/ppermute | solution.py:522
  72.1 54.9 %collective-permute-start.11 = (f32[2,384,512]{2,1,0:T(8,128)}, f32[2,384,512]{2,1,0:T(8,128)}, u32[]{:S(2)}, u32[]{:S(2)}) collective-permute-start(f32[2,384,512]{2,1,0:T(8,128)} %piece.14.refs_4_.refs_2_), channel_id=1, source_target_pairs={{0,8},{4,12},{24,16},{28,20},{1,9},{5,13},{25,17},{29,21},{2,10},{... | collective-permute-start | bytes 4718600 | tf_op jit(solution)/shard_map/ppermute | solution.py:522
  94.3 39.5 %collective-permute-start.16 = (f32[2,384,512]{2,1,0:T(8,128)}, f32[2,384,512]{2,1,0:T(8,128)}, u32[]{:S(2)}, u32[]{:S(2)}) collective-permute-start(f32[2,384,512]{2,1,0:T(8,128)} %piece.15.refs_4_), channel_id=1, source_target_pairs={{8,12},{12,8},{16,20},{20,16},{9,13},{13,9},{17,21},{21,17},{10,14... | collective-permute-start | bytes 4718600 | tf_op jit(solution)/shard_map/ppermute | solution.py:439
  104.3 58.0 %collective-permute-start.19 = (f32[2,384,512]{2,1,0:T(8,128)}, f32[2,384,512]{2,1,0:T(8,128)}, u32[]{:S(2)}, u32[]{:S(2)}) collective-permute-start(f32[2,384,512]{2,1,0:T(8,128)} %get-tuple-element.58.refs_2_), channel_id=1, source_target_pairs={{8,16},{12,20},{16,8},{20,12},{9,17},{13,21},{17,9},{21,13},{10,18... | collective-permute-start | bytes 4718600 | tf_op jit(solution)/shard_map/ppermute | solution.py:579
  106.7 55.7 %collective-permute-start.18 = (f32[2,384,512]{2,1,0:T(8,128)}, f32[2,384,512]{2,1,0:T(8,128)}, u32[]{:S(2)}, u32[]{:S(2)}) collective-permute-start(f32[2,384,512]{2,1,0:T(8,128)} %get-tuple-element.58.refs_2_), channel_id=1, source_target_pairs={{0,8},{4,12},{24,16},{28,20},{1,9},{5,13},{25,17},{29,21},{2,10},{... | collective-permute-start | bytes 4718600 | tf_op jit(solution)/shard_map/ppermute | solution.py:522
  108.0 54.4 %collective-permute-start.17 = (f32[1024,384]{1,0:T(8,128)}, f32[1024,384]{1,0:T(8,128)}, u32[]{:S(2)}, u32[]{:S(2)}) collective-permute-start(f32[1024,384]{1,0:T(8,128)} %get-tuple-element.61), channel_id=1, source_target_pairs={{0,4},{4,0},{8,12},{12,8},{16,20},{20,16},{24,28},{28,24},{1,5},{5... | collective-permute-start | bytes 4718600 | tf_op jit(solution)/shard_map/ppermute | solution.py:439
  139.8 54.6 %collective-permute-start.22 = (f32[2,384,512]{2,1,0:T(8,128)}, f32[2,384,512]{2,1,0:T(8,128)}, u32[]{:S(2)}, u32[]{:S(2)}) collective-permute-start(f32[2,384,512]{2,1,0:T(8,128)} %piece.17.refs_0_), channel_id=1, source_target_pairs={{0,8},{4,12},{24,16},{28,20},{1,9},{5,13},{25,17},{29,21},{2,10},{... | collective-permute-start | bytes 4718600 | tf_op jit(solution)/shard_map/ppermute | solution.py:522
  141.1 53.3 %collective-permute-start.21 = (f32[2,384,512]{2,1,0:T(8,128)}, f32[2,384,512]{2,1,0:T(8,128)}, u32[]{:S(2)}, u32[]{:S(2)}) collective-permute-start(f32[2,384,512]{2,1,0:T(8,128)} %piece.17.refs_0_), channel_id=1, source_target_pairs={{8,16},{12,20},{16,8},{20,12},{9,17},{13,21},{17,9},{21,13},{10,18... | collective-permute-start | bytes 4718600 | tf_op jit(solution)/shard_map/ppermute | solution.py:579
  169.5 58.6 %collective-permute-start.25 = (f32[2,384,512]{2,1,0:T(8,128)}, f32[2,384,512]{2,1,0:T(8,128)}, u32[]{:S(2)}, u32[]{:S(2)}) collective-permute-start(f32[2,384,512]{2,1,0:T(8,128)} %get-tuple-element.63.refs_2_), channel_id=1, source_target_pairs={{0,8},{4,12},{24,16},{28,20},{1,9},{5,13},{25,17},{29,21},{2,10},{... | collective-permute-start | bytes 4718600 | tf_op jit(solution)/shard_map/ppermute | solution.py:522
  170.8 57.3 %collective-permute-start.24 = (f32[2,384,512]{2,1,0:T(8,128)}, f32[2,384,512]{2,1,0:T(8,128)}, u32[]{:S(2)}, u32[]{:S(2)}) collective-permute-start(f32[2,384,512]{2,1,0:T(8,128)} %get-tuple-element.63.refs_2_), channel_id=1, source_target_pairs={{8,16},{12,20},{16,8},{20,12},{9,17},{13,21},{17,9},{21,13},{10,18... | collective-permute-start | bytes 4718600 | tf_op jit(solution)/shard_map/ppermute | solution.py:579
  172.9 55.2 %collective-permute-start.20 = (f32[1536,384]{1,0:T(8,128)}, f32[1536,384]{1,0:T(8,128)}, u32[]{:S(2)}, u32[]{:S(2)}) collective-permute-start(f32[1536,384]{1,0:T(8,128)} %get-tuple-element.62), channel_id=1, source_target_pairs={{0,4},{4,0},{8,12},{12,8},{16,20},{20,16},{24,28},{28,24},{1,5},{5... | collective-permute-start | bytes 7077896 | tf_op jit(solution)/shard_map/ppermute | solution.py:439
  200.5 61.3 %collective-permute-start.23 = (f32[2,384,512]{2,1,0:T(8,128)}, f32[2,384,512]{2,1,0:T(8,128)}, u32[]{:S(2)}, u32[]{:S(2)}) collective-permute-start(f32[2,384,512]{2,1,0:T(8,128)} %piece.20.refs_2_), channel_id=1, source_target_pairs={{0,8},{4,12},{24,16},{28,20},{8,0},{12,4},{16,24},{20,28},{1,9},{5... | collective-permute-start | bytes 4718600 | tf_op jit(solution)/shard_map/ppermute | solution.py:568
  206.4 37.5 %collective-permute-start.26 = (f32[2,384,512]{2,1,0:T(8,128)}, f32[2,384,512]{2,1,0:T(8,128)}, u32[]{:S(2)}, u32[]{:S(2)}) collective-permute-start(f32[2,384,512]{2,1,0:T(8,128)} %piece.21.refs_3_), channel_id=1, source_target_pairs={{8,16},{12,20},{16,8},{20,12},{9,17},{13,21},{17,9},{21,13},{10,18... | collective-permute-start | bytes 4718600 | tf_op jit(solution)/shard_map/ppermute | solution.py:579
  234.2 61.2 %collective-permute-start.31 = (f32[2,384,512]{2,1,0:T(8,128)}, f32[2,384,512]{2,1,0:T(8,128)}, u32[]{:S(2)}, u32[]{:S(2)}) collective-permute-start(f32[2,384,512]{2,1,0:T(8,128)} %piece.22.refs_4_), channel_id=1, source_target_pairs={{0,8},{4,12},{24,16},{28,20},{8,0},{12,4},{16,24},{20,28},{1,9},{5... | collective-permute-start | bytes 4718600 | tf_op jit(solution)/shard_map/ppermute | solution.py:568
  240.9 35.4 %collective-permute-start.28 = (f32[1024,384]{1,0:T(8,128)}, f32[1024,384]{1,0:T(8,128)}, u32[]{:S(2)}, u32[]{:S(2)}) collective-permute-start(f32[1024,384]{1,0:T(8,128)} %get-tuple-element.66), channel_id=1, source_target_pairs={{0,4},{4,0},{8,12},{12,8},{16,20},{20,16},{24,28},{28,24},{1,5},{5... | collective-permute-start | bytes 4718600 | tf_op jit(solution)/shard_map/ppermute | solution.py:439
  241.5 43.0 %collective-permute-start.29 = (f32[2,384,512]{2,1,0:T(8,128)}, f32[2,384,512]{2,1,0:T(8,128)}, u32[]{:S(2)}, u32[]{:S(2)}) collective-permute-start(f32[2,384,512]{2,1,0:T(8,128)} %get-tuple-element.64.refs_3_), channel_id=1, source_target_pairs={{8,16},{12,20},{16,8},{20,12},{9,17},{13,21},{17,9},{21,13},{10,18... | collective-permute-start | bytes 4718600 | tf_op jit(solution)/shard_map/ppermute | solution.py:579
  273.9 33.0 %collective-permute-start.32 = (f32[2,384,512]{2,1,0:T(8,128)}, f32[2,384,512]{2,1,0:T(8,128)}, u32[]{:S(2)}, u32[]{:S(2)}) collective-permute-start(f32[2,384,512]{2,1,0:T(8,128)} %piece.25.refs_1_), channel_id=1, source_target_pairs={{8,16},{12,20},{16,8},{20,12},{9,17},{13,21},{17,9},{21,13},{10,18... | collective-permute-start | bytes 4718600 | tf_op jit(solution)/shard_map/ppermute | solution.py:579
  276.2 48.3 %collective-permute-start.33 = (f32[2,384,512]{2,1,0:T(8,128)}, f32[2,384,512]{2,1,0:T(8,128)}, u32[]{:S(2)}, u32[]{:S(2)}) collective-permute-start(f32[2,384,512]{2,1,0:T(8,128)} %piece.24.refs_2_), channel_id=1, source_target_pairs={{0,8},{4,12},{24,16},{28,20},{8,0},{12,4},{16,24},{20,28},{1,9},{5... | collective-permute-start | bytes 4718600 | tf_op jit(solution)/shard_map/ppermute | solution.py:568
  (21 other events, 183.2 us)

commit v8 on v7

--- a/solution.py
+++ b/solution.py
@@ -241,7 +241,8 @@
     for n in counts:
         groups.append(refs[:n])
         refs = refs[n:]
-    partners, others, columns, sums, _, (out_ref, *sends) = groups + [refs]
+    partners, others, columns, sums, _, outs = groups + [refs]
+    outs, sends = (outs[:-1], outs[-1:]) if columns else (outs, [])
     partner = jnp.concatenate([ref[...] for ref in partners], axis=1)
     for ref in others:
         partner = jnp.where(table_ref[inner_at] > 0, ref[...], partner)
@@ -249,7 +250,11 @@
     for ref in sums:
         grad_in = grad_in + ref[0]
         grad_out = grad_out + ref[1]
-    out_ref[0], out_ref[1] = grad_in, grad_out
+    start = 0
+    for ref in outs:
+        end = start + ref.shape[1]
+        ref[0], ref[1] = grad_in[start:end], grad_out[start:end]
+        start = end
     rows = own_ref.shape[0]
     for ref in sends:
         for k, column_ref in enumerate(columns):
@@ -279,10 +284,11 @@
 
 
 def piece(
-    scale, table, at, pre_act, partners, place, g, x, w_out, sums=(), other=None, inner_at=0, sends=(), after=(), flops=1
+    scale, table, at, pre_act, partners, place, g, x, w_out, sums=(), other=None, inner_at=0, sends=(), split=(), after=(), flops=1
 ):
     rows, width = pre_act.shape[0], g.shape[1]
     size = sum(p.shape[1] for p in partners)
+    shapes = [(2, n, width) for n in split or (size,)]
     whole = pl.BlockSpec((2, size, width), lambda i, table: (0, 0, 0))
     others, other_specs = [], []
     if other is not None:
@@ -301,9 +307,10 @@
             + [columns_spec(rows, size, k) for k in sends]
             + [whole] * len(sums)
             + anywhere(after),
-            out_specs=[whole] + [pl.BlockSpec(shape, lambda i, table: (0, 0)) for shape in sent],
+            out_specs=[pl.BlockSpec(shape, lambda i, table: (0, 0, 0)) for shape in shapes]
+            + [pl.BlockSpec(shape, lambda i, table: (0, 0)) for shape in sent],
         ),
-        out_shape=[jax.ShapeDtypeStruct(shape, jnp.float32) for shape in [(2, size, width)] + sent],
+        out_shape=[jax.ShapeDtypeStruct(shape, jnp.float32) for shape in shapes + sent],
         compiler_params=params(),
         cost_estimate=piece_cost(flops),
         name="piece",
@@ -403,18 +410,23 @@
     out_ref[...] = a_ref[1] + b_ref[1]
 
 
-def final_add(place, a, b, held, after):
-    _, size, width = a.shape
-    steps = 2
-    block = pl.BlockSpec((2, size // steps, width), lambda i: (0, i, 0))
+def final_add(first_row, offset, a, b, held, steps, after):
+    _, size, width = b.shape
+    step = size // steps
     return pl.pallas_call(
         add_kernel,
         grid=(steps,),
-        in_specs=[block, block] + anywhere(held) + anywhere(after),
-        out_specs=[pl.BlockSpec((size // steps, width), lambda i: (place * steps + i, 0))] * 2,
+        in_specs=[
+            pl.BlockSpec((2, step, width), lambda i: (0, offset // step + i, 0)),
+            pl.BlockSpec((2, step, width), lambda i: (0, i, 0)),
+        ]
+        + anywhere(held)
+        + anywhere(after),
+        out_specs=[pl.BlockSpec((step, width), lambda i: (first_row // step + i, 0))] * 2,
         out_shape=[jax.ShapeDtypeStruct(h.shape, h.dtype) for h in held],
         input_output_aliases={2: 0, 3: 1},
         compiler_params=params(),
+        cost_estimate=piece_cost(),
         name="final_add",
     )(a, b, *held, *after)
 
@@ -558,14 +570,17 @@
         else:
             after = [last] + held_back + ([quarter_in] if s == 1 else [])
             if j >= 0:
-                (last,) = run(
+                split = (2 * third, third) if j == count - 1 else (size,)
+                last, *rest = run(
                     ("out", j),
                     partner,
                     sums=[across[j]],
                     other=(got[j], 0) if j < 2 else (got[4], 2),
+                    split=split,
                     after=after + sums,
                 )
-                toward.append(lax.ppermute(last, "dp", outer_to_inner + inner_to_outer))
+                parts = [lax.ppermute(array, "dp", outer_to_inner + inner_to_outer) for array in (last, *rest)]
+                toward.append(parts[0] if j < count - 1 else parts)
                 after = [last]
             out, *blocks = run(
                 ("main", s), partner, sums=sums, sends=sends, after=after, flops=FLOPS
@@ -638,11 +653,12 @@
         if i == 1:
             rows_kept, rows_given = fold(blk, rows_kept, rows_got, [out])
             rows_got = flip(rows_given, 1)
-            held = final_add(i, out, toward[double + i], held, [rows_given])
+            held = final_add(i * size, 0, out, toward[double + i], held, 2, [rows_given])
             grad_inputs = round_sum(rows_kept, rows_got, [held[0]])
             last = grad_inputs
         else:
-            held = final_add(i, out, toward[double + i], held, [])
+            held = final_add(i * size, 0, out, parts[0], held, 1, [])
+            held = final_add(i * size + 2 * third, 2 * third, out, parts[1], held, 1, [])
     return (grad_inputs, held[0], held[1])
 
 

time: 329 us -> 328 us (level)
  waiting for transfers between devices: 147 us -> 142 us
    ppermute x3 -> x4, waiting for transfers between devices: 31.8 us -> 27.4 us  [line_body(): lax.ppermute(array, 'dp', outer_to_inner + inner_to_outer)]
    pallas_call x2 -> x3, Pallas kernels: 5.61 us -> 7.38 us  [final_add(): pl.pallas_call(add_kernel, grid=(steps,), in_specs=[pl.BlockSpec((2, step...]
  transfers between devices with their start and end apart: 34 -> 35, of which waited for: 17 -> 18; matrix products, arithmetic and copies ran while one was open for 0% -> 0% of each run, Pallas kernels for 39% -> 40%
where the time goes in v8:
time: 328 us; the launch traced here: 327 us
  waiting for transfers between devices  142 us (43%)
  Pallas kernels  135 us (41%)
  starting transfers between devices  43.8 us (13%)
  local copies, waits for them, and re-layouts  4.06 us (1%)
    pallas_call x14, Pallas kernels, piece(): pl.pallas_call(functools.partial(piece_kernel, scale, counts, inner_at),...  85.1 us
    ppermute x9, waiting for transfers between devices, send_in(): return lax.ppermute(array, 'dp', outer_to_inner)  69.7 us
    ppermute x8, waiting for transfers between devices, swap(): lax.ppermute(array, 'dp', [(2 * a + h, 2 * a + 1 - h) for a in planes for...  28.3 us
    ppermute x4, waiting for transfers between devices, line_body(): lax.ppermute(array, 'dp', outer_to_inner + inner_to_outer)  27.4 us
    pallas_call x1, Pallas kernels, input_partial(): pl.pallas_call(input_kernel, grid_spec=pltpu.PrefetchScalarGridSpec(num_s...  16.4 us
    ppermute x6, starting transfers between devices, line_body(): across[s - 2] = lax.ppermute(out, 'dp', inner_to_inner)  14.5 us
    ppermute x9, starting transfers between devices, send_in(): return lax.ppermute(array, 'dp', outer_to_inner)  11.5 us
    ppermute x8, starting transfers between devices, swap(): lax.ppermute(array, 'dp', [(2 * a + h, 2 * a + 1 - h) for a in planes for...  11.1 us
  transfers between devices with their start and end apart: 35, of which 18 were waited for; matrix products, arithmetic and copies ran while one was open for 0% of the time, Pallas kernels for 40%

profile of v8, /device:TPU:16, one launch (start us, length us, event | category | flops | bytes accessed | tf_op | source)
XLA Modules:
  0.0 326.6 jit_solution(9266683237464495348)
XLA Ops:
  20.6 7.3 %collective-permute-done.5.refs_1_ = f32[512,256]{1,0:T(8,128)S(1)} collective-permute-done((f32[512,256]{1,0:T(8,128)}, f32[512,256]{1,0:T(8,128)S(1)}, u32[]{:S(2)}, u32[]{:S(2)}) %collective-permute-start.5) | collective-permute-done | bytes 524320 | tf_op jit(solution)/shard_map/ppermute | solution.py:534
  35.9 8.8 %collective-permute-done.7.refs_0_ = f32[512,384]{1,0:T(8,128)S(1)} collective-permute-done((f32[512,384]{1,0:T(8,128)}, f32[512,384]{1,0:T(8,128)S(1)}, u32[]{:S(2)}, u32[]{:S(2)}) %collective-permute-start.7) | collective-permute-done | bytes 786464 | tf_op jit(solution)/shard_map/ppermute | solution.py:534
  45.7 6.5 %first_piece.1 = (f32[2,384,512]{2,1,0:T(8,128)}, bf16[1024,512]{1,0:T(8,128)(2,1)}, bf16[1024,512]{1,0:T(8,128)(2,1)}, f32[1024,384]{1,0:T(8,128)}) custom-call(s32[31]{0:T(128)} %stack.124.idx_ref.table_ref, bf16[512,9216]{1,0:T(8,128)(2,1)} %own_ref.31, bf16[9216,512]{1,0:T(8,128)(2,1)} %w_ref.31, f32[512,384]{1,0:T(8,128)} %copy-done.1, ...), custom_call_target="tpu_custom_call" | custom-call | flops 1 | bytes 1 | tf_op jit(solution)/shard_map/first_piece/pallas_call | solution.py:339
  62.0 10.2 %collective-permute-done.14.refs_2_ = f32[256,512]{1,0:T(8,128)S(1)} collective-permute-done((f32[256,512]{1,0:T(8,128)}, f32[256,512]{1,0:T(8,128)S(1)}, u32[]{:S(2)}, u32[]{:S(2)}) %collective-permute-start.14) | collective-permute-done | bytes 524320 | tf_op jit(solution)/shard_map/ppermute | solution.py:454
  75.1 10.4 %collective-permute-done.8.refs_5_.refs_0_ = f32[1024,384]{1,0:T(8,128)} collective-permute-done((f32[1024,384]{1,0:T(8,128)}, f32[1024,384]{1,0:T(8,128)}, u32[]{:S(2)}, u32[]{:S(2)}) %collective-permute-start.8) | collective-permute-done | bytes 1572896 | tf_op jit(solution)/shard_map/ppermute | solution.py:451
  97.7 6.6 %piece.16 = (f32[2,384,512]{2,1,0:T(8,128)}, f32[1024,384]{1,0:T(8,128)}) custom-call(s32[31]{0:T(128)} %stack.124.idx_ref.table_ref, bf16[512,9216]{1,0:T(8,128)(2,1)} %own_ref.31, bf16[1024,512]{1,0:T(8,128)(2,1)} %get-tuple-element.52.g_ref, bf16[1024,512]{1,0:T(8,128)(2,1)} %get-tuple-element.53.x_ref, bf16[9216,512]{1,0:T(8,128)(2,1)} %w_ref.31, ...), custom_call_target="tpu_custom_call" | custom-call | flops 99999997952 | bytes 1 | tf_op jit(solution)/shard_map/piece/pallas_call | solution.py:299
  108.5 18.4 %collective-permute-done.11.refs_1_ = f32[2,384,512]{2,1,0:T(8,128)} collective-permute-done((f32[2,384,512]{2,1,0:T(8,128)}, f32[2,384,512]{2,1,0:T(8,128)}, u32[]{:S(2)}, u32[]{:S(2)}) %collective-permute-start.11) | collective-permute-done | bytes 1572896 | tf_op jit(solution)/shard_map/ppermute | solution.py:534
  127.0 6.8 %collective-permute-done.16.refs_3_.refs_1_ = f32[2,384,512]{2,1,0:T(8,128)} collective-permute-done((f32[2,384,512]{2,1,0:T(8,128)}, f32[2,384,512]{2,1,0:T(8,128)}, u32[]{:S(2)}, u32[]{:S(2)}) %collective-permute-start.16) | collective-permute-done | bytes 1572896 | tf_op jit(solution)/shard_map/ppermute | solution.py:451
  143.5 16.4 %input_partial.1 = (f32[256,512]{1,0:T(8,128)}, f32[256,512]{1,0:T(8,128)}) custom-call(s32[1]{0:T(128)} %bitcast.blk_ref, bf16[512,512]{1,0:T(8,128)(2,1)} %grads_ref.7, bf16[512,9216]{1,0:T(8,128)(2,1)} %own_ref.31, bf16[9216,512]{1,0:T(8,128)(2,1)} %w_ref.31, bf16[9216,512]{1,0:T(8,128)(2,1)} %in_rows_ref.1, f32[2,384,512]{2,1,0:T(8,128)} %piece.17.refs_0_), custom_call_target="tpu_custom_call" | custom-call | flops 1 | bytes 1 | tf_op jit(solution)/shard_map/input_partial/pallas_call | solution.py:174
  162.2 7.0 %piece.18 = (f32[2,384,512]{2,1,0:T(8,128)}, f32[1536,384]{1,0:T(8,128)}) custom-call(s32[31]{0:T(128)} %stack.124.idx_ref.table_ref, bf16[512,9216]{1,0:T(8,128)(2,1)} %own_ref.31, bf16[1024,512]{1,0:T(8,128)(2,1)} %get-tuple-element.52.g_ref, bf16[1024,512]{1,0:T(8,128)(2,1)} %get-tuple-element.53.x_ref, bf16[9216,512]{1,0:T(8,128)(2,1)} %w_ref.31, ...), custom_call_target="tpu_custom_call" | custom-call | flops 99999997952 | bytes 1 | tf_op jit(solution)/shard_map/piece/pallas_call | solution.py:299
  174.5 5.9 %piece.19.refs_3_.inner_ref = f32[2,384,512]{2,1,0:T(8,128)} custom-call(s32[31]{0:T(128)} %stack.124.idx_ref.table_ref, bf16[512,9216]{1,0:T(8,128)(2,1)} %own_ref.31, bf16[1024,512]{1,0:T(8,128)(2,1)} %get-tuple-element.58.g_ref, bf16[1024,512]{1,0:T(8,128)(2,1)} %get-tuple-element.59.x_ref, bf16[9216,512]{1,0:T(8,128)(2,1)} %w_ref.31, ...), custom_call_target="tpu_custom_call" | custom-call | flops 1 | bytes 1 | tf_op jit(solution)/shard_map/piece/pallas_call | solution.py:299
  180.4 14.0 %collective-permute-done.22.refs_5_.refs_1_ = f32[2,384,512]{2,1,0:T(8,128)} collective-permute-done((f32[2,384,512]{2,1,0:T(8,128)}, f32[2,384,512]{2,1,0:T(8,128)}, u32[]{:S(2)}, u32[]{:S(2)}) %collective-permute-start.22) | collective-permute-done | bytes 1572896 | tf_op jit(solution)/shard_map/ppermute | solution.py:534
  194.4 6.1 %piece.20.refs_2_ = f32[2,384,512]{2,1,0:T(8,128)} custom-call(s32[31]{0:T(128)} %stack.124.idx_ref.table_ref, bf16[512,9216]{1,0:T(8,128)(2,1)} %own_ref.31, bf16[1024,512]{1,0:T(8,128)(2,1)} %get-tuple-element.52.g_ref, bf16[1024,512]{1,0:T(8,128)(2,1)} %get-tuple-element.53.x_ref, bf16[9216,512]{1,0:T(8,128)(2,1)} %w_ref.31, ...), custom_call_target="tpu_custom_call" | custom-call | flops 1 | bytes 1 | tf_op jit(solution)/shard_map/piece/pallas_call | solution.py:299
  200.5 5.9 %piece.21.refs_3_ = f32[2,384,512]{2,1,0:T(8,128)} custom-call(s32[31]{0:T(128)} %stack.124.idx_ref.table_ref, bf16[512,9216]{1,0:T(8,128)(2,1)} %own_ref.31, bf16[1024,512]{1,0:T(8,128)(2,1)} %get-tuple-element.52.g_ref, bf16[1024,512]{1,0:T(8,128)(2,1)} %get-tuple-element.53.x_ref, bf16[9216,512]{1,0:T(8,128)(2,1)} %w_ref.31, ...), custom_call_target="tpu_custom_call" | custom-call | flops 99999997952 | bytes 1 | tf_op jit(solution)/shard_map/piece/pallas_call | solution.py:299
  208.8 19.3 %collective-permute-done.25.refs_5_.refs_3_ = f32[2,384,512]{2,1,0:T(8,128)} collective-permute-done((f32[2,384,512]{2,1,0:T(8,128)}, f32[2,384,512]{2,1,0:T(8,128)}, u32[]{:S(2)}, u32[]{:S(2)}) %collective-permute-start.25) | collective-permute-done | bytes 1572896 | tf_op jit(solution)/shard_map/ppermute | solution.py:534
  228.1 6.2 %piece.22.refs_4_ = f32[2,384,512]{2,1,0:T(8,128)} custom-call(s32[31]{0:T(128)} %stack.124.idx_ref.table_ref, bf16[512,9216]{1,0:T(8,128)(2,1)} %own_ref.31, bf16[1024,512]{1,0:T(8,128)(2,1)} %get-tuple-element.52.g_ref, bf16[1024,512]{1,0:T(8,128)(2,1)} %get-tuple-element.53.x_ref, bf16[9216,512]{1,0:T(8,128)(2,1)} %w_ref.31, ...), custom_call_target="tpu_custom_call" | custom-call | flops 1 | bytes 1 | tf_op jit(solution)/shard_map/piece/pallas_call | solution.py:299
  234.3 6.6 %piece.23 = (f32[2,384,512]{2,1,0:T(8,128)}, f32[1024,384]{1,0:T(8,128)}) custom-call(s32[31]{0:T(128)} %stack.124.idx_ref.table_ref, bf16[512,9216]{1,0:T(8,128)(2,1)} %own_ref.31, bf16[1024,512]{1,0:T(8,128)(2,1)} %get-tuple-element.52.g_ref, bf16[1024,512]{1,0:T(8,128)(2,1)} %get-tuple-element.53.x_ref, bf16[9216,512]{1,0:T(8,128)(2,1)} %w_ref.31, ...), custom_call_target="tpu_custom_call" | custom-call | flops 99999997952 | bytes 1 | tf_op jit(solution)/shard_map/piece/pallas_call | solution.py:299
  244.0 17.8 %collective-permute-done.23.refs_5_.refs_1_.outer_ref = f32[2,384,512]{2,1,0:T(8,128)} collective-permute-done((f32[2,384,512]{2,1,0:T(8,128)}, f32[2,384,512]{2,1,0:T(8,128)}, u32[]{:S(2)}, u32[]{:S(2)}) %collective-permute-start.23) | collective-permute-done | bytes 1572896 | tf_op jit(solution)/shard_map/ppermute | solution.py:582
  261.8 6.1 %piece.24 = (f32[2,256,512]{2,1,0:T(8,128)}, f32[2,128,512]{2,1,0:T(8,128)}) custom-call(s32[31]{0:T(128)} %stack.124.idx_ref.table_ref, bf16[512,9216]{1,0:T(8,128)(2,1)} %own_ref.31, bf16[1024,512]{1,0:T(8,128)(2,1)} %get-tuple-element.52.g_ref, bf16[1024,512]{1,0:T(8,128)(2,1)} %get-tuple-element.53.x_ref, bf16[9216,512]{1,0:T(8,128)(2,1)} %w_ref.31, ...), custom_call_target="tpu_custom_call" | custom-call | flops 1 | bytes 1 | tf_op jit(solution)/shard_map/piece/pallas_call | solution.py:299
  267.9 5.9 %piece.25.refs_1_ = f32[2,384,512]{2,1,0:T(8,128)} custom-call(s32[31]{0:T(128)} %stack.124.idx_ref.table_ref, bf16[512,9216]{1,0:T(8,128)(2,1)} %own_ref.31, bf16[1024,512]{1,0:T(8,128)(2,1)} %get-tuple-element.52.g_ref, bf16[1024,512]{1,0:T(8,128)(2,1)} %get-tuple-element.53.x_ref, bf16[9216,512]{1,0:T(8,128)(2,1)} %w_ref.31, ...), custom_call_target="tpu_custom_call" | custom-call | flops 99999997952 | bytes 1 | tf_op jit(solution)/shard_map/piece/pallas_call | solution.py:299
  279.8 6.6 %final_first.1 = (f32[1152,512]{1,0:T(8,128)}, f32[1152,512]{1,0:T(8,128)}) custom-call(s32[31]{0:T(128)} %stack.124.idx_ref.table_ref, bf16[512,9216]{1,0:T(8,128)(2,1)} %own_ref.31, bf16[1024,512]{1,0:T(8,128)(2,1)} %get-tuple-element.52.g_ref, bf16[1024,512]{1,0:T(8,128)(2,1)} %get-tuple-element.53.x_ref, bf16[9216,512]{1,0:T(8,128)(2,1)} %w_ref.31, ...), custom_call_target="tpu_custom_call" | custom-call | flops 1 | bytes 1 | tf_op jit(solution)/shard_map/final_first/pallas_call | solution.py:389
  286.4 5.9 %piece.26.refs_0_.a_ref = f32[2,384,512]{2,1,0:T(8,128)} custom-call(s32[31]{0:T(128)} %stack.124.idx_ref.table_ref, bf16[512,9216]{1,0:T(8,128)(2,1)} %own_ref.31, bf16[1024,512]{1,0:T(8,128)(2,1)} %get-tuple-element.52.g_ref, bf16[1024,512]{1,0:T(8,128)(2,1)} %get-tuple-element.53.x_ref, bf16[9216,512]{1,0:T(8,128)(2,1)} %w_ref.31, ...), custom_call_target="tpu_custom_call" | custom-call | flops 1 | bytes 1 | tf_op jit(solution)/shard_map/piece/pallas_call | solution.py:299
  300.7 6.1 %collective-permute-done.32.refs_1_ = f32[2,384,512]{2,1,0:T(8,128)} collective-permute-done((f32[2,384,512]{2,1,0:T(8,128)}, f32[2,384,512]{2,1,0:T(8,128)}, u32[]{:S(2)}, u32[]{:S(2)}) %collective-permute-start.32) | collective-permute-done | bytes 1572896 | tf_op jit(solution)/shard_map/ppermute | solution.py:594
  306.8 6.0 %piece.27.a_ref = f32[2,384,512]{2,1,0:T(8,128)} custom-call(s32[31]{0:T(128)} %stack.124.idx_ref.table_ref, bf16[512,9216]{1,0:T(8,128)(2,1)} %own_ref.31, bf16[1024,512]{1,0:T(8,128)(2,1)} %get-tuple-element.52.g_ref, bf16[1024,512]{1,0:T(8,128)(2,1)} %get-tuple-element.53.x_ref, bf16[9216,512]{1,0:T(8,128)(2,1)} %w_ref.31, ...), custom_call_target="tpu_custom_call" | custom-call | flops 1 | bytes 1 | tf_op jit(solution)/shard_map/piece/pallas_call | solution.py:299
  (94 shorter events, 107.9 us)
Async XLA Ops:
  10.4 24.1 %collective-permute-start.4 = (f32[512,384]{1,0:T(8,128)}, f32[512,384]{1,0:T(8,128)S(1)}, u32[]{:S(2)}, u32[]{:S(2)}) collective-permute-start(f32[512,384]{1,0:T(8,128)} %get-tuple-element.46), channel_id=1, source_target_pairs={{0,4},{4,0},{8,12},{12,8},{16,20},{20,16},{24,28},{28,24},{1,5},{5... | collective-permute-start | bytes 2359304 | tf_op jit(solution)/shard_map/ppermute | solution.py:451
  19.3 25.5 %collective-permute-start.7 = (f32[512,384]{1,0:T(8,128)}, f32[512,384]{1,0:T(8,128)S(1)}, u32[]{:S(2)}, u32[]{:S(2)}) collective-permute-start(f32[512,384]{1,0:T(8,128)} %get-tuple-element.51), channel_id=1, source_target_pairs={{0,8},{4,12},{24,16},{28,20},{1,9},{5,13},{25,17},{29,21},{2,10},{... | collective-permute-start | bytes 2359304 | tf_op jit(solution)/shard_map/ppermute | solution.py:534
  27.9 27.1 %collective-permute-start.9 = (f32[512,384]{1,0:T(8,128)}, f32[512,384]{1,0:T(8,128)}, u32[]{:S(2)}, u32[]{:S(2)}) collective-permute-start(f32[512,384]{1,0:T(8,128)} %get-tuple-element.55), channel_id=1, source_target_pairs={{0,4},{4,0},{8,12},{12,8},{16,20},{20,16},{24,28},{28,24},{1,5},{5... | collective-permute-start | bytes 2359304 | tf_op jit(solution)/shard_map/ppermute | solution.py:451
  34.6 20.4 %collective-permute-start.10 = (f32[256,512]{1,0:T(8,128)}, f32[256,512]{1,0:T(8,128)}, u32[]{:S(2)}, u32[]{:S(2)}) collective-permute-start(f32[256,512]{1,0:T(8,128)} %get-tuple-element.43), channel_id=1, source_target_pairs={{0,8},{4,12},{24,16},{28,20},{1,9},{5,13},{25,17},{29,21},{2,10},{... | collective-permute-start | bytes 1572872 | tf_op jit(solution)/shard_map/ppermute | solution.py:534
  52.2 33.3 %collective-permute-start.8 = (f32[1024,384]{1,0:T(8,128)}, f32[1024,384]{1,0:T(8,128)}, u32[]{:S(2)}, u32[]{:S(2)}) collective-permute-start(f32[1024,384]{1,0:T(8,128)} %get-tuple-element.54), channel_id=1, source_target_pairs={{0,4},{4,0},{8,12},{12,8},{16,20},{20,16},{24,28},{28,24},{1,5},{5... | collective-permute-start | bytes 4718600 | tf_op jit(solution)/shard_map/ppermute | solution.py:451
  53.7 43.9 %collective-permute-start.12 = (f32[2,384,512]{2,1,0:T(8,128)}, f32[2,384,512]{2,1,0:T(8,128)}, u32[]{:S(2)}, u32[]{:S(2)}) collective-permute-start(f32[2,384,512]{2,1,0:T(8,128)} %get-tuple-element.56.refs_1_), channel_id=1, source_target_pairs={{0,8},{4,12},{24,16},{28,20},{1,9},{5,13},{25,17},{29,21},{2,10},{... | collective-permute-start | bytes 4718600 | tf_op jit(solution)/shard_map/ppermute | solution.py:534
  72.2 54.7 %collective-permute-start.11 = (f32[2,384,512]{2,1,0:T(8,128)}, f32[2,384,512]{2,1,0:T(8,128)}, u32[]{:S(2)}, u32[]{:S(2)}) collective-permute-start(f32[2,384,512]{2,1,0:T(8,128)} %piece.14.refs_4_.refs_2_), channel_id=1, source_target_pairs={{0,8},{4,12},{24,16},{28,20},{1,9},{5,13},{25,17},{29,21},{2,10},{... | collective-permute-start | bytes 4718600 | tf_op jit(solution)/shard_map/ppermute | solution.py:534
  94.2 39.5 %collective-permute-start.16 = (f32[2,384,512]{2,1,0:T(8,128)}, f32[2,384,512]{2,1,0:T(8,128)}, u32[]{:S(2)}, u32[]{:S(2)}) collective-permute-start(f32[2,384,512]{2,1,0:T(8,128)} %piece.15.refs_4_), channel_id=1, source_target_pairs={{8,12},{12,8},{16,20},{20,16},{9,13},{13,9},{17,21},{21,17},{10,14... | collective-permute-start | bytes 4718600 | tf_op jit(solution)/shard_map/ppermute | solution.py:451
  104.3 57.9 %collective-permute-start.19 = (f32[2,384,512]{2,1,0:T(8,128)}, f32[2,384,512]{2,1,0:T(8,128)}, u32[]{:S(2)}, u32[]{:S(2)}) collective-permute-start(f32[2,384,512]{2,1,0:T(8,128)} %get-tuple-element.62.refs_2_), channel_id=1, source_target_pairs={{8,16},{12,20},{16,8},{20,12},{9,17},{13,21},{17,9},{21,13},{10,18... | collective-permute-start | bytes 4718600 | tf_op jit(solution)/shard_map/ppermute | solution.py:594
  106.7 55.6 %collective-permute-start.18 = (f32[2,384,512]{2,1,0:T(8,128)}, f32[2,384,512]{2,1,0:T(8,128)}, u32[]{:S(2)}, u32[]{:S(2)}) collective-permute-start(f32[2,384,512]{2,1,0:T(8,128)} %get-tuple-element.62.refs_2_), channel_id=1, source_target_pairs={{0,8},{4,12},{24,16},{28,20},{1,9},{5,13},{25,17},{29,21},{2,10},{... | collective-permute-start | bytes 4718600 | tf_op jit(solution)/shard_map/ppermute | solution.py:534
  108.0 54.3 %collective-permute-start.17 = (f32[1024,384]{1,0:T(8,128)}, f32[1024,384]{1,0:T(8,128)}, u32[]{:S(2)}, u32[]{:S(2)}) collective-permute-start(f32[1024,384]{1,0:T(8,128)} %get-tuple-element.65), channel_id=1, source_target_pairs={{0,4},{4,0},{8,12},{12,8},{16,20},{20,16},{24,28},{28,24},{1,5},{5... | collective-permute-start | bytes 4718600 | tf_op jit(solution)/shard_map/ppermute | solution.py:451
  139.7 54.7 %collective-permute-start.22 = (f32[2,384,512]{2,1,0:T(8,128)}, f32[2,384,512]{2,1,0:T(8,128)}, u32[]{:S(2)}, u32[]{:S(2)}) collective-permute-start(f32[2,384,512]{2,1,0:T(8,128)} %piece.17.refs_0_), channel_id=1, source_target_pairs={{0,8},{4,12},{24,16},{28,20},{1,9},{5,13},{25,17},{29,21},{2,10},{... | collective-permute-start | bytes 4718600 | tf_op jit(solution)/shard_map/ppermute | solution.py:534
  141.0 53.4 %collective-permute-start.21 = (f32[2,384,512]{2,1,0:T(8,128)}, f32[2,384,512]{2,1,0:T(8,128)}, u32[]{:S(2)}, u32[]{:S(2)}) collective-permute-start(f32[2,384,512]{2,1,0:T(8,128)} %piece.17.refs_0_), channel_id=1, source_target_pairs={{8,16},{12,20},{16,8},{20,12},{9,17},{13,21},{17,9},{21,13},{10,18... | collective-permute-start | bytes 4718600 | tf_op jit(solution)/shard_map/ppermute | solution.py:594
  169.2 58.9 %collective-permute-start.25 = (f32[2,384,512]{2,1,0:T(8,128)}, f32[2,384,512]{2,1,0:T(8,128)}, u32[]{:S(2)}, u32[]{:S(2)}) collective-permute-start(f32[2,384,512]{2,1,0:T(8,128)} %get-tuple-element.67.refs_2_), channel_id=1, source_target_pairs={{0,8},{4,12},{24,16},{28,20},{1,9},{5,13},{25,17},{29,21},{2,10},{... | collective-permute-start | bytes 4718600 | tf_op jit(solution)/shard_map/ppermute | solution.py:534
  170.5 57.6 %collective-permute-start.24 = (f32[2,384,512]{2,1,0:T(8,128)}, f32[2,384,512]{2,1,0:T(8,128)}, u32[]{:S(2)}, u32[]{:S(2)}) collective-permute-start(f32[2,384,512]{2,1,0:T(8,128)} %get-tuple-element.67.refs_2_), channel_id=1, source_target_pairs={{8,16},{12,20},{16,8},{20,12},{9,17},{13,21},{17,9},{21,13},{10,18... | collective-permute-start | bytes 4718600 | tf_op jit(solution)/shard_map/ppermute | solution.py:594
  172.9 55.2 %collective-permute-start.20 = (f32[1536,384]{1,0:T(8,128)}, f32[1536,384]{1,0:T(8,128)}, u32[]{:S(2)}, u32[]{:S(2)}) collective-permute-start(f32[1536,384]{1,0:T(8,128)} %get-tuple-element.66), channel_id=1, source_target_pairs={{0,4},{4,0},{8,12},{12,8},{16,20},{20,16},{24,28},{28,24},{1,5},{5... | collective-permute-start | bytes 7077896 | tf_op jit(solution)/shard_map/ppermute | solution.py:451
  200.5 61.3 %collective-permute-start.23 = (f32[2,384,512]{2,1,0:T(8,128)}, f32[2,384,512]{2,1,0:T(8,128)}, u32[]{:S(2)}, u32[]{:S(2)}) collective-permute-start(f32[2,384,512]{2,1,0:T(8,128)} %piece.20.refs_2_), channel_id=1, source_target_pairs={{0,8},{4,12},{24,16},{28,20},{8,0},{12,4},{16,24},{20,28},{1,9},{5... | collective-permute-start | bytes 4718600 | tf_op jit(solution)/shard_map/ppermute | solution.py:582
  206.5 37.5 %collective-permute-start.26 = (f32[2,384,512]{2,1,0:T(8,128)}, f32[2,384,512]{2,1,0:T(8,128)}, u32[]{:S(2)}, u32[]{:S(2)}) collective-permute-start(f32[2,384,512]{2,1,0:T(8,128)} %piece.21.refs_3_), channel_id=1, source_target_pairs={{8,16},{12,20},{16,8},{20,12},{9,17},{13,21},{17,9},{21,13},{10,18... | collective-permute-start | bytes 4718600 | tf_op jit(solution)/shard_map/ppermute | solution.py:594
  234.2 61.2 %collective-permute-start.31 = (f32[2,384,512]{2,1,0:T(8,128)}, f32[2,384,512]{2,1,0:T(8,128)}, u32[]{:S(2)}, u32[]{:S(2)}) collective-permute-start(f32[2,384,512]{2,1,0:T(8,128)} %piece.22.refs_4_), channel_id=1, source_target_pairs={{0,8},{4,12},{24,16},{28,20},{8,0},{12,4},{16,24},{20,28},{1,9},{5... | collective-permute-start | bytes 4718600 | tf_op jit(solution)/shard_map/ppermute | solution.py:582
  240.9 35.4 %collective-permute-start.28 = (f32[1024,384]{1,0:T(8,128)}, f32[1024,384]{1,0:T(8,128)}, u32[]{:S(2)}, u32[]{:S(2)}) collective-permute-start(f32[1024,384]{1,0:T(8,128)} %get-tuple-element.71), channel_id=1, source_target_pairs={{0,4},{4,0},{8,12},{12,8},{16,20},{20,16},{24,28},{28,24},{1,5},{5... | collective-permute-start | bytes 4718600 | tf_op jit(solution)/shard_map/ppermute | solution.py:451
  241.4 36.4 %collective-permute-start.29 = (f32[2,384,512]{2,1,0:T(8,128)}, f32[2,384,512]{2,1,0:T(8,128)}, u32[]{:S(2)}, u32[]{:S(2)}) collective-permute-start(f32[2,384,512]{2,1,0:T(8,128)} %get-tuple-element.68.refs_3_), channel_id=1, source_target_pairs={{8,16},{12,20},{16,8},{20,12},{9,17},{13,21},{17,9},{21,13},{10,18... | collective-permute-start | bytes 4718600 | tf_op jit(solution)/shard_map/ppermute | solution.py:594
  273.8 33.0 %collective-permute-start.32 = (f32[2,384,512]{2,1,0:T(8,128)}, f32[2,384,512]{2,1,0:T(8,128)}, u32[]{:S(2)}, u32[]{:S(2)}) collective-permute-start(f32[2,384,512]{2,1,0:T(8,128)} %piece.25.refs_1_), channel_id=1, source_target_pairs={{8,16},{12,20},{16,8},{20,12},{9,17},{13,21},{17,9},{21,13},{10,18... | collective-permute-start | bytes 4718600 | tf_op jit(solution)/shard_map/ppermute | solution.py:594
  276.2 41.8 %collective-permute-start.34 = (f32[2,256,512]{2,1,0:T(8,128)}, f32[2,256,512]{2,1,0:T(8,128)}, u32[]{:S(2)}, u32[]{:S(2)}) collective-permute-start(f32[2,256,512]{2,1,0:T(8,128)} %get-tuple-element.69.refs_2_), channel_id=1, source_target_pairs={{0,8},{4,12},{24,16},{28,20},{8,0},{12,4},{16,24},{20,28},{1,9},{5... | collective-permute-start | bytes 3145736 | tf_op jit(solution)/shard_map/ppermute | solution.py:582
  277.9 46.7 %collective-permute-start.33 = (f32[2,128,512]{2,1,0:T(8,128)}, f32[2,128,512]{2,1,0:T(8,128)}, u32[]{:S(2)}, u32[]{:S(2)}) collective-permute-start(f32[2,128,512]{2,1,0:T(8,128)} %get-tuple-element.77), channel_id=1, source_target_pairs={{0,8},{4,12},{24,16},{28,20},{8,0},{12,4},{16,24},{20,28},{1,9},{5... | collective-permute-start | bytes 1572872 | tf_op jit(solution)/shard_map/ppermute | solution.py:582
  (22 other events, 200.1 us)

commit v9 on v8

--- a/solution.py
+++ b/solution.py
@@ -9,7 +9,7 @@
 
 PIECES = 3
 FLOPS = 100_000_000_000
-VMEM_LIMIT = 63 * 1024 * 1024
+VMEM_LIMIT = 64 * 1024 * 1024
 
 
 def contract_rows(left, right):

time: 328 us -> 327 us (level)
  transfers between devices with their start and end apart: 35 -> 35, of which waited for: 18 -> 19; matrix products, arithmetic and copies ran while one was open for 0% -> 0% of each run, Pallas kernels for 40% -> 40%
where the time goes in v9:
time: 327 us; the launch traced here: 326 us
  waiting for transfers between devices  143 us (44%)
  Pallas kernels  135 us (41%)
  starting transfers between devices  43.8 us (13%)
    pallas_call x14, Pallas kernels, piece(): pl.pallas_call(functools.partial(piece_kernel, scale, counts, inner_at),...  85.2 us
    ppermute x9, waiting for transfers between devices, send_in(): return lax.ppermute(array, 'dp', outer_to_inner)  69.8 us
    ppermute x4, waiting for transfers between devices, line_body(): lax.ppermute(array, 'dp', outer_to_inner + inner_to_outer)  28.5 us
    ppermute x8, waiting for transfers between devices, swap(): lax.ppermute(array, 'dp', [(2 * a + h, 2 * a + 1 - h) for a in planes for...  26.4 us
    pallas_call x1, Pallas kernels, input_partial(): pl.pallas_call(input_kernel, grid_spec=pltpu.PrefetchScalarGridSpec(num_s...  16.4 us
    ppermute x6, starting transfers between devices, line_body(): across[s - 2] = lax.ppermute(out, 'dp', inner_to_inner)  14.5 us
    ppermute x9, starting transfers between devices, send_in(): return lax.ppermute(array, 'dp', outer_to_inner)  11.5 us
    ppermute x8, waiting for transfers between devices, flip(): return lax.ppermute(array, 'blk', [(i, i ^ bit) for i in range(4)])  11.3 us
  transfers between devices with their start and end apart: 35, of which 19 were waited for; matrix products, arithmetic and copies ran while one was open for 0% of the time, Pallas kernels for 40%

profile of v9, /device:TPU:16, one launch (start us, length us, event | category | flops | bytes accessed | tf_op | source)
XLA Modules:
  0.0 326.0 jit_solution(1054626462874365588)
XLA Ops:
  20.6 7.4 %collective-permute-done.5.refs_1_ = f32[512,256]{1,0:T(8,128)S(1)} collective-permute-done((f32[512,256]{1,0:T(8,128)}, f32[512,256]{1,0:T(8,128)S(1)}, u32[]{:S(2)}, u32[]{:S(2)}) %collective-permute-start.5) | collective-permute-done | bytes 524320 | tf_op jit(solution)/shard_map/ppermute | solution.py:534
  36.8 8.1 %collective-permute-done.7.refs_0_ = f32[512,384]{1,0:T(8,128)} collective-permute-done((f32[512,384]{1,0:T(8,128)}, f32[512,384]{1,0:T(8,128)}, u32[]{:S(2)}, u32[]{:S(2)}) %collective-permute-start.7) | collective-permute-done | bytes 786464 | tf_op jit(solution)/shard_map/ppermute | solution.py:534
  44.9 6.5 %first_piece.1 = (f32[2,384,512]{2,1,0:T(8,128)}, bf16[1024,512]{1,0:T(8,128)(2,1)}, bf16[1024,512]{1,0:T(8,128)(2,1)}, f32[1024,384]{1,0:T(8,128)}) custom-call(s32[31]{0:T(128)} %stack.124.idx_ref.table_ref, bf16[512,9216]{1,0:T(8,128)(2,1)} %own_ref.31, bf16[9216,512]{1,0:T(8,128)(2,1)} %w_ref.31, f32[512,384]{1,0:T(8,128)} %collective-permute-done.4.partner_ref.refs_1_, ...), custom_call_target="tpu_custom_call" | custom-call | flops 1 | bytes 1 | tf_op jit(solution)/shard_map/first_piece/pallas_call | solution.py:339
  61.5 10.7 %collective-permute-done.14.refs_2_ = f32[256,512]{1,0:T(8,128)S(1)} collective-permute-done((f32[256,512]{1,0:T(8,128)}, f32[256,512]{1,0:T(8,128)S(1)}, u32[]{:S(2)}, u32[]{:S(2)}) %collective-permute-start.14) | collective-permute-done | bytes 524320 | tf_op jit(solution)/shard_map/ppermute | solution.py:454
  75.9 8.8 %collective-permute-done.8.refs_5_.refs_0_ = f32[1024,384]{1,0:T(8,128)} collective-permute-done((f32[1024,384]{1,0:T(8,128)}, f32[1024,384]{1,0:T(8,128)}, u32[]{:S(2)}, u32[]{:S(2)}) %collective-permute-start.8) | collective-permute-done | bytes 1572896 | tf_op jit(solution)/shard_map/ppermute | solution.py:451
  96.8 6.7 %piece.16 = (f32[2,384,512]{2,1,0:T(8,128)}, f32[1024,384]{1,0:T(8,128)}) custom-call(s32[31]{0:T(128)} %stack.124.idx_ref.table_ref, bf16[512,9216]{1,0:T(8,128)(2,1)} %own_ref.31, bf16[1024,512]{1,0:T(8,128)(2,1)} %get-tuple-element.52.g_ref, bf16[1024,512]{1,0:T(8,128)(2,1)} %get-tuple-element.53.x_ref, bf16[9216,512]{1,0:T(8,128)(2,1)} %w_ref.31, ...), custom_call_target="tpu_custom_call" | custom-call | flops 99999997952 | bytes 1 | tf_op jit(solution)/shard_map/piece/pallas_call | solution.py:299
  107.7 18.5 %collective-permute-done.11.refs_1_ = f32[2,384,512]{2,1,0:T(8,128)} collective-permute-done((f32[2,384,512]{2,1,0:T(8,128)}, f32[2,384,512]{2,1,0:T(8,128)}, u32[]{:S(2)}, u32[]{:S(2)}) %collective-permute-start.11) | collective-permute-done | bytes 1572896 | tf_op jit(solution)/shard_map/ppermute | solution.py:534
  126.2 6.7 %collective-permute-done.16.refs_3_.refs_1_ = f32[2,384,512]{2,1,0:T(8,128)} collective-permute-done((f32[2,384,512]{2,1,0:T(8,128)}, f32[2,384,512]{2,1,0:T(8,128)}, u32[]{:S(2)}, u32[]{:S(2)}) %collective-permute-start.16) | collective-permute-done | bytes 1572896 | tf_op jit(solution)/shard_map/ppermute | solution.py:451
  142.6 16.4 %input_partial.1 = (f32[256,512]{1,0:T(8,128)}, f32[256,512]{1,0:T(8,128)}) custom-call(s32[1]{0:T(128)} %bitcast.blk_ref, bf16[512,512]{1,0:T(8,128)(2,1)} %grads_ref.7, bf16[512,9216]{1,0:T(8,128)(2,1)} %own_ref.31, bf16[9216,512]{1,0:T(8,128)(2,1)} %w_ref.31, bf16[9216,512]{1,0:T(8,128)(2,1)} %in_rows_ref.1, f32[2,384,512]{2,1,0:T(8,128)} %piece.17.refs_0_), custom_call_target="tpu_custom_call" | custom-call | flops 1 | bytes 1 | tf_op jit(solution)/shard_map/input_partial/pallas_call | solution.py:174
  161.2 7.0 %piece.18 = (f32[2,384,512]{2,1,0:T(8,128)}, f32[1536,384]{1,0:T(8,128)}) custom-call(s32[31]{0:T(128)} %stack.124.idx_ref.table_ref, bf16[512,9216]{1,0:T(8,128)(2,1)} %own_ref.31, bf16[1024,512]{1,0:T(8,128)(2,1)} %get-tuple-element.52.g_ref, bf16[1024,512]{1,0:T(8,128)(2,1)} %get-tuple-element.53.x_ref, bf16[9216,512]{1,0:T(8,128)(2,1)} %w_ref.31, ...), custom_call_target="tpu_custom_call" | custom-call | flops 99999997952 | bytes 1 | tf_op jit(solution)/shard_map/piece/pallas_call | solution.py:299
  173.5 5.9 %piece.19.refs_3_.inner_ref = f32[2,384,512]{2,1,0:T(8,128)} custom-call(s32[31]{0:T(128)} %stack.124.idx_ref.table_ref, bf16[512,9216]{1,0:T(8,128)(2,1)} %own_ref.31, bf16[1024,512]{1,0:T(8,128)(2,1)} %get-tuple-element.58.g_ref, bf16[1024,512]{1,0:T(8,128)(2,1)} %get-tuple-element.59.x_ref, bf16[9216,512]{1,0:T(8,128)(2,1)} %w_ref.31, ...), custom_call_target="tpu_custom_call" | custom-call | flops 1 | bytes 1 | tf_op jit(solution)/shard_map/piece/pallas_call | solution.py:299
  179.4 14.2 %collective-permute-done.22.refs_5_.refs_1_ = f32[2,384,512]{2,1,0:T(8,128)} collective-permute-done((f32[2,384,512]{2,1,0:T(8,128)}, f32[2,384,512]{2,1,0:T(8,128)}, u32[]{:S(2)}, u32[]{:S(2)}) %collective-permute-start.22) | collective-permute-done | bytes 1572896 | tf_op jit(solution)/shard_map/ppermute | solution.py:534
  193.6 6.1 %piece.20.refs_2_ = f32[2,384,512]{2,1,0:T(8,128)} custom-call(s32[31]{0:T(128)} %stack.124.idx_ref.table_ref, bf16[512,9216]{1,0:T(8,128)(2,1)} %own_ref.31, bf16[1024,512]{1,0:T(8,128)(2,1)} %get-tuple-element.52.g_ref, bf16[1024,512]{1,0:T(8,128)(2,1)} %get-tuple-element.53.x_ref, bf16[9216,512]{1,0:T(8,128)(2,1)} %w_ref.31, ...), custom_call_target="tpu_custom_call" | custom-call | flops 1 | bytes 1 | tf_op jit(solution)/shard_map/piece/pallas_call | solution.py:299
  199.8 5.9 %piece.21.refs_3_ = f32[2,384,512]{2,1,0:T(8,128)} custom-call(s32[31]{0:T(128)} %stack.124.idx_ref.table_ref, bf16[512,9216]{1,0:T(8,128)(2,1)} %own_ref.31, bf16[1024,512]{1,0:T(8,128)(2,1)} %get-tuple-element.52.g_ref, bf16[1024,512]{1,0:T(8,128)(2,1)} %get-tuple-element.53.x_ref, bf16[9216,512]{1,0:T(8,128)(2,1)} %w_ref.31, ...), custom_call_target="tpu_custom_call" | custom-call | flops 99999997952 | bytes 1 | tf_op jit(solution)/shard_map/piece/pallas_call | solution.py:299
  208.1 19.3 %collective-permute-done.25.refs_5_.refs_3_ = f32[2,384,512]{2,1,0:T(8,128)} collective-permute-done((f32[2,384,512]{2,1,0:T(8,128)}, f32[2,384,512]{2,1,0:T(8,128)}, u32[]{:S(2)}, u32[]{:S(2)}) %collective-permute-start.25) | collective-permute-done | bytes 1572896 | tf_op jit(solution)/shard_map/ppermute | solution.py:534
  227.3 6.2 %piece.22.refs_4_ = f32[2,384,512]{2,1,0:T(8,128)} custom-call(s32[31]{0:T(128)} %stack.124.idx_ref.table_ref, bf16[512,9216]{1,0:T(8,128)(2,1)} %own_ref.31, bf16[1024,512]{1,0:T(8,128)(2,1)} %get-tuple-element.52.g_ref, bf16[1024,512]{1,0:T(8,128)(2,1)} %get-tuple-element.53.x_ref, bf16[9216,512]{1,0:T(8,128)(2,1)} %w_ref.31, ...), custom_call_target="tpu_custom_call" | custom-call | flops 1 | bytes 1 | tf_op jit(solution)/shard_map/piece/pallas_call | solution.py:299
  233.5 6.6 %piece.23 = (f32[2,384,512]{2,1,0:T(8,128)}, f32[1024,384]{1,0:T(8,128)}) custom-call(s32[31]{0:T(128)} %stack.124.idx_ref.table_ref, bf16[512,9216]{1,0:T(8,128)(2,1)} %own_ref.31, bf16[1024,512]{1,0:T(8,128)(2,1)} %get-tuple-element.52.g_ref, bf16[1024,512]{1,0:T(8,128)(2,1)} %get-tuple-element.53.x_ref, bf16[9216,512]{1,0:T(8,128)(2,1)} %w_ref.31, ...), custom_call_target="tpu_custom_call" | custom-call | flops 99999997952 | bytes 1 | tf_op jit(solution)/shard_map/piece/pallas_call | solution.py:299
  243.2 17.8 %collective-permute-done.23.refs_5_.refs_1_.outer_ref = f32[2,384,512]{2,1,0:T(8,128)} collective-permute-done((f32[2,384,512]{2,1,0:T(8,128)}, f32[2,384,512]{2,1,0:T(8,128)}, u32[]{:S(2)}, u32[]{:S(2)}) %collective-permute-start.23) | collective-permute-done | bytes 1572896 | tf_op jit(solution)/shard_map/ppermute | solution.py:582
  261.0 6.2 %piece.24 = (f32[2,256,512]{2,1,0:T(8,128)}, f32[2,128,512]{2,1,0:T(8,128)}) custom-call(s32[31]{0:T(128)} %stack.124.idx_ref.table_ref, bf16[512,9216]{1,0:T(8,128)(2,1)} %own_ref.31, bf16[1024,512]{1,0:T(8,128)(2,1)} %get-tuple-element.52.g_ref, bf16[1024,512]{1,0:T(8,128)(2,1)} %get-tuple-element.53.x_ref, bf16[9216,512]{1,0:T(8,128)(2,1)} %w_ref.31, ...), custom_call_target="tpu_custom_call" | custom-call | flops 1 | bytes 1 | tf_op jit(solution)/shard_map/piece/pallas_call | solution.py:299
  267.2 5.9 %piece.25.refs_1_ = f32[2,384,512]{2,1,0:T(8,128)} custom-call(s32[31]{0:T(128)} %stack.124.idx_ref.table_ref, bf16[512,9216]{1,0:T(8,128)(2,1)} %own_ref.31, bf16[1024,512]{1,0:T(8,128)(2,1)} %get-tuple-element.52.g_ref, bf16[1024,512]{1,0:T(8,128)(2,1)} %get-tuple-element.53.x_ref, bf16[9216,512]{1,0:T(8,128)(2,1)} %w_ref.31, ...), custom_call_target="tpu_custom_call" | custom-call | flops 99999997952 | bytes 1 | tf_op jit(solution)/shard_map/piece/pallas_call | solution.py:299
  279.1 6.6 %final_first.1 = (f32[1152,512]{1,0:T(8,128)}, f32[1152,512]{1,0:T(8,128)}) custom-call(s32[31]{0:T(128)} %stack.124.idx_ref.table_ref, bf16[512,9216]{1,0:T(8,128)(2,1)} %own_ref.31, bf16[1024,512]{1,0:T(8,128)(2,1)} %get-tuple-element.52.g_ref, bf16[1024,512]{1,0:T(8,128)(2,1)} %get-tuple-element.53.x_ref, bf16[9216,512]{1,0:T(8,128)(2,1)} %w_ref.31, ...), custom_call_target="tpu_custom_call" | custom-call | flops 1 | bytes 1 | tf_op jit(solution)/shard_map/final_first/pallas_call | solution.py:389
  285.6 5.9 %piece.26.refs_0_.a_ref = f32[2,384,512]{2,1,0:T(8,128)} custom-call(s32[31]{0:T(128)} %stack.124.idx_ref.table_ref, bf16[512,9216]{1,0:T(8,128)(2,1)} %own_ref.31, bf16[1024,512]{1,0:T(8,128)(2,1)} %get-tuple-element.52.g_ref, bf16[1024,512]{1,0:T(8,128)(2,1)} %get-tuple-element.53.x_ref, bf16[9216,512]{1,0:T(8,128)(2,1)} %w_ref.31, ...), custom_call_target="tpu_custom_call" | custom-call | flops 1 | bytes 1 | tf_op jit(solution)/shard_map/piece/pallas_call | solution.py:299
  299.2 6.6 %collective-permute-done.32.refs_1_ = f32[2,384,512]{2,1,0:T(8,128)} collective-permute-done((f32[2,384,512]{2,1,0:T(8,128)}, f32[2,384,512]{2,1,0:T(8,128)}, u32[]{:S(2)}, u32[]{:S(2)}) %collective-permute-start.32) | collective-permute-done | bytes 1572896 | tf_op jit(solution)/shard_map/ppermute | solution.py:594
  305.9 6.0 %piece.27.a_ref = f32[2,384,512]{2,1,0:T(8,128)} custom-call(s32[31]{0:T(128)} %stack.124.idx_ref.table_ref, bf16[512,9216]{1,0:T(8,128)(2,1)} %own_ref.31, bf16[1024,512]{1,0:T(8,128)(2,1)} %get-tuple-element.52.g_ref, bf16[1024,512]{1,0:T(8,128)(2,1)} %get-tuple-element.53.x_ref, bf16[9216,512]{1,0:T(8,128)(2,1)} %w_ref.31, ...), custom_call_target="tpu_custom_call" | custom-call | flops 1 | bytes 1 | tf_op jit(solution)/shard_map/piece/pallas_call | solution.py:299
  (82 shorter events, 108.5 us)
Async XLA Ops:
  10.4 24.3 %collective-permute-start.4 = (f32[512,384]{1,0:T(8,128)}, f32[512,384]{1,0:T(8,128)}, u32[]{:S(2)}, u32[]{:S(2)}) collective-permute-start(f32[512,384]{1,0:T(8,128)} %get-tuple-element.46), channel_id=1, source_target_pairs={{0,4},{4,0},{8,12},{12,8},{16,20},{20,16},{24,28},{28,24},{1,5},{5... | collective-permute-start | bytes 2359304 | tf_op jit(solution)/shard_map/ppermute | solution.py:451
  19.3 25.6 %collective-permute-start.7 = (f32[512,384]{1,0:T(8,128)}, f32[512,384]{1,0:T(8,128)}, u32[]{:S(2)}, u32[]{:S(2)}) collective-permute-start(f32[512,384]{1,0:T(8,128)} %get-tuple-element.51), channel_id=1, source_target_pairs={{0,8},{4,12},{24,16},{28,20},{1,9},{5,13},{25,17},{29,21},{2,10},{... | collective-permute-start | bytes 2359304 | tf_op jit(solution)/shard_map/ppermute | solution.py:534
  27.9 26.7 %collective-permute-start.9 = (f32[512,384]{1,0:T(8,128)}, f32[512,384]{1,0:T(8,128)}, u32[]{:S(2)}, u32[]{:S(2)}) collective-permute-start(f32[512,384]{1,0:T(8,128)} %get-tuple-element.55), channel_id=1, source_target_pairs={{0,4},{4,0},{8,12},{12,8},{16,20},{20,16},{24,28},{28,24},{1,5},{5... | collective-permute-start | bytes 2359304 | tf_op jit(solution)/shard_map/ppermute | solution.py:451
  35.5 19.1 %collective-permute-start.10 = (f32[256,512]{1,0:T(8,128)}, f32[256,512]{1,0:T(8,128)}, u32[]{:S(2)}, u32[]{:S(2)}) collective-permute-start(f32[256,512]{1,0:T(8,128)} %get-tuple-element.43), channel_id=1, source_target_pairs={{0,8},{4,12},{24,16},{28,20},{1,9},{5,13},{25,17},{29,21},{2,10},{... | collective-permute-start | bytes 1572872 | tf_op jit(solution)/shard_map/ppermute | solution.py:534
  51.4 33.2 %collective-permute-start.8 = (f32[1024,384]{1,0:T(8,128)}, f32[1024,384]{1,0:T(8,128)}, u32[]{:S(2)}, u32[]{:S(2)}) collective-permute-start(f32[1024,384]{1,0:T(8,128)} %get-tuple-element.54), channel_id=1, source_target_pairs={{0,4},{4,0},{8,12},{12,8},{16,20},{20,16},{24,28},{28,24},{1,5},{5... | collective-permute-start | bytes 4718600 | tf_op jit(solution)/shard_map/ppermute | solution.py:451
  53.0 43.8 %collective-permute-start.12 = (f32[2,384,512]{2,1,0:T(8,128)}, f32[2,384,512]{2,1,0:T(8,128)}, u32[]{:S(2)}, u32[]{:S(2)}) collective-permute-start(f32[2,384,512]{2,1,0:T(8,128)} %get-tuple-element.56.refs_1_), channel_id=1, source_target_pairs={{0,8},{4,12},{24,16},{28,20},{1,9},{5,13},{25,17},{29,21},{2,10},{... | collective-permute-start | bytes 4718600 | tf_op jit(solution)/shard_map/ppermute | solution.py:534
  73.0 53.2 %collective-permute-start.11 = (f32[2,384,512]{2,1,0:T(8,128)}, f32[2,384,512]{2,1,0:T(8,128)}, u32[]{:S(2)}, u32[]{:S(2)}) collective-permute-start(f32[2,384,512]{2,1,0:T(8,128)} %piece.14.refs_4_.refs_2_), channel_id=1, source_target_pairs={{0,8},{4,12},{24,16},{28,20},{1,9},{5,13},{25,17},{29,21},{2,10},{... | collective-permute-start | bytes 4718600 | tf_op jit(solution)/shard_map/ppermute | solution.py:534
  93.3 39.5 %collective-permute-start.16 = (f32[2,384,512]{2,1,0:T(8,128)}, f32[2,384,512]{2,1,0:T(8,128)}, u32[]{:S(2)}, u32[]{:S(2)}) collective-permute-start(f32[2,384,512]{2,1,0:T(8,128)} %piece.15.refs_4_), channel_id=1, source_target_pairs={{8,12},{12,8},{16,20},{20,16},{9,13},{13,9},{17,21},{21,17},{10,14... | collective-permute-start | bytes 4718600 | tf_op jit(solution)/shard_map/ppermute | solution.py:451
  103.5 57.8 %collective-permute-start.19 = (f32[2,384,512]{2,1,0:T(8,128)}, f32[2,384,512]{2,1,0:T(8,128)}, u32[]{:S(2)}, u32[]{:S(2)}) collective-permute-start(f32[2,384,512]{2,1,0:T(8,128)} %get-tuple-element.62.refs_2_), channel_id=1, source_target_pairs={{8,16},{12,20},{16,8},{20,12},{9,17},{13,21},{17,9},{21,13},{10,18... | collective-permute-start | bytes 4718600 | tf_op jit(solution)/shard_map/ppermute | solution.py:594
  105.8 55.4 %collective-permute-start.18 = (f32[2,384,512]{2,1,0:T(8,128)}, f32[2,384,512]{2,1,0:T(8,128)}, u32[]{:S(2)}, u32[]{:S(2)}) collective-permute-start(f32[2,384,512]{2,1,0:T(8,128)} %get-tuple-element.62.refs_2_), channel_id=1, source_target_pairs={{0,8},{4,12},{24,16},{28,20},{1,9},{5,13},{25,17},{29,21},{2,10},{... | collective-permute-start | bytes 4718600 | tf_op jit(solution)/shard_map/ppermute | solution.py:534
  107.1 54.1 %collective-permute-start.17 = (f32[1024,384]{1,0:T(8,128)}, f32[1024,384]{1,0:T(8,128)}, u32[]{:S(2)}, u32[]{:S(2)}) collective-permute-start(f32[1024,384]{1,0:T(8,128)} %get-tuple-element.65), channel_id=1, source_target_pairs={{0,4},{4,0},{8,12},{12,8},{16,20},{20,16},{24,28},{28,24},{1,5},{5... | collective-permute-start | bytes 4718600 | tf_op jit(solution)/shard_map/ppermute | solution.py:451
  138.8 54.8 %collective-permute-start.22 = (f32[2,384,512]{2,1,0:T(8,128)}, f32[2,384,512]{2,1,0:T(8,128)}, u32[]{:S(2)}, u32[]{:S(2)}) collective-permute-start(f32[2,384,512]{2,1,0:T(8,128)} %piece.17.refs_0_), channel_id=1, source_target_pairs={{0,8},{4,12},{24,16},{28,20},{1,9},{5,13},{25,17},{29,21},{2,10},{... | collective-permute-start | bytes 4718600 | tf_op jit(solution)/shard_map/ppermute | solution.py:534
  140.1 53.5 %collective-permute-start.21 = (f32[2,384,512]{2,1,0:T(8,128)}, f32[2,384,512]{2,1,0:T(8,128)}, u32[]{:S(2)}, u32[]{:S(2)}) collective-permute-start(f32[2,384,512]{2,1,0:T(8,128)} %piece.17.refs_0_), channel_id=1, source_target_pairs={{8,16},{12,20},{16,8},{20,12},{9,17},{13,21},{17,9},{21,13},{10,18... | collective-permute-start | bytes 4718600 | tf_op jit(solution)/shard_map/ppermute | solution.py:594
  168.2 59.1 %collective-permute-start.25 = (f32[2,384,512]{2,1,0:T(8,128)}, f32[2,384,512]{2,1,0:T(8,128)}, u32[]{:S(2)}, u32[]{:S(2)}) collective-permute-start(f32[2,384,512]{2,1,0:T(8,128)} %get-tuple-element.67.refs_2_), channel_id=1, source_target_pairs={{0,8},{4,12},{24,16},{28,20},{1,9},{5,13},{25,17},{29,21},{2,10},{... | collective-permute-start | bytes 4718600 | tf_op jit(solution)/shard_map/ppermute | solution.py:534
  169.5 57.8 %collective-permute-start.24 = (f32[2,384,512]{2,1,0:T(8,128)}, f32[2,384,512]{2,1,0:T(8,128)}, u32[]{:S(2)}, u32[]{:S(2)}) collective-permute-start(f32[2,384,512]{2,1,0:T(8,128)} %get-tuple-element.67.refs_2_), channel_id=1, source_target_pairs={{8,16},{12,20},{16,8},{20,12},{9,17},{13,21},{17,9},{21,13},{10,18... | collective-permute-start | bytes 4718600 | tf_op jit(solution)/shard_map/ppermute | solution.py:594
  171.9 55.4 %collective-permute-start.20 = (f32[1536,384]{1,0:T(8,128)}, f32[1536,384]{1,0:T(8,128)}, u32[]{:S(2)}, u32[]{:S(2)}) collective-permute-start(f32[1536,384]{1,0:T(8,128)} %get-tuple-element.66), channel_id=1, source_target_pairs={{0,4},{4,0},{8,12},{12,8},{16,20},{20,16},{24,28},{28,24},{1,5},{5... | collective-permute-start | bytes 7077896 | tf_op jit(solution)/shard_map/ppermute | solution.py:451
  199.8 61.3 %collective-permute-start.23 = (f32[2,384,512]{2,1,0:T(8,128)}, f32[2,384,512]{2,1,0:T(8,128)}, u32[]{:S(2)}, u32[]{:S(2)}) collective-permute-start(f32[2,384,512]{2,1,0:T(8,128)} %piece.20.refs_2_), channel_id=1, source_target_pairs={{0,8},{4,12},{24,16},{28,20},{8,0},{12,4},{16,24},{20,28},{1,9},{5... | collective-permute-start | bytes 4718600 | tf_op jit(solution)/shard_map/ppermute | solution.py:582
  205.7 37.5 %collective-permute-start.26 = (f32[2,384,512]{2,1,0:T(8,128)}, f32[2,384,512]{2,1,0:T(8,128)}, u32[]{:S(2)}, u32[]{:S(2)}) collective-permute-start(f32[2,384,512]{2,1,0:T(8,128)} %piece.21.refs_3_), channel_id=1, source_target_pairs={{8,16},{12,20},{16,8},{20,12},{9,17},{13,21},{17,9},{21,13},{10,18... | collective-permute-start | bytes 4718600 | tf_op jit(solution)/shard_map/ppermute | solution.py:594
  233.5 61.2 %collective-permute-start.31 = (f32[2,384,512]{2,1,0:T(8,128)}, f32[2,384,512]{2,1,0:T(8,128)}, u32[]{:S(2)}, u32[]{:S(2)}) collective-permute-start(f32[2,384,512]{2,1,0:T(8,128)} %piece.22.refs_4_), channel_id=1, source_target_pairs={{0,8},{4,12},{24,16},{28,20},{8,0},{12,4},{16,24},{20,28},{1,9},{5... | collective-permute-start | bytes 4718600 | tf_op jit(solution)/shard_map/ppermute | solution.py:582
  240.1 35.4 %collective-permute-start.28 = (f32[1024,384]{1,0:T(8,128)}, f32[1024,384]{1,0:T(8,128)}, u32[]{:S(2)}, u32[]{:S(2)}) collective-permute-start(f32[1024,384]{1,0:T(8,128)} %get-tuple-element.71), channel_id=1, source_target_pairs={{0,4},{4,0},{8,12},{12,8},{16,20},{20,16},{24,28},{28,24},{1,5},{5... | collective-permute-start | bytes 4718600 | tf_op jit(solution)/shard_map/ppermute | solution.py:451
  240.6 36.5 %collective-permute-start.29 = (f32[2,384,512]{2,1,0:T(8,128)}, f32[2,384,512]{2,1,0:T(8,128)}, u32[]{:S(2)}, u32[]{:S(2)}) collective-permute-start(f32[2,384,512]{2,1,0:T(8,128)} %get-tuple-element.68.refs_3_), channel_id=1, source_target_pairs={{8,16},{12,20},{16,8},{20,12},{9,17},{13,21},{17,9},{21,13},{10,18... | collective-permute-start | bytes 4718600 | tf_op jit(solution)/shard_map/ppermute | solution.py:594
  273.1 32.7 %collective-permute-start.32 = (f32[2,384,512]{2,1,0:T(8,128)}, f32[2,384,512]{2,1,0:T(8,128)}, u32[]{:S(2)}, u32[]{:S(2)}) collective-permute-start(f32[2,384,512]{2,1,0:T(8,128)} %piece.25.refs_1_), channel_id=1, source_target_pairs={{8,16},{12,20},{16,8},{20,12},{9,17},{13,21},{17,9},{21,13},{10,18... | collective-permute-start | bytes 4718600 | tf_op jit(solution)/shard_map/ppermute | solution.py:594
  275.5 41.7 %collective-permute-start.34 = (f32[2,256,512]{2,1,0:T(8,128)}, f32[2,256,512]{2,1,0:T(8,128)}, u32[]{:S(2)}, u32[]{:S(2)}) collective-permute-start(f32[2,256,512]{2,1,0:T(8,128)} %get-tuple-element.69.refs_2_), channel_id=1, source_target_pairs={{0,8},{4,12},{24,16},{28,20},{8,0},{12,4},{16,24},{20,28},{1,9},{5... | collective-permute-start | bytes 3145736 | tf_op jit(solution)/shard_map/ppermute | solution.py:582
  277.1 46.9 %collective-permute-start.33 = (f32[2,128,512]{2,1,0:T(8,128)}, f32[2,128,512]{2,1,0:T(8,128)}, u32[]{:S(2)}, u32[]{:S(2)}) collective-permute-start(f32[2,128,512]{2,1,0:T(8,128)} %get-tuple-element.77), channel_id=1, source_target_pairs={{0,8},{4,12},{24,16},{28,20},{8,0},{12,4},{16,24},{20,28},{1,9},{5... | collective-permute-start | bytes 1572872 | tf_op jit(solution)/shard_map/ppermute | solution.py:582
  (16 other events, 142.7 us)
